TPU v7x, 32 devices: a whole 2x2x4 slice. The times are simulated.
32 devices in a mesh: seq: 16 (over z, x, core), head: 2 (over y).
Axes of the slice: x: 2, y: 2, z: 4, core: 2. Of those that a mesh axis runs over, the one named last changes fastest.
Arguments:
- tokens: bfloat16 [16384, 1152], P(('seq', 'head')), may hold values from -6 to 6
- cotangent: bfloat16 [16384, 1152], P(('seq', 'head')), may hold values from -6 to 6
- buckets: int32 [16], P('seq'), may hold values from 0 to 7
- timesteps: int32 [16], P('seq'), may hold values from 0 to 999
- labels: int32 [16], P('seq'), may hold values from 0 to 999
- class_table: bfloat16 [1000, 1152], replicated, may hold values from -6 to 6
- step_count: int32 [], replicated, may hold values from 2 to 20
- modulate_master: float32 [1152, 6912], P('seq', 'head'), may hold values from -0.1875 to 0.1875
- modulate_first: float32 [1152, 6912], P('seq', 'head'), may hold values from -0.0008544922 to 0.0008544922
- modulate_second: float32 [1152, 6912], P('seq', 'head'), may hold values from 2.049866e-08 to 8.199464e-08
- attend_master: float32 [1152, 3456], P('seq', 'head'), may hold values from -0.1875 to 0.1875
- attend_first: float32 [1152, 3456], P('seq', 'head'), may hold values from -0.00048828125 to 0.00048828125
- attend_second: float32 [1152, 3456], P('seq', 'head'), may hold values from 6.6934405e-09 to 2.6773762e-08
- project_master: float32 [1152, 1152], P('seq', 'head'), may hold values from -0.1875 to 0.1875
- project_first: float32 [1152, 1152], P('seq', 'head'), may hold values from -0.0012207031 to 0.0012207031
- project_second: float32 [1152, 1152], P('seq', 'head'), may hold values from 4.1834003e-08 to 1.6733601e-07
- expand_master: float32 [1152, 4608], P('seq', 'head'), may hold values from -0.1875 to 0.1875
- expand_first: float32 [1152, 4608], P('seq', 'head'), may hold values from -0.0007324219 to 0.0007324219
- expand_second: float32 [1152, 4608], P('seq', 'head'), may hold values from 1.5060241e-08 to 6.0240964e-08
- reduce_master: float32 [4608, 1152], P('seq', 'head'), may hold values from -0.09375 to 0.09375
- reduce_first: float32 [4608, 1152], P('seq', 'head'), may hold values from -0.0012207031 to 0.0012207031
- reduce_second: float32 [4608, 1152], P('seq', 'head'), may hold values from 4.1834003e-08 to 1.6733601e-07
- biases_master: float32 [16128], replicated, may hold values from -1 to 1
- biases_first: float32 [16128], replicated, may hold values from -0.0009765625 to 0.0009765625
- biases_second: float32 [16128], replicated, may hold values from 2.6773762e-08 to 1.0709505e-07
Outputs:
- output: bfloat16 [16384, 1152], P(('seq', 'head'))
- input_grad: float32 [16384, 1152], P(('seq', 'head'))
- grad_norm: float32 [], replicated
- modulate_updated: float32 [1152, 6912], P('seq', 'head')
- modulate_momentum: float32 [1152, 6912], P('seq', 'head')
- modulate_variance: float32 [1152, 6912], P('seq', 'head')
- attend_updated: float32 [1152, 3456], P('seq', 'head')
- attend_momentum: float32 [1152, 3456], P('seq', 'head')
- attend_variance: float32 [1152, 3456], P('seq', 'head')
- project_updated: float32 [1152, 1152], P('seq', 'head')
- project_momentum: float32 [1152, 1152], P('seq', 'head')
- project_variance: float32 [1152, 1152], P('seq', 'head')
- expand_updated: float32 [1152, 4608], P('seq', 'head')
- expand_momentum: float32 [1152, 4608], P('seq', 'head')
- expand_variance: float32 [1152, 4608], P('seq', 'head')
- reduce_updated: float32 [4608, 1152], P('seq', 'head')
- reduce_momentum: float32 [4608, 1152], P('seq', 'head')
- reduce_variance: float32 [4608, 1152], P('seq', 'head')
- biases_updated: float32 [16128], replicated
- biases_momentum: float32 [16128], replicated
- biases_variance: float32 [16128], replicated
All inputs are finite; a program needn't handle non-finite values.
Results may differ from a plain program's by a relative error of at most 0.035.
Values may be sent and summed in bfloat16 or wider, within the bound.
A program may use at most 256 MiB of HBM per device.

v0:
```python
import math

import jax
import jax.numpy as jnp
from jax import lax
from jax.sharding import PartitionSpec as P

D = 1152
HEAD_DIM = 72
FF = 4608
SIDE = 32
LMAX = 1024


highest = lax.Precision.HIGHEST
row_units = (8, 4, 16, 6, 10, 7, 4, 6)
col_units = (8, 16, 4, 10, 6, 9, 8, 6)


def table_pick(indices, entries):
    matches = indices[..., None] == jnp.arange(len(entries), dtype=jnp.int32)
    return jnp.sum(jnp.where(matches, jnp.array(entries, jnp.int32), 0), axis=-1)


def layer_norm(value):
    average = jnp.mean(value, axis=-1, keepdims=True)
    centred = value - average
    spread = jnp.mean(centred * centred, axis=-1, keepdims=True)
    return centred * lax.rsqrt(spread + 1e-06)


def modulate(value, shift, scaling):
    return layer_norm(value) * (1.0 + scaling) + shift


def time_features(moments, width):
    half_width = width // 2
    frequency = jnp.exp(-math.log(10000.0) * jnp.arange(half_width, dtype=jnp.float32) / half_width)
    angles = moments.astype(jnp.float32)[:, None] * frequency[None, :]
    return jnp.concatenate([jnp.cos(angles), jnp.sin(angles)], axis=1)


def grid_features(position, row_wide, width):
    quarter = width // 4
    omegas = jnp.exp(-math.log(10000.0) * jnp.arange(quarter, dtype=jnp.float32) / quarter)
    row_angle = (position // row_wide).astype(jnp.float32)[:, None] * omegas[None, :]
    col_angle = (position % row_wide).astype(jnp.float32)[:, None] * omegas[None, :]
    return jnp.concatenate(
        [jnp.sin(row_angle), jnp.cos(row_angle), jnp.sin(col_angle), jnp.cos(col_angle)], axis=1
    )


def fold_rows(left_side, weight_slab):
    return jnp.dot(
        left_side,
        lax.all_gather(weight_slab, "seq", axis=0, tiled=True),
        preferred_element_type=jnp.float32,
    )


def back_cols(gradient, weight_slab):
    return lax.dot_general(
        gradient,
        lax.all_gather(weight_slab, "seq", axis=0, tiled=True),
        (((1,), (1,)), ((), ())),
        preferred_element_type=jnp.float32,
    )


def rows_seq(left_side, right_side):
    return lax.psum_scatter(
        lax.dot_general(
            left_side, right_side, (((0,), (0,)), ((), ())), preferred_element_type=jnp.float32
        ).astype(jnp.bfloat16),
        "seq",
        scatter_dimension=0,
        tiled=True,
    ).astype(jnp.float32)


def attend(queries, key_rows, value_rows, lengths):
    heads_here = queries.shape[1] // HEAD_DIM
    block_rows = min(512, LMAX)
    score_scale = HEAD_DIM ** (-0.5)
    image_count = lengths.shape[0]

    def per_image(packed):
        query_image, key_image, value_image, length = packed
        key_heads = key_image.reshape(LMAX, heads_here, HEAD_DIM)
        value_heads = value_image.reshape(LMAX, heads_here, HEAD_DIM)
        live_keys = jnp.arange(LMAX, dtype=jnp.int32) < length

        def per_block(query_block):
            scores = (
                jnp.einsum(
                    "qhe,khe->hqk", query_block, key_heads, preferred_element_type=jnp.float32
                )
                * score_scale
            )
            scores = jnp.where(live_keys[None, None, :], scores, -1e30)
            maximum = jnp.max(scores, axis=-1, keepdims=True)
            weights = jnp.exp(scores - maximum)
            totals = jnp.sum(weights, axis=-1, keepdims=True)
            probability = (weights / totals).astype(jnp.bfloat16)
            result = jnp.einsum(
                "hqk,khe->qhe", probability, value_heads, preferred_element_type=jnp.float32
            )
            return (result.astype(jnp.bfloat16), (maximum + jnp.log(totals))[:, :, 0])

        blocks = query_image.reshape(LMAX // block_rows, block_rows, heads_here, HEAD_DIM)
        result, log_sums = lax.map(per_block, blocks)
        return (result.reshape(LMAX, heads_here * HEAD_DIM), log_sums)

    stacked = (
        queries.reshape(image_count, LMAX, -1),
        key_rows.reshape(image_count, LMAX, -1),
        value_rows.reshape(image_count, LMAX, -1),
        lengths,
    )
    result, log_sums = lax.map(per_image, stacked)
    return (result.reshape(image_count * LMAX, -1), log_sums)


def attend_back(queries, key_rows, value_rows, grad_rows, log_sums, lengths):
    heads_here = queries.shape[1] // HEAD_DIM
    block_rows = min(512, LMAX)
    score_scale = HEAD_DIM ** (-0.5)
    image_count = lengths.shape[0]

    def per_image(packed):
        query_image, key_image, value_image, grad_image, logsum_image, length = packed
        key_heads = key_image.reshape(LMAX, heads_here, HEAD_DIM)
        value_heads = value_image.reshape(LMAX, heads_here, HEAD_DIM)
        live_keys = jnp.arange(LMAX, dtype=jnp.int32) < length

        def per_block(running, inputs):
            key_grad, value_grad = running
            query_block, grad_block, logsum_block = inputs
            scores = (
                jnp.einsum(
                    "qhe,khe->hqk", query_block, key_heads, preferred_element_type=jnp.float32
                )
                * score_scale
            )
            scores = jnp.where(live_keys[None, None, :], scores, -1e30)
            probability = jnp.exp(scores - logsum_block[:, :, None])
            grad_prob = jnp.einsum(
                "qhe,khe->hqk", grad_block, value_heads, preferred_element_type=jnp.float32
            )
            inner_sum = jnp.sum(probability * grad_prob, axis=-1, keepdims=True)
            grad_score = (probability * (grad_prob - inner_sum)).astype(jnp.bfloat16)
            query_grad = (
                jnp.einsum(
                    "hqk,khe->qhe", grad_score, key_heads, preferred_element_type=jnp.float32
                )
                * score_scale
            )
            key_grad = (
                key_grad
                + jnp.einsum(
                    "hqk,qhe->khe", grad_score, query_block, preferred_element_type=jnp.float32
                )
                * score_scale
            )
            value_grad = value_grad + jnp.einsum(
                "hqk,qhe->khe",
                probability.astype(jnp.bfloat16),
                grad_block,
                preferred_element_type=jnp.float32,
            )
            return ((key_grad, value_grad), query_grad.astype(jnp.bfloat16))

        initial = (
            jnp.zeros((LMAX, heads_here, HEAD_DIM), jnp.float32),
            jnp.zeros((LMAX, heads_here, HEAD_DIM), jnp.float32),
        )
        blocks = (
            query_image.reshape(LMAX // block_rows, block_rows, heads_here, HEAD_DIM),
            grad_image.reshape(LMAX // block_rows, block_rows, heads_here, HEAD_DIM),
            logsum_image,
        )
        (key_grad, value_grad), query_grad = lax.scan(per_block, initial, blocks)
        return (
            query_grad.reshape(LMAX, -1),
            key_grad.reshape(LMAX, -1).astype(jnp.bfloat16),
            value_grad.reshape(LMAX, -1).astype(jnp.bfloat16),
        )

    stacked = (
        queries.reshape(image_count, LMAX, -1),
        key_rows.reshape(image_count, LMAX, -1),
        value_rows.reshape(image_count, LMAX, -1),
        grad_rows.reshape(image_count, LMAX, -1),
        log_sums,
        lengths,
    )
    query_grad, key_grad, value_grad = lax.map(per_image, stacked)
    return (
        query_grad.reshape(image_count * LMAX, -1),
        key_grad.reshape(image_count * LMAX, -1),
        value_grad.reshape(image_count * LMAX, -1),
    )


def adam_update(master, first_moment, second_moment, gradient, learn_rate, clip_factor, correction):
    clipped = gradient * clip_factor
    first_new = 0.5 * first_moment + 0.5 * clipped
    second_new = 0.5 * second_moment + 0.5 * clipped * clipped
    direction = first_new / correction / (jnp.sqrt(second_new / correction) + 1e-08)
    return (master - learn_rate * (direction + 0.1 * master), first_new, second_new)


def on_device(
    tokens,
    cotangent,
    buckets,
    timesteps,
    labels,
    class_table,
    step_count,
    modulate_master,
    modulate_first,
    modulate_second,
    attend_master,
    attend_first,
    attend_second,
    project_master,
    project_first,
    project_second,
    expand_master,
    expand_first,
    expand_second,
    reduce_master,
    reduce_first,
    reduce_second,
    biases_master,
    biases_first,
    biases_second,
):
    head_index = lax.axis_index("head")
    head_count = lax.axis_size("head")
    tok_rows = tokens.shape[0]
    image_count = buckets.shape[0]
    unit_cells = SIDE // 8
    heights = table_pick(buckets, row_units) * unit_cells
    widths = table_pick(buckets, col_units) * unit_cells
    lengths = heights * widths
    row_index = head_index * tok_rows + jnp.arange(tok_rows, dtype=jnp.int32)
    image_of = row_index // LMAX
    position = row_index % LMAX
    choose = image_of[:, None] == jnp.arange(image_count, dtype=jnp.int32)[None, :]
    pick_rows = choose.astype(jnp.float32)
    row_wide = jnp.sum(jnp.where(choose, widths[None, :], 0), axis=1)
    row_length = jnp.sum(jnp.where(choose, lengths[None, :], 0), axis=1)
    live_rows = (position < row_length).astype(jnp.float32)
    grid_cells = grid_features(position, row_wide, D)
    class_pick = (
        labels[:, None] == jnp.arange(class_table.shape[0], dtype=jnp.int32)[None, :]
    ).astype(jnp.bfloat16)
    class_rows = jnp.dot(class_pick, class_table, preferred_element_type=jnp.float32)
    condition = jax.nn.silu(class_rows + time_features(timesteps, D)).astype(jnp.bfloat16)
    bias_low = biases_master.astype(jnp.bfloat16).astype(jnp.float32)
    offset_base = 6 * D
    bias_query = bias_low[offset_base : offset_base + D]
    bias_value = bias_low[offset_base + D : offset_base + 2 * D]
    bias_proj = bias_low[offset_base + 2 * D : offset_base + 3 * D]
    bias_hidden = bias_low[offset_base + 3 * D : offset_base + 3 * D + FF]
    bias_output = bias_low[offset_base + 3 * D + FF :]
    head_slabs = (
        lax.all_gather(attend_master.astype(jnp.bfloat16), "head", axis=1, tiled=True),
        lax.all_gather(project_master.astype(jnp.bfloat16), "head", axis=1, tiled=True),
        lax.all_gather(expand_master.astype(jnp.bfloat16), "head", axis=1, tiled=True),
        lax.all_gather(reduce_master.astype(jnp.bfloat16), "head", axis=1, tiled=True),
    )
    attend_slab, project_slab, expand_slab, reduce_slab = head_slabs
    mod_width = 6 * D // head_count
    mod_share = fold_rows(condition, modulate_master.astype(jnp.bfloat16))
    mod_share = mod_share + lax.dynamic_slice_in_dim(bias_low, head_index * mod_width, mod_width)
    modulation = lax.all_gather(mod_share, "head", axis=1, tiled=True)
    mod_rows = jnp.dot(pick_rows, modulation, precision=highest)
    shift_one, scale_one, gating_one, shift_two, scale_two, gating_two = jnp.split(
        mod_rows, 6, axis=1
    )
    residual_zero = tokens.astype(jnp.float32) + grid_cells
    hidden_attend = modulate(residual_zero, shift_one, scale_one).astype(jnp.bfloat16)
    packed = fold_rows(hidden_attend, attend_slab)
    queries = (packed[:, :D] + bias_query).astype(jnp.bfloat16)
    key_rows = packed[:, D : 2 * D].astype(jnp.bfloat16)
    value_rows = (packed[:, 2 * D :] + bias_value).astype(jnp.bfloat16)
    query_heads, key_heads, value_heads = (
        lax.all_to_all(queries, "head", split_axis=1, concat_axis=0, tiled=True),
        lax.all_to_all(key_rows, "head", split_axis=1, concat_axis=0, tiled=True),
        lax.all_to_all(value_rows, "head", split_axis=1, concat_axis=0, tiled=True),
    )
    head_out, log_sums = attend(query_heads, key_heads, value_heads, lengths)
    attention = lax.all_to_all(head_out, "head", split_axis=0, concat_axis=1, tiled=True)
    branch_attend = fold_rows(attention, project_slab) + bias_proj
    residual_one = residual_zero + gating_one * branch_attend
    hidden_expand = modulate(residual_one, shift_two, scale_two).astype(jnp.bfloat16)
    widened = fold_rows(hidden_expand, expand_slab) + bias_hidden
    activated = jax.nn.gelu(widened, approximate=True).astype(jnp.bfloat16)
    branch_expand = fold_rows(activated, reduce_slab) + bias_output
    output = (residual_one + gating_two * branch_expand).astype(jnp.bfloat16)
    outer_grad = cotangent.astype(jnp.float32) * live_rows[:, None]
    gating_later = outer_grad * branch_expand
    closing_grad = (outer_grad * gating_two).astype(jnp.bfloat16)
    active_grad = back_cols(closing_grad, reduce_slab)
    gelu_value, gelu_pullback = jax.vjp(lambda inner: jax.nn.gelu(inner, approximate=True), widened)
    widened_grad = gelu_pullback(active_grad)[0].astype(jnp.bfloat16)
    hidden_grad = back_cols(widened_grad, expand_slab)
    later_value, later_pullback = jax.vjp(modulate, residual_one, shift_two, scale_two)
    residual_part, shift_later, scale_later = later_pullback(hidden_grad)
    middle_grad = outer_grad + residual_part
    gating_early = middle_grad * branch_attend
    branch_grad = (middle_grad * gating_one).astype(jnp.bfloat16)
    attend_grad = back_cols(branch_grad, project_slab).astype(jnp.bfloat16)
    heads_grad = lax.all_to_all(attend_grad, "head", split_axis=1, concat_axis=0, tiled=True)
    query_grad, keyrow_grad, value_grad = attend_back(
        query_heads, key_heads, value_heads, heads_grad, log_sums, lengths
    )
    query_back, keys_back, values_back = (
        lax.all_to_all(query_grad, "head", split_axis=0, concat_axis=1, tiled=True),
        lax.all_to_all(keyrow_grad, "head", split_axis=0, concat_axis=1, tiled=True),
        lax.all_to_all(value_grad, "head", split_axis=0, concat_axis=1, tiled=True),
    )
    packed_grad = jnp.concatenate([query_back, keys_back, values_back], axis=1)
    normed_grad = back_cols(packed_grad, attend_slab)
    early_value, early_pullback = jax.vjp(modulate, residual_zero, shift_one, scale_one)
    input_part, shift_early, scale_early = early_pullback(normed_grad)
    input_grad = middle_grad + input_part
    mod_token_grad = jnp.concatenate(
        [shift_early, scale_early, gating_early, shift_later, scale_later, gating_later], axis=1
    )
    mod_grad = lax.dot_general(
        pick_rows, mod_token_grad, (((0,), (0,)), ((), ())), precision=highest
    )
    mod_summed = lax.psum_scatter(mod_grad, "head", scatter_dimension=1, tiled=True)
    mod_rounded = mod_summed.astype(jnp.bfloat16)
    grad_mod = rows_seq(condition, mod_rounded)
    mod_slot = lax.dynamic_update_slice_in_dim(
        jnp.zeros((6 * D,), jnp.float32),
        jnp.sum(mod_rounded.astype(jnp.float32), axis=0),
        head_index * mod_width,
        0,
    )
    bias_share = jnp.concatenate(
        [
            mod_slot,
            jnp.sum(query_back.astype(jnp.float32), axis=0),
            jnp.sum(values_back.astype(jnp.float32), axis=0),
            jnp.sum(branch_grad.astype(jnp.float32), axis=0),
            jnp.sum(widened_grad.astype(jnp.float32), axis=0),
            jnp.sum(closing_grad.astype(jnp.float32), axis=0),
        ]
    )
    operand_pairs = (
        (hidden_attend, packed_grad),
        (attention, branch_grad),
        (hidden_expand, widened_grad),
        (activated, closing_grad),
    )
    term_slabs = tuple((rows_seq(left_side, right_side) for left_side, right_side in operand_pairs))
    reduced = (
        lax.psum_scatter(
            term_slabs[0].astype(jnp.bfloat16), "head", scatter_dimension=1, tiled=True
        ).astype(jnp.float32),
        lax.psum_scatter(
            term_slabs[1].astype(jnp.bfloat16), "head", scatter_dimension=1, tiled=True
        ).astype(jnp.float32),
        lax.psum_scatter(
            term_slabs[2].astype(jnp.bfloat16), "head", scatter_dimension=1, tiled=True
        ).astype(jnp.float32),
        lax.psum_scatter(
            term_slabs[3].astype(jnp.bfloat16), "head", scatter_dimension=1, tiled=True
        ).astype(jnp.float32),
    )
    grad_attend, grad_project, grad_expand, grad_reduce = reduced
    local_squares = jnp.sum(grad_mod * grad_mod) + sum(
        (jnp.sum(gradient * gradient) for gradient in reduced)
    )
    bias_total, square_total = lax.psum((bias_share, local_squares), ("seq", "head"))
    grad_norm = jnp.sqrt(square_total + jnp.sum(bias_total * bias_total))
    clip_factor = jnp.minimum(1.0, 1.0 / (grad_norm + 1e-06))
    correction = 1.0 - jnp.power(0.5, step_count.astype(jnp.float32))
    modulate_new = adam_update(
        modulate_master,
        modulate_first,
        modulate_second,
        grad_mod,
        0.5 * D ** (-0.5),
        clip_factor,
        correction,
    )
    attend_new = adam_update(
        attend_master,
        attend_first,
        attend_second,
        grad_attend,
        0.5 * D ** (-0.5),
        clip_factor,
        correction,
    )
    project_new = adam_update(
        project_master,
        project_first,
        project_second,
        grad_project,
        0.5 * D ** (-0.5),
        clip_factor,
        correction,
    )
    expand_new = adam_update(
        expand_master,
        expand_first,
        expand_second,
        grad_expand,
        0.5 * D ** (-0.5),
        clip_factor,
        correction,
    )
    reduce_new = adam_update(
        reduce_master,
        reduce_first,
        reduce_second,
        grad_reduce,
        0.5 * FF ** (-0.5),
        clip_factor,
        correction,
    )
    biases_new = adam_update(
        biases_master, biases_first, biases_second, bias_total, 0.1, clip_factor, correction
    )
    return (
        output,
        input_grad,
        grad_norm,
        modulate_new[0],
        modulate_new[1],
        modulate_new[2],
        attend_new[0],
        attend_new[1],
        attend_new[2],
        project_new[0],
        project_new[1],
        project_new[2],
        expand_new[0],
        expand_new[1],
        expand_new[2],
        reduce_new[0],
        reduce_new[1],
        reduce_new[2],
        biases_new[0],
        biases_new[1],
        biases_new[2],
    )


def solution(mesh):
    return jax.shard_map(
        on_device,
        mesh=mesh,
        in_specs=(
            P(("seq", "head"), None),
            P(("seq", "head"), None),
            P("seq"),
            P("seq"),
            P("seq"),
            P(),
            P(),
            P("seq", "head"),
            P("seq", "head"),
            P("seq", "head"),
            P("seq", "head"),
            P("seq", "head"),
            P("seq", "head"),
            P("seq", "head"),
            P("seq", "head"),
            P("seq", "head"),
            P("seq", "head"),
            P("seq", "head"),
            P("seq", "head"),
            P("seq", "head"),
            P("seq", "head"),
            P("seq", "head"),
            P(),
            P(),
            P(),
        ),
        out_specs=(
            P(("seq", "head"), None),
            P(("seq", "head"), None),
            P(),
            P("seq", "head"),
            P("seq", "head"),
            P("seq", "head"),
            P("seq", "head"),
            P("seq", "head"),
            P("seq", "head"),
            P("seq", "head"),
            P("seq", "head"),
            P("seq", "head"),
            P("seq", "head"),
            P("seq", "head"),
            P("seq", "head"),
            P("seq", "head"),
            P("seq", "head"),
            P("seq", "head"),
            P(),
            P(),
            P(),
        ),
        check_vma=False,
    )
```

profile of v0, /device:TPU:0, one launch (start us, length us, event | category | flops | bytes accessed | tf_op | source)
XLA Modules:
  0.0 1353.4 jit_solution(16809095590841780459)
XLA Ops:
  10.6 9.8 all-gather.2
  22.1 5.4 all-gather.3
  29.7 9.0 all_gather.40
  38.9 8.8 all-gather.4
  55.0 5.5 multiply_cosine_fusion
  65.9 19.8 %all-gather.11.cloned.1.call-done = bf16[1152,3456]{1,0:T(8,128)(2,1)} async-done(((bf16[72,3456]{1,0:T(8,128)(2,1)}), bf16[1152,3456]{1,0:T(8,128)(2,1)}) %all-gather.11.cloned.1.call-update) | async-done | bytes 7962640 | tf_op jit(solution)/shard_map/all_gather | solution.py:56
  101.5 57.5 %all-gather.13.cloned.1.call-done = bf16[1152,3456]{1,0:T(8,128)(2,1)} async-done(((bf16[72,3456]{1,0:T(8,128)(2,1)}), bf16[1152,3456]{1,0:T(8,128)(2,1)}) %all-gather.13.cloned.1.call-update) | async-done | bytes 7962640 | tf_op jit(solution)/shard_map/all_gather | solution.py:56
  159.0 7.4 fusion.97
  178.7 11.5 all-to-all-done.1
  195.2 13.5 %all-to-all-done.2 = bf16[512,2,576]{0,2,1:T(8,128)(2,1)S(1)} async-done(((bf16[512,2,576]{0,2,1:T(8,128)(2,1)}), bf16[512,2,576]{0,2,1:T(8,128)(2,1)S(1)}, u32[]{:S(2)}, u32[]{:S(2)}) %all-to-all-start.2) | async-done | bytes 1179680 | tf_op jit(solution)/shard_map/all_to_all | solution.py:293
  227.5 30.2 %while.48 = (s32[]{:T(128)}, bf16[2,512,8,72]{1,3,2,0:T(8,128)(2,1)}, f32[2,8,512]{2,1,0:T(8,128)}, bf16[2,512,8,72]{1,3,2,0:T(8,128)(2,1)S(1)}, bf16[1024,8,72]...) while((s32[]{:T(128)}, bf16[2,512,8,72]{1,3,2,0:T(8,128)(2,1)}, ...), condition=%wide.region_7.8_spmd.clone, body=%wide.region_4.7_spmd.clone.sunk | while | flops 1258583040 | bytes 54005868 | solution.py:111
  235.6 6.2 fusion.152
  250.9 6.2 fusion.152
  257.7 13.5 all-to-all-start.3
  272.6 11.3 all-to-all-done.3
  283.8 6.6 fusion.94
  295.8 13.0 fusion.98
  308.8 73.7 %all-gather.19.cloned.1.call-done = bf16[4608,1152]{1,0:T(8,128)(2,1)} async-done(((bf16[288,1152]{1,0:T(8,128)(2,1)}), bf16[4608,1152]{1,0:T(8,128)(2,1)}) %all-gather.19.cloned.1.call-update) | async-done | bytes 10616848 | tf_op jit(solution)/shard_map/all_gather | solution.py:56
  382.6 17.8 %convert_reduce_fusion = (f32[4608]{0:T(1024)}, bf16[512,4608]{1,0:T(8,128)(2,1)}) fusion(f32[512,4608]{1,0:T(8,128)} %fusion.98, f32[4608]{0:T(1024)} %slice.39, bf16[512,1152]{1,0:T(8,128)(2,1)} %get-tuple-element.277, bf16[4608,1152]{1,0:T(8,128)(2,1)} %all-gather.19.cloned.1.call-done), kind=kOutput, calls=%fused_computation.58 | convolution fusion | flops 5490077184 | bytes 25989120 | tf_op jit(solution)/shard_map/dot_general | solution.py:62
  400.4 12.0 multiply_reduce_fusion.2
  412.4 16.5 %fusion.93 = (f32[512]{0:T(512)S(1)}, f32[512,1152]{1,0:T(8,128)S(1)}, bf16[512,1152]{1,0:T(8,128)(2,1)}, f32[512,1152]{1,0:T(8,128)}) fusion(f32[512]{0:T(512)S(1)} %multiply_multiply_fusion.9, f32[512,1152]{1,0:T(8,128)S(1)} %copy-done.11, f32[512]{0:T(512)S(1)} %broadcast_multiply_fusion.1, f32[512]{0:T(512)S(1)} %fusion.77, ...), kind=kOutput, calls=%fused_computation.217 | convolution fusion | flops 5466488320 | bytes 35420672 | tf_op jit(solution)/shard_map/dot_general | solution.py:54
  440.7 15.7 %all-to-all-done.4 = bf16[512,2,576]{0,2,1:T(8,128)(2,1)S(1)} async-done(((bf16[512,2,576]{0,2,1:T(8,128)(2,1)}), bf16[512,2,576]{0,2,1:T(8,128)(2,1)S(1)}, u32[]{:S(2)}, u32[]{:S(2)}) %all-to-all-start.4) | async-done | bytes 1179680 | tf_op jit(solution)/shard_map/all_to_all | solution.py:317
  457.5 87.9 %while.49 = (s32[]{:T(128)}, f32[1024,8,72]{0,2,1:T(8,128)}, f32[1024,8,72]{0,2,1:T(8,128)}, bf16[2,512,8,72]{1,3,2,0:T(8,128)(2,1)}, bf16[2,512,8,72]{1,3,2,0:T...) while((s32[]{:T(128)}, f32[1024,8,72]{0,2,1:T(8,128)}, ...), condition=%wide.region_14.15_spmd.clone, body=%wide.region_12.14_spmd.clone.sunk | while | flops 3061183488 | bytes 203704688 | solution.py:182
  463.8 10.7 multiply_reduce_fusion.7
  474.5 9.3 multiply_convert_fusion.12
  483.8 9.1 bitcast_add_fusion.5
  506.2 10.7 multiply_reduce_fusion.7
  516.9 9.3 multiply_convert_fusion.12
  526.2 9.8 bitcast_add_fusion.5
  540.1 5.3 bitcast_add_fusion.4
  553.0 10.9 all-to-all-done.5
  574.5 7.9 all-to-all-done.6
  587.1 12.9 all-to-all-done.7
  600.0 11.3 constant_dynamic-update-slice_fusion.1
  625.1 16.4 %convolution_bitcast_fusion = f32[6912,1]{1,0:T(8,128)} fusion(pred[512,1]{0,1:T(4,128)(4,1)S(1)} %reshape.378, f32[512,6912]{1,0:T(8,128)} %multiply_dynamic-update-slice_fusion), kind=kOutput, calls=%fused_computation.60 | convolution fusion | flops 42467328 | bytes 14183936
  648.5 9.4 convolution_convert_fusion.2
  659.2 12.9 convolution_convert_fusion
  673.4 10.2 convolution_convert_fusion.1
  688.8 66.2 %reduce-scatter.43.cloned.1.call-done = bf16[72,1152]{1,0:T(8,128)(2,1)} async-done(((bf16[1152,1152]{1,0:T(8,128)(2,1)}), bf16[72,1152]{1,0:T(8,128)(2,1)}) %reduce-scatter.43.cloned.1.call-update) | async-done | bytes 165904
  761.6 97.3 %reduce-scatter.41.cloned.1.call-done = bf16[72,3456]{1,0:T(8,128)(2,1)} async-done(((bf16[1152,3456]{1,0:T(8,128)(2,1)}), bf16[72,3456]{1,0:T(8,128)(2,1)}) %reduce-scatter.41.cloned.1.call-update) | async-done | bytes 497680
  861.2 122.3 %reduce-scatter.29.cloned.1.call-done = bf16[288,1152]{1,0:T(8,128)(2,1)} async-done(((bf16[4608,1152]{1,0:T(8,128)(2,1)}), bf16[288,1152]{1,0:T(8,128)(2,1)}) %reduce-scatter.29.cloned.1.call-update) | async-done | bytes 663568 | tf_op jit(solution)/shard_map/reduce_scatter | solution.py:71
  987.0 121.0 %reduce-scatter.25.cloned.1.call-done = bf16[72,4608]{1,0:T(8,128)(2,1)} async-done(((bf16[1152,4608]{1,0:T(8,128)(2,1)}), bf16[72,4608]{1,0:T(8,128)(2,1)}) %reduce-scatter.25.cloned.1.call-update) | async-done | bytes 663568 | tf_op jit(solution)/shard_map/reduce_scatter | solution.py:71
  1110.3 12.5 reduce-scatter.35.cloned.1.call-done
  1124.5 103.6 %reduce-scatter.39.cloned.1.call-done = bf16[72,3456]{1,0:T(8,128)(2,1)} async-done(((bf16[1152,3456]{1,0:T(8,128)(2,1)}), bf16[72,3456]{1,0:T(8,128)(2,1)}) %reduce-scatter.39.cloned.1.call-update) | async-done | bytes 497680
  1230.0 19.3 %reduce-scatter.33.cloned.1.call-done = bf16[1728,72]{1,0:T(8,128)(2,1)} async-done(((bf16[3456,72]{1,0:T(8,128)(2,1)}), bf16[1728,72]{1,0:T(8,128)(2,1)}) %reduce-scatter.33.cloned.1.call-update) | async-done | bytes 248848
  1252.6 18.0 %reduce-scatter.37.cloned.1.call-done = bf16[576,288]{1,0:T(8,128)(2,1)} async-done(((bf16[1152,288]{1,0:T(8,128)(2,1)}), bf16[576,288]{1,0:T(8,128)(2,1)}) %reduce-scatter.37.cloned.1.call-update) | async-done | bytes 331792
  1272.6 16.2 %reduce-scatter.27.cloned.1.call-done = bf16[72,2304]{1,0:T(8,128)(2,1)} async-done(((bf16[72,4608]{1,0:T(8,128)(2,1)}), bf16[72,2304]{1,0:T(8,128)(2,1)}) %reduce-scatter.27.cloned.1.call-update) | async-done | bytes 331792 | tf_op jit(solution)/shard_map/reduce_scatter | solution.py:370
  1292.5 40.3 %all-reduce.3 = (f32[]{:T(128)}, f32[16128]{0:T(1024)S(1)}) all-reduce(f32[]{:T(128)S(6)} %add.392, f32[16128]{0:T(1024)S(1)} %copy-done.60), channel_id=1, replica_groups=mesh['seq'=16,'head'=2] {'seq','head'}, use_global_device_ids=true, to_apply=%region_32.33 | all-reduce | flops 16129 | bytes 129032 | tf_op jit(solution)/shard_map/psum | solution.py:381
  (352 shorter events, 213.3 us)
Async XLA Ops:
  7.2 46.0 %copy-start = (bf16[1000,1152]{1,0:T(8,128)(2,1)S(1)}, bf16[1000,1152]{1,0:T(8,128)(2,1)}, u32[]{:S(2)}) copy-start(bf16[1000,1152]{1,0:T(8,128)(2,1)} %param.36) | copy-start | bytes 6912004
  7.2 78.5 %all-gather.11.cloned.1.call-start = ((), (), s32[]{:S(2)}) async-start(), calls=%async_computation.18 | async-start | bytes 8460288 | tf_op jit(solution)/shard_map/all_gather | solution.py:56
  9.5 149.5 %all-gather.13.cloned.1.call-start = ((), (), s32[]{:S(2)}) async-start(), calls=%async_computation.19 | async-start | bytes 8460288 | tf_op jit(solution)/shard_map/all_gather | solution.py:56
  22.1 250.5 %all-gather.15.cloned.1.call-start = ((), (), s32[]{:S(2)}) async-start(), calls=%async_computation.20 | async-start | bytes 2820096 | tf_op jit(solution)/shard_map/all_gather | solution.py:56
  28.5 267.3 %all-gather.17.cloned.1.call-start = ((), (), s32[]{:S(2)}) async-start(), calls=%async_computation.21 | async-start | bytes 11280384 | tf_op jit(solution)/shard_map/all_gather | solution.py:56
  38.7 343.8 %all-gather.19.cloned.1.call-start = ((), (), s32[]{:S(2)}) async-start(), calls=%async_computation.22 | async-start | bytes 11280384 | tf_op jit(solution)/shard_map/all_gather | solution.py:56
  54.4 35.7 %copy-start.51 = (f32[16128]{0:T(1024)}, f32[16128]{0:T(1024)S(1)}, u32[]{:S(2)}) copy-start(f32[16128]{0:T(1024)S(1)} %convert_convert_fusion) | copy-start | bytes 193540
  65.5 30.5 %copy-start.7 = (f32[512,1152]{1,0:T(8,128)}, f32[512,1152]{1,0:T(8,128)S(1)}, u32[]{:S(2)}) copy-start(f32[512,1152]{1,0:T(8,128)S(1)} %get-tuple-element.291) | copy-start | bytes 7077892
  65.5 30.5 %copy-start.63 = (f32[512]{0:T(512)}, f32[512]{0:T(512)S(1)}, u32[]{:S(2)}) copy-start(f32[512]{0:T(512)S(1)} %broadcast_multiply_fusion.2) | copy-start | bytes 6148
  65.9 30.1 %copy-start.73 = (f32[512]{0:T(512)}, f32[512]{0:T(512)S(1)}, u32[]{:S(2)}) copy-start(f32[512]{0:T(512)S(1)} %fusion.76) | copy-start | bytes 6148
  101.5 64.9 %copy-start.34 = (bf16[512,1152]{1,0:T(8,128)(2,1)}, bf16[512,1152]{1,0:T(8,128)(2,1)S(1)}, u32[]{:S(2)}) copy-start(bf16[512,1152]{1,0:T(8,128)(2,1)S(1)} %fusion.46) | copy-start | bytes 3538948
  170.8 19.3 %all-to-all-start.1 = ((bf16[512,2,576]{0,2,1:T(8,128)(2,1)}), bf16[512,2,576]{0,2,1:T(8,128)(2,1)S(1)}, u32[]{:S(2)}, u32[]{:S(2)}) async-start(bf16[512,2,576]{0,2,1:T(8,128)(2,1)} %bitcast.9), calls=%async_computation.1 | async-start | bytes 2359296 | tf_op jit(solution)/shard_map/all_to_all | solution.py:292
  190.1 18.6 %all-to-all-start.2 = ((bf16[512,2,576]{0,2,1:T(8,128)(2,1)}), bf16[512,2,576]{0,2,1:T(8,128)(2,1)S(1)}, u32[]{:S(2)}, u32[]{:S(2)}) async-start(bf16[512,2,576]{0,2,1:T(8,128)(2,1)} %bitcast.185), calls=%async_computation.2 | async-start | bytes 2359296 | tf_op jit(solution)/shard_map/all_to_all | solution.py:293
  208.7 17.7 %all-to-all-start = ((bf16[512,2,576]{0,2,1:T(8,128)(2,1)}), bf16[512,2,576]{0,2,1:T(8,128)(2,1)S(1)}, u32[]{:S(2)}, u32[]{:S(2)}) async-start(bf16[512,2,576]{0,2,1:T(8,128)(2,1)} %bitcast.184), calls=%async_computation | async-start | bytes 2359296 | tf_op jit(solution)/shard_map/all_to_all | solution.py:291
  257.7 26.2 %all-to-all-start.3 = ((bf16[2,512,576]{1,2,0:T(8,128)(2,1)}), bf16[2,512,576]{1,2,0:T(8,128)(2,1)}, u32[]{:S(2)}, u32[]{:S(2)}) async-start(bf16[2,512,576]{1,2,0:T(8,128)(2,1)} %bitcast.13), calls=%async_computation.3 | async-start | bytes 2359296 | tf_op jit(solution)/shard_map/all_to_all | solution.py:296
  272.5 156.5 %copy-start.61 = (f32[512]{0:T(512)}, f32[512]{0:T(512)S(1)}, u32[]{:S(2)}) copy-start(f32[512]{0:T(512)S(1)} %fusion.74) | copy-start | bytes 6148
  290.5 121.9 %copy-start.65 = (f32[512]{0:T(512)}, f32[512]{0:T(512)S(1)}, u32[]{:S(2)}) copy-start(f32[512]{0:T(512)S(1)} %broadcast_multiply_fusion.1) | copy-start | bytes 6148
  293.2 119.1 %copy-start.75 = (f32[512]{0:T(512)}, f32[512]{0:T(512)S(1)}, u32[]{:S(2)}) copy-start(f32[512]{0:T(512)S(1)} %fusion.77) | copy-start | bytes 6148
  437.1 19.3 %all-to-all-start.4 = ((bf16[512,2,576]{0,2,1:T(8,128)(2,1)}), bf16[512,2,576]{0,2,1:T(8,128)(2,1)S(1)}, u32[]{:S(2)}, u32[]{:S(2)}) async-start(bf16[512,2,576]{0,2,1:T(8,128)(2,1)} %bitcast.23), calls=%async_computation.4 | async-start | bytes 2359296 | tf_op jit(solution)/shard_map/all_to_all | solution.py:317
  545.4 18.5 %all-to-all-start.5 = ((bf16[2,512,576]{1,2,0:T(8,128)(2,1)}), bf16[2,512,576]{1,2,0:T(8,128)(2,1)S(1)}, u32[]{:S(2)}, u32[]{:S(2)}) async-start(bf16[2,512,576]{1,2,0:T(8,128)(2,1)} %bitcast.186), calls=%async_computation.5 | async-start | bytes 2359296 | tf_op jit(solution)/shard_map/all_to_all | solution.py:322
  563.9 18.5 %all-to-all-start.6 = ((bf16[2,512,576]{1,2,0:T(8,128)(2,1)}), bf16[2,512,576]{1,2,0:T(8,128)(2,1)}, u32[]{:S(2)}, u32[]{:S(2)}) async-start(bf16[2,512,576]{1,2,0:T(8,128)(2,1)} %copy.91), calls=%async_computation.6 | async-start | bytes 2359296 | tf_op jit(solution)/shard_map/all_to_all | solution.py:323
  571.9 28.1 %copy-start.9 = (f32[512,1152]{1,0:T(8,128)S(1)}, f32[512,1152]{1,0:T(8,128)}, u32[]{:S(2)}) copy-start(f32[512,1152]{1,0:T(8,128)} %copy-done.7) | copy-start | bytes 7077892
  571.9 28.1 %copy-start.64 = (f32[512]{0:T(512)S(1)}, f32[512]{0:T(512)}, u32[]{:S(2)}) copy-start(f32[512]{0:T(512)} %copy-done.63) | copy-start | bytes 6148
  582.4 17.6 %all-to-all-start.7 = ((bf16[2,512,576]{1,2,0:T(8,128)(2,1)}), bf16[2,512,576]{1,2,0:T(8,128)(2,1)}, u32[]{:S(2)}, u32[]{:S(2)}) async-start(bf16[2,512,576]{1,2,0:T(8,128)(2,1)} %copy.92), calls=%async_computation.7 | async-start | bytes 2359296 | tf_op jit(solution)/shard_map/all_to_all | solution.py:324
  586.8 99.9 %reduce-scatter.31.cloned.1.call-start = ((), (), s32[]{:S(2)}) async-start(), calls=%async_computation.26 | async-start | bytes 5308416
  641.6 113.4 %reduce-scatter.43.cloned.1.call-start = ((), (), s32[]{:S(2)}) async-start(), calls=%async_computation.32 | async-start | bytes 2820096
  647.3 211.6 %reduce-scatter.41.cloned.1.call-start = ((), (), s32[]{:S(2)}) async-start(), calls=%async_computation.31 | async-start | bytes 8460288
  657.9 325.7 %reduce-scatter.29.cloned.1.call-start = ((), (), s32[]{:S(2)}) async-start(), calls=%async_computation.25 | async-start | bytes 11280384 | tf_op jit(solution)/shard_map/reduce_scatter | solution.py:71
  672.1 435.9 %reduce-scatter.25.cloned.1.call-start = ((), (), s32[]{:S(2)}) async-start(), calls=%async_computation.23 | async-start | bytes 11280384 | tf_op jit(solution)/shard_map/reduce_scatter | solution.py:71
  683.6 73.2 %copy-start.67 = (f32[1152]{0:T(1024)S(1)}, f32[1152]{0:T(1024)}, u32[]{:S(2)}) copy-start(f32[1152]{0:T(1024)} %get-tuple-element.282) | copy-start | bytes 13828
  683.6 439.1 %reduce-scatter.35.cloned.1.call-start = ((), (), s32[]{:S(2)}) async-start(), calls=%async_computation.28 | async-start | bytes 442368
  756.8 471.3 %reduce-scatter.39.cloned.1.call-start = ((), (), s32[]{:S(2)}) async-start(), calls=%async_computation.30 | async-start | bytes 8460288
  761.5 487.8 %reduce-scatter.33.cloned.1.call-start = ((), (), s32[]{:S(2)}) async-start(), calls=%async_computation.27 | async-start | bytes 1327104
  861.2 409.4 %reduce-scatter.37.cloned.1.call-start = ((), (), s32[]{:S(2)}) async-start(), calls=%async_computation.29 | async-start | bytes 1327104
  985.9 124.3 %copy-start.69 = (f32[1152]{0:T(1024)S(1)}, f32[1152]{0:T(1024)}, u32[]{:S(2)}) copy-start(f32[1152]{0:T(1024)} %get-tuple-element.280) | copy-start | bytes 13828
  985.9 124.3 %copy-start.70 = (f32[4608]{0:T(1024)S(1)}, f32[4608]{0:T(1024)}, u32[]{:S(2)}) copy-start(f32[4608]{0:T(1024)} %get-tuple-element.278) | copy-start | bytes 55300
  985.9 124.4 %copy-start.68 = (f32[1152]{0:T(1024)S(1)}, f32[1152]{0:T(1024)}, u32[]{:S(2)}) copy-start(f32[1152]{0:T(1024)} %get-tuple-element.276) | copy-start | bytes 13828
  985.9 302.9 %reduce-scatter.27.cloned.1.call-start = ((), (), s32[]{:S(2)}) async-start(), calls=%async_computation.24 | async-start | bytes 995328 | tf_op jit(solution)/shard_map/reduce_scatter | solution.py:370
  1108.1 226.8 %copy-start.53 = (f32[16128]{0:T(1024)S(1)}, f32[16128]{0:T(1024)}, u32[]{:S(2)}) copy-start(f32[16128]{0:T(1024)} %param.53) | copy-start | bytes 193540
  1108.1 226.8 %copy-start.57 = (f32[16128]{0:T(1024)S(1)}, f32[16128]{0:T(1024)}, u32[]{:S(2)}) copy-start(f32[16128]{0:T(1024)} %param.55) | copy-start | bytes 193540
  1108.1 226.8 %copy-start.58 = (f32[16128]{0:T(1024)S(1)}, f32[16128]{0:T(1024)}, u32[]{:S(2)}) copy-start(f32[16128]{0:T(1024)} %param.54) | copy-start | bytes 193540
  1109.7 225.9 %copy-start.46 = (f32[72,576]{1,0:T(8,128)S(1)}, f32[72,576]{1,0:T(8,128)}, u32[]{:S(2)}) copy-start(f32[72,576]{1,0:T(8,128)} %param.44) | copy-start | bytes 497668
  1109.7 225.9 %copy-start.54 = (f32[72,576]{1,0:T(8,128)S(1)}, f32[72,576]{1,0:T(8,128)}, u32[]{:S(2)}) copy-start(f32[72,576]{1,0:T(8,128)} %param.46) | copy-start | bytes 497668
  1109.7 225.9 %copy-start.55 = (f32[72,576]{1,0:T(8,128)S(1)}, f32[72,576]{1,0:T(8,128)}, u32[]{:S(2)}) copy-start(f32[72,576]{1,0:T(8,128)} %param.45) | copy-start | bytes 497668
  1124.5 168.0 %copy-start.60 = (f32[16128]{0:T(1024)S(1)}, f32[16128]{0:T(1024)}, u32[]{:S(2)}) copy-start(f32[16128]{0:T(1024)} %copy-done.59) | copy-start | bytes 193540
  1124.5 212.0 %copy-start.31 = (f32[72,1728]{1,0:T(8,128)S(1)}, f32[72,1728]{1,0:T(8,128)}, u32[]{:S(2)}) copy-start(f32[72,1728]{1,0:T(8,128)} %param.41) | copy-start | bytes 1492996
  1124.5 212.0 %copy-start.49 = (f32[72,1728]{1,0:T(8,128)S(1)}, f32[72,1728]{1,0:T(8,128)}, u32[]{:S(2)}) copy-start(f32[72,1728]{1,0:T(8,128)} %param.43) | copy-start | bytes 1492996
  1124.5 212.0 %copy-start.50 = (f32[72,1728]{1,0:T(8,128)S(1)}, f32[72,1728]{1,0:T(8,128)}, u32[]{:S(2)}) copy-start(f32[72,1728]{1,0:T(8,128)} %param.42) | copy-start | bytes 1492996
  (66 other events, 413.3 us)
Sparse Core Ops, SparseCore 0:
  10.8 74.8 all-gather.10
  88.4 70.5 all-gather.12
  161.7 41.6 all-gather.14
  205.6 87.3 all-gather.16
  295.7 86.8 all-gather.18
  641.7 44.9 reduce-scatter.30
  691.1 63.8 reduce-scatter.42
  759.1 99.7 reduce-scatter.40
  863.5 120.0 reduce-scatter.28
  988.0 119.9 reduce-scatter.24
  1110.9 11.7 reduce-scatter.34
  1127.3 100.8 reduce-scatter.38
  1231.0 18.3 reduce-scatter.32
  1252.0 18.5 reduce-scatter.36
  1272.7 16.0 reduce-scatter.26
where the time goes:
time: 1360 us; the launch traced here: 1350 us
  waiting for transfers between devices  818 us (60%)
  matrix products  230 us (17%)
  other arithmetic  89.4 us (7%)
  blocking collectives  78 us (6%)
  local copies, waits for them, and re-layouts  70.1 us (5%)
  starting transfers between devices  41.3 us (3%)
  between operations  25.9 us (2%)
    unnamed x22, waiting for transfers between devices  320 us
    reduce_scatter x2, waiting for transfers between devices, rows_seq(): lax.psum_scatter(lax.dot_general(left_side, right_side, (((0,), (0,)), ((...  243 us
    all_gather x5, waiting for transfers between devices, fold_rows(): lax.all_gather(weight_slab, 'seq', axis=0, tiled=True)  151 us
    dot_general x5, matrix products, fold_rows(): jnp.dot(left_side, lax.all_gather(weight_slab, 'seq', axis=0, tiled=True)...  48 us
    dot_general x4, matrix products, back_cols(): lax.dot_general(gradient, lax.all_gather(weight_slab, 'seq', axis=0, tile...  43 us
    psum x1, blocking collectives, on_device(): lax.psum((bias_share, local_squares), ('seq', 'head'))  40.3 us
    dot_general x4, matrix products, rows_seq(): lax.dot_general(left_side, right_side, (((0,), (0,)), ((), ())), preferre...  36.9 us
    unnamed x172, local copies, waits for them, and re-layouts  36 us
  transfers between devices with their start and end apart: 23, of which 21 were waited for; matrix products, arithmetic and copies ran while one was open for 13% of the time, Pallas kernels for 0%

commit v1 on v0

--- a/solution.py
+++ b/solution.py
@@ -1,8 +1,12 @@
+import functools
 import math
 
 import jax
 import jax.numpy as jnp
 from jax import lax
+from jax.experimental import pallas as pl
+from jax.experimental.pallas import tpu as pltpu
+from jax.sharding import Mesh
 from jax.sharding import PartitionSpec as P
 
 D = 1152
@@ -455,7 +459,711 @@
     )
 
 
-def solution(mesh):
+MESH = pl.DeviceIdType.MESH
+PIECES = {"q": (144, 864, 96), "p": (72, 576, None), "u": (144, 1152, 96), "d": (288, 576, 192)}
+NAMES = ("q", "p", "u", "d")
+
+
+def place():
+    return tuple(lax.axis_index(a) for a in ("z", "x", "c", "y"))
+
+
+def at_z(k):
+    z = lax.axis_index("z")
+    return (z + 1 - 2 * (z % 2), (z + 2) % 4, 3 - z)[k - 1]
+
+
+def rdma(src, dst, send, recv, to):
+    return pltpu.make_async_remote_copy(
+        src_ref=src, dst_ref=dst, send_sem=send, recv_sem=recv, device_id=to, device_id_type=MESH
+    )
+
+
+def greet(partners):
+    barrier = pltpu.get_barrier_semaphore()
+    for to in partners:
+        pl.semaphore_signal(barrier, inc=1, device_id=to, device_id_type=MESH)
+    pl.semaphore_wait(barrier, len(partners))
+
+
+def parts_of(rows, cut, k):
+    if cut is None:
+        return ((0, rows), None) if k % 2 == 0 else (None, (0, rows))
+    return (0, cut), (cut, rows - cut)
+
+
+def gather_kernel(*refs):
+    own, full = refs[0:4], refs[4:8]
+    lsem, zs, zr, xs, xr, ys, yr, fs, fr = refs[8:]
+    z, x, c, y = place()
+    xn, yn = (z, 1 - x, c, y), (z, x, c, 1 - y)
+    zn = [None] + [(at_z(k), x, c, y) for k in (1, 2, 3)]
+    greet([xn, yn] + zn[1:])
+    pending = []
+    for w in range(4):
+        mine = full[w].at[y, z, x]
+        pltpu.make_async_copy(own[w], mine, lsem.at[w]).start()
+        for k in (1, 2, 3):
+            d = rdma(own[w], mine, zs.at[w, k], zr.at[w, k], zn[k])
+            d.start()
+            pending.append(d)
+        for to, s, r in ((xn, xs, xr), (yn, ys, yr)):
+            d = rdma(own[w], mine, s.at[w, 0], r.at[w, 0], to)
+            d.start()
+            pending.append(d)
+    for w in range(4):
+        rows, _, cut = PIECES[NAMES[w]]
+        for k in (1, 2, 3):
+            piece = full[w].at[y, at_z(k), x]
+            rdma(piece, piece, zs.at[w, k], zr.at[w, k], zn[k]).wait_recv()
+            for to, s, r in ((xn, xs, xr), (yn, ys, yr)):
+                d = rdma(piece, piece, s.at[w, k], r.at[w, k], to)
+                d.start()
+                pending.append(d)
+        for k in range(4):
+            zk = z if k == 0 else at_z(k)
+            by_x, by_y = parts_of(rows, cut, k)
+            piece = full[w].at[y, zk, 1 - x]
+            rdma(piece, piece, xs.at[w, k], xr.at[w, k], xn).wait_recv()
+            if by_x is not None:
+                part = full[w].at[y, zk, 1 - x, pl.ds(*by_x)]
+                d = rdma(part, part, fs.at[w, k, 0], fr.at[w, k, 0], yn)
+                d.start()
+                pending.append(d)
+            piece = full[w].at[1 - y, zk, x]
+            rdma(piece, piece, ys.at[w, k], yr.at[w, k], yn).wait_recv()
+            if by_y is not None:
+                part = full[w].at[1 - y, zk, x, pl.ds(*by_y)]
+                d = rdma(part, part, fs.at[w, k, 1], fr.at[w, k, 1], xn)
+                d.start()
+                pending.append(d)
+    for w in range(4):
+        rows, _, cut = PIECES[NAMES[w]]
+        pltpu.make_async_copy(own[w], full[w].at[y, z, x], lsem.at[w]).wait()
+        for k in range(4):
+            zk = z if k == 0 else at_z(k)
+            for i, span in enumerate(parts_of(rows, cut, k)):
+                if span is not None:
+                    part = full[w].at[1 - y, zk, 1 - x, pl.ds(*span)]
+                    rdma(part, part, fs.at[w, k, i], fr.at[w, k, i], xn).wait_recv()
+    for d in pending:
+        d.wait_send()
+
+
+def gather_weights(own):
+    any_space = pl.BlockSpec(memory_space=pl.ANY)
+    dma = pltpu.SemaphoreType.DMA
+    return pl.pallas_call(
+        gather_kernel,
+        out_shape=[
+            jax.ShapeDtypeStruct((2, 4, 2) + PIECES[n][:2], jnp.bfloat16) for n in NAMES
+        ],
+        in_specs=[any_space] * 4,
+        out_specs=[any_space] * 4,
+        scratch_shapes=[dma((4,))] + [dma((4, 4))] * 6 + [dma((4, 4, 2))] * 2,
+        compiler_params=pltpu.CompilerParams(collective_id=0, has_side_effects=True),
+        name="gather_weights",
+    )(*own)
+
+
+def scatter_kernel(*refs):
+    grads, outs = refs[0:4], refs[4:8]
+    held, diag, by_x, by_y, by_z = (refs[8 + 4 * i : 12 + 4 * i] for i in range(5))
+    lsem, fs, fr, xs, xr, ys, yr, zs, zr = refs[28:]
+    z, x, c, y = place()
+    xn, yn = (z, 1 - x, c, y), (z, x, c, 1 - y)
+    zn = [None] + [(at_z(k), x, c, y) for k in (1, 2, 3)]
+    f32 = jnp.float32
+    for w in range(4):
+        pltpu.make_async_copy(grads[w], held[w], lsem.at[w]).start()
+    greet([xn, yn] + zn[1:])
+    pending = []
+    order = (3, 2, 1, 0)
+
+    def z_of(k):
+        return z if k == 0 else at_z(k)
+
+    for w in range(4):
+        rows, _, cut = PIECES[NAMES[w]]
+        pltpu.make_async_copy(grads[w], held[w], lsem.at[w]).wait()
+        for k in order:
+            spans = parts_of(rows, cut, k)
+            for i, (span, to) in enumerate(zip(spans, (yn, xn))):
+                if span is not None:
+                    d = rdma(
+                        held[w].at[1 - y, z_of(k), 1 - x, pl.ds(*span)],
+                        diag[w].at[k, pl.ds(*span)],
+                        fs.at[w, k, i],
+                        fr.at[w, k, i],
+                        to,
+                    )
+                    d.start()
+                    pending.append(d)
+    for w in range(4):
+        rows, _, cut = PIECES[NAMES[w]]
+        for k in order:
+            spans = parts_of(rows, cut, k)
+            for i, span in enumerate(spans):
+                piece = held[w].at[(y, z_of(k), 1 - x) if i == 0 else (1 - y, z_of(k), x)]
+                if span is not None:
+                    part = diag[w].at[k, pl.ds(*span)]
+                    rdma(part, part, fs.at[w, k, i], fr.at[w, k, i], xn).wait_recv()
+                    target = piece.at[pl.ds(*span)]
+                    target[...] = (target[...].astype(f32) + part[...].astype(f32)).astype(
+                        jnp.bfloat16
+                    )
+                box, to, s, r = ((by_x, xn, xs, xr), (by_y, yn, ys, yr))[i]
+                d = rdma(piece, box[w].at[k], s.at[w, k], r.at[w, k], to)
+                d.start()
+                pending.append(d)
+    for w in range(4):
+        for k in order:
+            for box, s, r in ((by_x, xs, xr), (by_y, ys, yr)):
+                part = box[w].at[k]
+                rdma(part, part, s.at[w, k], r.at[w, k], xn).wait_recv()
+            piece = held[w].at[y, z_of(k), x]
+            total = piece[...].astype(f32) + by_x[w][k].astype(f32) + by_y[w][k].astype(f32)
+            if k == 0:
+                outs[w][...] = total
+            else:
+                piece[...] = total.astype(jnp.bfloat16)
+                d = rdma(piece, by_z[w].at[k - 1], zs.at[w, k - 1], zr.at[w, k - 1], zn[k])
+                d.start()
+                pending.append(d)
+    for w in range(4):
+        total = outs[w][...]
+        for k in (1, 2, 3):
+            part = by_z[w].at[k - 1]
+            rdma(part, part, zs.at[w, k - 1], zr.at[w, k - 1], zn[k]).wait_recv()
+            total = total + part[...].astype(f32)
+        outs[w][...] = total
+    for d in pending:
+        d.wait_send()
+
+
+def scatter_grads(grads):
+    dma = pltpu.SemaphoreType.DMA
+    shapes = [PIECES[n][:2] for n in NAMES]
+
+    def boxes(*lead):
+        return [pltpu.VMEM(lead + s, jnp.bfloat16) for s in shapes]
+
+    return pl.pallas_call(
+        scatter_kernel,
+        out_shape=[jax.ShapeDtypeStruct(s, jnp.float32) for s in shapes],
+        in_specs=[pl.BlockSpec(memory_space=pl.ANY)] * 4,
+        out_specs=[pl.BlockSpec(memory_space=pltpu.VMEM)] * 4,
+        scratch_shapes=boxes(2, 4, 2)
+        + boxes(4)
+        + boxes(4)
+        + boxes(4)
+        + boxes(3)
+        + [dma((4,))]
+        + [dma((4, 4, 2))] * 2
+        + [dma((4, 4))] * 6,
+        compiler_params=pltpu.CompilerParams(
+            collective_id=1, has_side_effects=True, vmem_limit_bytes=56 * 2**20
+        ),
+        name="scatter_grads",
+    )(*grads)
+
+
+def mod_kernel(cond_ref, weight_ref, out_ref, lhs, conds, part, got_z, mid, got_x, near, got_c, s, r):
+    z, x, c, y = place()
+    xn, yn, twin = (z, 1 - x, c, y), (z, x, c, 1 - y), (z, x, 1 - c, y)
+    zn = [None] + [(at_z(k), x, c, y) for k in (1, 2, 3)]
+    greet([xn, yn, twin] + zn[1:])
+    conds[z, x, c] = cond_ref[...]
+    d = rdma(conds.at[z, x, c], conds.at[z, x, c], s.at[0], r.at[0], twin)
+    d.start()
+    d.wait()
+    d = rdma(conds.at[z, x], conds.at[z, x], s.at[1], r.at[1], xn)
+    d.start()
+    d.wait()
+    ds = [rdma(conds.at[z], conds.at[z], s.at[1 + k], r.at[1 + k], zn[k]) for k in (1, 2, 3)]
+    for d in ds:
+        d.start()
+    for d in ds:
+        d.wait()
+    me = (z * 2 + x) * 2 + c
+    for i in range(16):
+        lhs[pl.ds(i, 1), :] = conds[i // 4, i // 2 % 2, i % 2, pl.ds(me, 1), :]
+    result = jnp.dot(
+        lhs[:, :72].astype(jnp.bfloat16), weight_ref[...], preferred_element_type=jnp.float32
+    )
+    for i in range(16):
+        part[i // 4, i // 2 % 2, i % 2] = result[i : i + 1]
+    ds = [
+        rdma(part.at[at_z(k)], got_z.at[k - 1], s.at[4 + k], r.at[4 + k], zn[k]) for k in (1, 2, 3)
+    ]
+    for d in ds:
+        d.start()
+    for d in ds:
+        d.wait()
+    mid[...] = part[z] + got_z[0] + got_z[1] + got_z[2]
+    d = rdma(mid.at[1 - x], got_x, s.at[8], r.at[8], xn)
+    d.start()
+    d.wait()
+    near[0] = mid[x] + got_x[...]
+    d = rdma(near.at[0], got_c, s.at[9], r.at[9], twin)
+    d.start()
+    d.wait()
+    near[1] = near[0] + got_c[...]
+    out_ref[y] = near[1, y]
+    d = rdma(near.at[1, 1 - y], out_ref.at[y], s.at[10], r.at[10], yn)
+    d.start()
+    d.wait()
+
+
+def image_modulation(cond, weight):
+    f32, vm = jnp.float32, pltpu.VMEM
+    return pl.pallas_call(
+        mod_kernel,
+        out_shape=[
+            jax.ShapeDtypeStruct((2, 1, 3456), f32),
+            jax.ShapeDtypeStruct((16, 128), f32),
+        ],
+        in_specs=[pl.BlockSpec(memory_space=vm)] * 2,
+        out_specs=[pl.BlockSpec(memory_space=vm)] * 2,
+        scratch_shapes=[
+            vm((4, 2, 2, 16, 128), f32),
+            vm((4, 2, 2, 1, 3456), f32),
+            vm((3, 2, 2, 1, 3456), f32),
+            vm((2, 2, 1, 3456), f32),
+            vm((2, 1, 3456), f32),
+            vm((2, 2, 1, 3456), f32),
+            vm((2, 1, 3456), f32),
+            pltpu.SemaphoreType.DMA((11,)),
+            pltpu.SemaphoreType.DMA((11,)),
+        ],
+        compiler_params=pltpu.CompilerParams(collective_id=2, has_side_effects=True),
+        name="image_modulation",
+    )(cond, weight)
+
+
+def totals_kernel(mod_ref, bias_ref, mods, sums, got_m, got_b, got_z, s, r):
+    z, x, c, y = place()
+    xn, yn, twin = (z, 1 - x, c, y), (z, x, c, 1 - y), (z, x, 1 - c, y)
+    zn = [None] + [(at_z(k), x, c, y) for k in (1, 2, 3)]
+    greet([xn, yn, twin] + zn[1:])
+    d = rdma(mod_ref, got_m, s.at[0], r.at[0], twin)
+    e = rdma(bias_ref, got_b.at[0], s.at[1], r.at[1], twin)
+    d.start()
+    e.start()
+    d.wait()
+    e.wait()
+    mods[z, x, y] = (mod_ref[...] + got_m[...]).astype(jnp.bfloat16)
+    sums[...] = bias_ref[...] + got_b[0]
+    d = rdma(mods.at[z, x, y], mods.at[z, x, y], s.at[2], r.at[2], yn)
+    e = rdma(sums, got_b.at[1], s.at[3], r.at[3], yn)
+    d.start()
+    e.start()
+    d.wait()
+    e.wait()
+    sums[...] = sums[...] + got_b[1]
+    d = rdma(mods.at[z, x], mods.at[z, x], s.at[4], r.at[4], xn)
+    e = rdma(sums, got_b.at[2], s.at[5], r.at[5], xn)
+    d.start()
+    e.start()
+    d.wait()
+    e.wait()
+    got_z[0] = sums[...] + got_b[2]
+    ds = [rdma(mods.at[z], mods.at[z], s.at[5 + k], r.at[5 + k], zn[k]) for k in (1, 2, 3)]
+    ds += [rdma(got_z.at[0], got_z.at[k], s.at[8 + k], r.at[8 + k], zn[k]) for k in (1, 2, 3)]
+    for d in ds:
+        d.start()
+    for d in ds:
+        d.wait()
+    sums[...] = (got_z[0] + got_z[1]) + (got_z[2] + got_z[3])
+
+
+def share_totals(mod_grad, bias_grad):
+    f32, vm = jnp.float32, pltpu.VMEM
+    return pl.pallas_call(
+        totals_kernel,
+        out_shape=[
+            jax.ShapeDtypeStruct((4, 2, 2, 16, 432), jnp.bfloat16),
+            jax.ShapeDtypeStruct((72, 128), f32),
+        ],
+        in_specs=[pl.BlockSpec(memory_space=vm)] * 2,
+        out_specs=[pl.BlockSpec(memory_space=vm)] * 2,
+        scratch_shapes=[
+            vm((16, 432), f32),
+            vm((3, 72, 128), f32),
+            vm((4, 72, 128), f32),
+            pltpu.SemaphoreType.DMA((12,)),
+            pltpu.SemaphoreType.DMA((12,)),
+        ],
+        compiler_params=pltpu.CompilerParams(collective_id=3, has_side_effects=True),
+        name="share_totals",
+    )(mod_grad, bias_grad)
+
+
+def norm_kernel(in_ref, out_ref, box, got_z, s, r):
+    z, x, c, y = place()
+    xn, yn, twin = (z, 1 - x, c, y), (z, x, c, 1 - y), (z, x, 1 - c, y)
+    zn = [None] + [(at_z(k), x, c, y) for k in (1, 2, 3)]
+    greet([xn, yn, twin] + zn[1:])
+    total = in_ref[...]
+    for i, to in enumerate((twin, yn, xn)):
+        box[2 * i] = total
+        d = rdma(box.at[2 * i], box.at[2 * i + 1], s.at[i], r.at[i], to)
+        d.start()
+        d.wait()
+        total = total + box[2 * i + 1]
+    got_z[0] = total
+    ds = [rdma(got_z.at[0], got_z.at[k], s.at[2 + k], r.at[2 + k], zn[k]) for k in (1, 2, 3)]
+    for d in ds:
+        d.start()
+    for d in ds:
+        d.wait()
+    out_ref[...] = (got_z[0] + got_z[1]) + (got_z[2] + got_z[3])
+
+
+def sum_everywhere(value):
+    f32, vm = jnp.float32, pltpu.VMEM
+    return pl.pallas_call(
+        norm_kernel,
+        out_shape=jax.ShapeDtypeStruct((8, 128), f32),
+        in_specs=[pl.BlockSpec(memory_space=vm)],
+        out_specs=pl.BlockSpec(memory_space=vm),
+        scratch_shapes=[
+            vm((6, 8, 128), f32),
+            vm((4, 8, 128), f32),
+            pltpu.SemaphoreType.DMA((6,)),
+            pltpu.SemaphoreType.DMA((6,)),
+        ],
+        compiler_params=pltpu.CompilerParams(collective_id=4, has_side_effects=True),
+        name="sum_everywhere",
+    )(value)
+
+
+def swap_halves(value):
+    return lax.ppermute(value, ("c", "y"), [(0, 0), (1, 2), (2, 1), (3, 3)])
+
+
+def to_twin(value):
+    return lax.ppermute(value, "c", [(0, 1), (1, 0)])
+
+
+def both_halves(value):
+    c = lax.axis_index("c")
+    other = to_twin(value)
+    return jnp.where(c == 0, jnp.concatenate([value, other]), jnp.concatenate([other, value]))
+
+
+def sum_halves(value):
+    c = lax.axis_index("c")
+    half = value.shape[0] // 2
+    mine = lax.dynamic_slice_in_dim(value, c * half, half)
+    other = to_twin(lax.dynamic_slice_in_dim(value, (1 - c) * half, half).astype(jnp.bfloat16))
+    return mine + other.astype(jnp.float32)
+
+
+def wide(left, weight):
+    return jnp.concatenate(
+        [jnp.dot(left, weight[i], preferred_element_type=jnp.float32) for i in (0, 1)], axis=1
+    )
+
+
+def wide_back(gradient, weight):
+    half = weight.shape[2]
+    return sum(
+        lax.dot_general(
+            gradient[:, i * half : (i + 1) * half],
+            weight[i],
+            (((1,), (1,)), ((), ())),
+            preferred_element_type=jnp.float32,
+        )
+        for i in (0, 1)
+    )
+
+
+def weight_grad(left, right, name):
+    rows, cols, _ = PIECES[name]
+    half = right.shape[1] // 2
+    return jnp.stack(
+        [
+            lax.dot_general(
+                left,
+                right[:, i * half : (i + 1) * half],
+                (((0,), (0,)), ((), ())),
+                preferred_element_type=jnp.float32,
+            ).astype(jnp.bfloat16)
+            for i in (0, 1)
+        ]
+    ).reshape(2, 4, 2, rows, cols)
+
+
+def core_columns(shard, width):
+    rows, cols = shard.shape
+    blocks = shard.reshape(rows, cols // (2 * width), 2, width)
+    return blocks.transpose(2, 0, 1, 3).reshape(2, rows, cols // 2)
+
+
+def chip_piece(shard, width):
+    c = lax.axis_index("c")
+    split = core_columns(shard, width)
+    mine = lax.dynamic_index_in_dim(split, c, 0, keepdims=False)
+    other = to_twin(lax.dynamic_index_in_dim(split, 1 - c, 0, keepdims=False))
+    return jnp.where(c == 0, jnp.concatenate([mine, other]), jnp.concatenate([other, mine]))
+
+
+def shard_from_pieces(piece, width):
+    c = lax.axis_index("c")
+    half = piece.shape[0] // 2
+    mine = lax.dynamic_slice_in_dim(piece, c * half, half)
+    other = to_twin(lax.dynamic_slice_in_dim(piece, (1 - c) * half, half))
+    split = jnp.where(c == 0, jnp.stack([mine, other]), jnp.stack([other, mine]))
+    cols = piece.shape[1]
+    return split.reshape(2, half, cols // width, width).transpose(1, 2, 0, 3).reshape(half, 2 * cols)
+
+
+def core_bias(piece, width):
+    c = lax.axis_index("c")
+    blocks = piece.reshape(-1, 2, width)
+    return lax.dynamic_index_in_dim(blocks, c, 1, keepdims=False).reshape(-1)
+
+
+def bias_slot(piece, width):
+    c = lax.axis_index("c")
+    blocks = piece.reshape(-1, 1, width)
+    pick = (jnp.arange(2) == c).astype(jnp.float32)[None, :, None]
+    return (blocks * pick).reshape(-1)
+
+
+def on_device_fast(
+    tokens,
+    cotangent,
+    buckets,
+    timesteps,
+    labels,
+    class_table,
+    step_count,
+    modulate_master,
+    modulate_first,
+    modulate_second,
+    attend_master,
+    attend_first,
+    attend_second,
+    project_master,
+    project_first,
+    project_second,
+    expand_master,
+    expand_first,
+    expand_second,
+    reduce_master,
+    reduce_first,
+    reduce_second,
+    biases_master,
+    biases_first,
+    biases_second,
+):
+    z, x, c, y = place()
+    bf16, f32 = jnp.bfloat16, jnp.float32
+    block = FF // 16
+    own = (
+        chip_piece(attend_master.astype(bf16), HEAD_DIM),
+        project_master.astype(bf16),
+        chip_piece(expand_master.astype(bf16), block),
+        reduce_master.astype(bf16),
+    )
+    weight_q, weight_p, weight_u, weight_d = gather_weights(own)
+    weight_q = weight_q.reshape(2, D, 864)
+    weight_p = weight_p.reshape(2, 576, 576)
+    weight_u = weight_u.reshape(2, D, D)
+    weight_d = weight_d.reshape(2, 2304, 576)
+
+    class_row = lax.dynamic_slice_in_dim(class_table, labels[0], 1).astype(f32)
+    condition = jax.nn.silu(class_row + time_features(timesteps, D)).astype(bf16).astype(f32)
+    cond_tiles = jnp.pad(condition.reshape(16, 72), ((0, 0), (0, 56)))
+    bias_low = biases_master.astype(bf16).astype(f32)
+    modulation, cond_all = image_modulation(cond_tiles, modulate_master.astype(bf16))
+    modulation = modulation.reshape(6 * D) + bias_low[: 6 * D]
+    shift_one, scale_one, gating_one, shift_two, scale_two, gating_two = (
+        modulation[i * D : (i + 1) * D][None, :] for i in range(6)
+    )
+    offset_base = 6 * D
+    bias_query = core_bias(bias_low[offset_base : offset_base + D], HEAD_DIM)
+    bias_value = core_bias(bias_low[offset_base + D : offset_base + 2 * D], HEAD_DIM)
+    bias_proj = bias_low[offset_base + 2 * D : offset_base + 3 * D]
+    bias_hidden = core_bias(bias_low[offset_base + 3 * D : offset_base + 3 * D + FF], block)
+    bias_output = bias_low[offset_base + 3 * D + FF :]
+
+    moved = swap_halves(jnp.stack([tokens, cotangent]))
+    tokens, cotangent = moved[0], moved[1]
+    bucket = swap_halves(buckets)
+    unit_cells = SIDE // 8
+    heights = table_pick(bucket, row_units) * unit_cells
+    widths = table_pick(bucket, col_units) * unit_cells
+    lengths = heights * widths
+    half_rows = tokens.shape[0]
+    position = c * half_rows + jnp.arange(half_rows, dtype=jnp.int32)
+    live_rows = (position < lengths[0]).astype(f32)
+    residual_zero = tokens.astype(f32) + grid_features(position, widths, D)
+
+    hidden_attend = both_halves(modulate(residual_zero, shift_one, scale_one).astype(bf16))
+    packed = wide(hidden_attend, weight_q)
+    queries = (packed[:, :576] + bias_query).astype(bf16)
+    key_rows = packed[:, 576:1152].astype(bf16)
+    value_rows = (packed[:, 1152:] + bias_value).astype(bf16)
+    attention, log_sums = attend(queries, key_rows, value_rows, lengths)
+    branch_attend = sum_halves(wide(attention, weight_p)) + bias_proj
+    residual_one = residual_zero + gating_one * branch_attend
+    hidden_expand = both_halves(modulate(residual_one, shift_two, scale_two).astype(bf16))
+    widened = wide(hidden_expand, weight_u) + bias_hidden
+    activated = jax.nn.gelu(widened, approximate=True).astype(bf16)
+    branch_expand = sum_halves(wide(activated, weight_d)) + bias_output
+    output = swap_halves((residual_one + gating_two * branch_expand).astype(bf16))
+
+    outer_grad = cotangent.astype(f32) * live_rows[:, None]
+    gating_later = jnp.sum(outer_grad * branch_expand, axis=0)
+    closing_grad = (outer_grad * gating_two).astype(bf16)
+    closing_all = both_halves(closing_grad)
+    active_grad = wide_back(closing_all, weight_d)
+    _, gelu_pullback = jax.vjp(lambda inner: jax.nn.gelu(inner, approximate=True), widened)
+    widened_grad = gelu_pullback(active_grad)[0].astype(bf16)
+    grad_reduce = weight_grad(activated, closing_all, "d")
+    grad_expand = weight_grad(hidden_expand, widened_grad, "u")
+    hidden_grad = sum_halves(wide_back(widened_grad, weight_u))
+
+    def norm_back(residual, scaling, gradient):
+        average = jnp.mean(residual, axis=-1, keepdims=True)
+        centred = residual - average
+        inverse = lax.rsqrt(jnp.mean(centred * centred, axis=-1, keepdims=True) + 1e-06)
+        normed = centred * inverse
+        inner = gradient * (1.0 + scaling)
+        part = (
+            inner
+            - jnp.mean(inner, axis=-1, keepdims=True)
+            - normed * jnp.mean(inner * normed, axis=-1, keepdims=True)
+        ) * inverse
+        return part, jnp.sum(gradient, axis=0), jnp.sum(gradient * normed, axis=0)
+
+    residual_part, shift_later, scale_later = norm_back(residual_one, scale_two, hidden_grad)
+    middle_grad = outer_grad + residual_part
+    gating_early = jnp.sum(middle_grad * branch_attend, axis=0)
+    branch_grad = (middle_grad * gating_one).astype(bf16)
+    branch_all = both_halves(branch_grad)
+    heads_grad = wide_back(branch_all, weight_p).astype(bf16)
+    grad_project = weight_grad(attention, branch_all, "p")
+    query_grad, keyrow_grad, value_grad = attend_back(
+        queries, key_rows, value_rows, heads_grad, log_sums, lengths
+    )
+    packed_grad = jnp.concatenate([query_grad, keyrow_grad, value_grad], axis=1)
+    grad_attend = weight_grad(hidden_attend, packed_grad, "q")
+    normed_grad = sum_halves(wide_back(packed_grad, weight_q))
+    input_part, shift_early, scale_early = norm_back(residual_zero, scale_one, normed_grad)
+    input_grad = swap_halves((middle_grad + input_part).astype(bf16)).astype(f32)
+
+    mod_grad = jnp.concatenate(
+        [shift_early, scale_early, gating_early, shift_later, scale_later, gating_later]
+    )
+    bias_share = jnp.concatenate(
+        [
+            bias_slot(jnp.sum(query_grad.astype(f32), axis=0), HEAD_DIM),
+            bias_slot(jnp.sum(value_grad.astype(f32), axis=0), HEAD_DIM),
+            jnp.sum(branch_grad.astype(f32), axis=0),
+            bias_slot(jnp.sum(widened_grad.astype(f32), axis=0), block),
+            jnp.sum(closing_grad.astype(f32), axis=0),
+        ]
+    )
+    sums_q, sums_p, sums_u, sums_d = scatter_grads(
+        (grad_attend, grad_project, grad_expand, grad_reduce)
+    )
+    mods, bias_sums = share_totals(mod_grad.reshape(16, 432), bias_share.reshape(72, 128))
+    mods = mods.reshape(16, 2, 3456)
+    grad_mod = lax.dot_general(
+        cond_all[:, :72].astype(bf16),
+        lax.dynamic_index_in_dim(mods, y, 1, keepdims=False),
+        (((0,), (0,)), ((), ())),
+        preferred_element_type=f32,
+    )
+    bias_total = jnp.concatenate([jnp.sum(mods.astype(f32), axis=0).reshape(-1), bias_sums.reshape(-1)])
+    grad_attend = shard_from_pieces(sums_q, HEAD_DIM)
+    grad_expand = shard_from_pieces(sums_u, block)
+    reduced = (grad_mod, grad_attend, sums_p, grad_expand, sums_d)
+    local_squares = sum(jnp.sum(gradient * gradient) for gradient in reduced)
+    square_total = sum_everywhere(jnp.full((8, 128), local_squares))[0, 0]
+    grad_norm = jnp.sqrt(square_total + jnp.sum(bias_total * bias_total))
+    clip_factor = jnp.minimum(1.0, 1.0 / (grad_norm + 1e-06))
+    correction = 1.0 - jnp.power(0.5, step_count.astype(f32))
+    rate = 0.5 * D ** (-0.5)
+    states = (
+        (modulate_master, modulate_first, modulate_second, grad_mod, rate),
+        (attend_master, attend_first, attend_second, grad_attend, rate),
+        (project_master, project_first, project_second, sums_p, rate),
+        (expand_master, expand_first, expand_second, grad_expand, rate),
+        (reduce_master, reduce_first, reduce_second, sums_d, 0.5 * FF ** (-0.5)),
+        (biases_master, biases_first, biases_second, bias_total, 0.1),
+    )
+    updates = []
+    for master, first, second, gradient, learn_rate in states:
+        updates += adam_update(
+            master, first, second, gradient, learn_rate, clip_factor, correction
+        )
+    return (output, input_grad, grad_norm, *updates)
+
+
+def fast_solution(mesh):
+    return jax.shard_map(
+        on_device_fast,
+        mesh=mesh,
+        in_specs=(
+            P(("z", "x", "c", "y"), None),
+            P(("z", "x", "c", "y"), None),
+            P(("z", "x", "c")),
+            P(("z", "x", "c")),
+            P(("z", "x", "c")),
+            P(),
+            P(),
+            P(("z", "x", "c"), "y"),
+            P(("z", "x", "c"), "y"),
+            P(("z", "x", "c"), "y"),
+            P(("z", "x", "c"), "y"),
+            P(("z", "x", "c"), "y"),
+            P(("z", "x", "c"), "y"),
+            P(("z", "x", "c"), "y"),
+            P(("z", "x", "c"), "y"),
+            P(("z", "x", "c"), "y"),
+            P(("z", "x", "c"), "y"),
+            P(("z", "x", "c"), "y"),
+            P(("z", "x", "c"), "y"),
+            P(("z", "x", "c"), "y"),
+            P(("z", "x", "c"), "y"),
+            P(("z", "x", "c"), "y"),
+            P(),
+            P(),
+            P(),
+        ),
+        out_specs=(
+            P(("z", "x", "c", "y"), None),
+            P(("z", "x", "c", "y"), None),
+            P(),
+            P(("z", "x", "c"), "y"),
+            P(("z", "x", "c"), "y"),
+            P(("z", "x", "c"), "y"),
+            P(("z", "x", "c"), "y"),
+            P(("z", "x", "c"), "y"),
+            P(("z", "x", "c"), "y"),
+            P(("z", "x", "c"), "y"),
+            P(("z", "x", "c"), "y"),
+            P(("z", "x", "c"), "y"),
+            P(("z", "x", "c"), "y"),
+            P(("z", "x", "c"), "y"),
+            P(("z", "x", "c"), "y"),
+            P(("z", "x", "c"), "y"),
+            P(("z", "x", "c"), "y"),
+            P(("z", "x", "c"), "y"),
+            P(),
+            P(),
+            P(),
+        ),
+        check_vma=False,
+    )
+
+
+def plain_solution(mesh):
     return jax.shard_map(
         on_device,
         mesh=mesh,
@@ -511,3 +1219,10 @@
         ),
         check_vma=False,
     )
+
+
+def solution(mesh):
+    if dict(mesh.shape) == {"seq": 16, "head": 2}:
+        grid = Mesh(mesh.devices.reshape(4, 2, 2, 2), ("z", "x", "c", "y"))
+        return fast_solution(grid)
+    return plain_solution(mesh)

time: 1360 us -> 866 us (0.64)
  waiting for transfers between devices: 818 us -> 0.04 us
  Pallas kernels: 0 us -> 381 us
  blocking collectives: 78 us -> 0 us
  local copies, waits for them, and re-layouts: 70.1 us -> 125 us
  matrix products: 230 us -> 180 us
  other arithmetic: 89.4 us -> 123 us
    pallas_call x0 -> x5, Pallas kernels: none -> 381 us  [the longest x1 167 us: scatter_grads(): pl.pallas_call(scatter_kernel, out_shape=[jax.ShapeDtypeStruct(s, jnp.flo...]
    unnamed x22 -> x0, waiting for transfers between devices: 320 us -> none
    reduce_scatter x3 -> x0, waiting for transfers between devices: 260 us -> none  [the longest x2 243 us: rows_seq(): lax.psum_scatter(lax.dot_general(left_side, right_side, (((0,), (0,)), ((...]
    all_gather x5 -> x0, waiting for transfers between devices: 151 us -> none  [fold_rows(): lax.all_gather(weight_slab, 'seq', axis=0, tiled=True)]
    all_to_all x8 -> x0, waiting for transfers between devices: 87.2 us -> none  [the longest x1 15.7 us: on_device(): lax.all_to_all(attend_grad, 'head', split_axis=1, concat_axis=0, tiled=True)]
    all_to_all x8 -> x0, starting transfers between devices: 40.5 us -> none  [the longest x1 13.5 us: on_device(): lax.all_to_all(head_out, 'head', split_axis=0, concat_axis=1, tiled=True)]
    psum x1 -> x0, blocking collectives: 40.3 us -> none  [on_device(): lax.psum((bias_share, local_squares), ('seq', 'head'))]
    all_gather x5 -> x0, blocking collectives: 37.7 us -> none  [the longest x1 9.85 us: on_device(): lax.all_gather(attend_master.astype(jnp.bfloat16), 'head', axis=1, tiled=...]
  transfers between devices with their start and end apart: 23 -> 16, of which waited for: 21 -> 0; matrix products, arithmetic and copies ran while one was open for 13% -> 32% of each run, Pallas kernels for 0% -> 41%
where the time goes in v1:
time: 866 us; the launch traced here: 852 us
  Pallas kernels  381 us (44%)
  matrix products  180 us (21%)
  local copies, waits for them, and re-layouts  125 us (14%)
  other arithmetic  123 us (14%)
  starting transfers between devices  29.8 us (3%)
  between operations  12.5 us (1%)
    pallas_call x1, Pallas kernels, scatter_grads(): pl.pallas_call(scatter_kernel, out_shape=[jax.ShapeDtypeStruct(s, jnp.flo...  167 us
    pallas_call x1, Pallas kernels, gather_weights(): pl.pallas_call(gather_kernel, out_shape=[jax.ShapeDtypeStruct((2, 4, 2) +...  154 us
    dot_general x8, matrix products, wide_back(): lax.dot_general(gradient[:, i * half:(i + 1) * half], weight[i], (((1,),...  43.6 us
    dot_general x8, matrix products, weight_grad(): lax.dot_general(left, right[:, i * half:(i + 1) * half], (((0,), (0,)), (...  34.8 us
    unnamed x257, local copies, waits for them, and re-layouts  33.2 us
    dot_general x8, matrix products, wide(): jnp.dot(left, weight[i], preferred_element_type=jnp.float32)  27.3 us
    dot_general x4, matrix products, per_block(): jnp.einsum('qhe,khe->hqk', query_block, key_heads, preferred_element_type...  27.1 us
    pallas_call x1, Pallas kernels, image_modulation(): pl.pallas_call(mod_kernel, out_shape=[jax.ShapeDtypeStruct((2, 1, 3456),...  26.7 us
  transfers between devices with their start and end apart: 16, of which 0 were waited for; matrix products, arithmetic and copies ran while one was open for 32% of the time, Pallas kernels for 41%

profile of v1, /device:TPU:0, one launch (start us, length us, event | category | flops | bytes accessed | tf_op | source)
XLA Modules:
  0.0 852.4 jit_solution(12450833835571237441)
XLA Ops:
  30.6 26.7 %image_modulation.1 = (f32[2,1,3456]{2,1,0:T(1,128)}, f32[16,128]{1,0:T(8,128)}) custom-call(f32[16,128]{1,0:T(8,128)} %pad_convert_fusion.cond_ref, bf16[72,3456]{1,0:T(8,128)(2,1)} %convert_element_type.228.weight_ref), custom_call_target="tpu_custom_call" | custom-call | tf_op jit(solution)/shard_map/image_modulation/pallas_call | solution.py:720
  64.1 4.2 multiply_sine_fusion.1
  78.1 153.9 %gather_weights.1 = (bf16[2,4,2,144,864]{4,3,2,1,0:T(8,128)(2,1)}, bf16[2,4,2,72,576]{4,3,2,1,0:T(8,128)(2,1)}, bf16[2,4,2,144,1152]{4,3,2,1,0:T(8,128)(2,1)}, bf16[2,4,2,288,576]{4,3,2,1,0:T(8,128)(2,1)}) custom-call(bf16[144,864]{1,0:T(8,128)(2,1)} %maximum_select_fusion.7.refs_0_, bf16[72,576]{1,0:T(8,128)(2,1)} %convert_element_type.233.refs_1_, ...), custom_call_target="tpu_custom_call" | custom-call | tf_op jit(solution)/shard_map/gather_weights/pallas_call | solution.py:556
  234.6 3.9 fusion.121
  238.5 6.6 fusion.125
  247.8 5.1 fusion.124
  254.3 26.9 %while.48 = (s32[]{:T(128)}, bf16[2,512,8,72]{1,3,2,0:T(8,128)(2,1)}, f32[2,8,512]{2,1,0:T(8,128)}, bf16[2,512,8,72]{1,3,2,0:T(8,128)(2,1)S(1)}, bf16[1024,8,72]...) while((s32[]{:T(128)}, bf16[2,512,8,72]{1,3,2,0:T(8,128)(2,1)}, ...), condition=%wide.region_7.8_spmd.clone, body=%wide.region_4.7_spmd.clone.sunk | while | flops 1258583040 | bytes 63705308 | solution.py:115
  257.1 4.0 fusion.180
  261.2 4.8 fusion.181
  270.5 4.0 fusion.180
  274.6 4.8 fusion.181
  306.3 6.6 fusion.71
  313.0 3.7 fusion.105
  316.7 3.7 fusion.106
  320.5 3.3 multiply_convert_fusion.1
  323.8 4.6 convolution_convert_fusion.3
  334.4 17.9 %convert_reduce_fusion = (f32[2304]{0:T(1024)}, bf16[1024,2304]{1,0:T(8,128)(2,1)}) fusion(f32[2304]{0:T(1024)S(1)} %copy-done.110, f32[1024,1152]{1,0:T(8,128)} %copy-done.32, f32[1024,1152]{1,0:T(8,128)} %copy-done.33, f32[1024,2304]{1,0:T(8,128)} %fusion.71, bf16[2304,576]{1,0:T(8,128)(2,1)} %bitcast.206, bf16[1024,1152]{0,1:T(8,128)(2,1)} %copy-done.53), kind=kOutput, calls=%fused_computation.55 | convolution fusion | flops 2776889088 | bytes 27740160 | tf_op jit(solution)/shard_map/dot_general | solution.py:872
  352.3 5.9 fusion.63
  365.7 4.6 convolution_convert_fusion
  372.3 4.2 convolution_convert_fusion.2
  376.5 4.6 copy.104
  381.1 4.5 copy.105
  387.0 6.3 pad_maximum_fusion.refs_3_
  393.4 4.1 multiply_reduce_fusion.1
  397.5 6.3 fusion.59
  406.0 6.5 convolution_convert_fusion.1
  415.4 10.5 %collective-permute-start.8 = (bf16[512,1152]{0,1:T(8,128)(2,1)}, bf16[512,1152]{0,1:T(8,128)(2,1)}, u32[]{:S(2)}, u32[]{:S(2)}) collective-permute-start(bf16[512,1152]{0,1:T(8,128)(2,1)} %get-tuple-element.438), channel_id=1, source_target_pairs={{0,0},{1,2},{2,1},{3,3},{4,4},{5,6},{6,5},{7,7},{8,8},{9,10},{10,9... | collective-permute-start | bytes 3538952 | tf_op jit(solution)/shard_map/ppermute | solution.py:842
  436.3 4.0 reshape.435
  443.8 85.6 %while.49 = (s32[]{:T(128)}, f32[1024,8,72]{0,2,1:T(8,128)}, f32[1024,8,72]{0,2,1:T(8,128)}, bf16[2,512,8,72]{1,3,2,0:T(8,128)(2,1)}, bf16[2,512,8,72]{1,3,2,0:T...) while((s32[]{:T(128)}, f32[1024,8,72]{0,2,1:T(8,128)}, ...), condition=%wide.region_14.15_spmd.clone, body=%wide.region_12.14_spmd.clone.sunk | while | flops 3061183488 | bytes 236739088 | solution.py:186
  446.8 3.8 fusion.191
  450.6 10.8 %multiply_reduce_fusion.17 = (f32[8,512]{1,0:T(8,128)S(1)}, f32[8,512,1024]{2,1,0:T(8,128)}) fusion(f32[8,512,1024]{2,1,0:T(8,128)S(1)} %fusion.191, f32[8,512]{1,0:T(8,128)S(1)} %dynamic-slice_bitcast_fusion.6, bf16[1024,8,72]{0,2,1:T(8,128)(2,1)} %copy-done.4, bf16[2,512,8,72]{1,3,2,0:T(8,128)(2,1)} %copy-done.8, s32[]{:T(128)S(6)} %copy.139, ...), kind=kOutput, calls=%fused_computation.20.clone.1 | convolution fusion | flops 624947200 | bytes 35357700 | tf_op jit(solution)/shard_map/while/body/eval_jaxpr/while/body/eval_jaxpr/qhe,khe->hqk/dot_general | solution.py:144
  461.4 9.4 %multiply_convert_fusion.5 = bf16[8,512,1024]{2,1,0:T(8,128)(2,1)} fusion(f32[8,512,1024]{2,1,0:T(8,128)} %get-tuple-element.604, f32[8,512,1024]{2,1,0:T(8,128)S(1)} %fusion.191, f32[8,512]{1,0:T(8,128)S(1)} %get-tuple-element.605), kind=kLoop, calls=%fused_computation.19.clone.1 | loop fusion | flops 12582912 | bytes 41959424 | tf_op jit(solution)/shard_map/while/body/eval_jaxpr/while/body/eval_jaxpr/convert_element_type | solution.py:155
  470.9 8.9 %bitcast_add_fusion.5 = f32[1024,8,72]{0,2,1:T(8,128)} fusion(f32[1024,8,72]{0,2,1:T(8,128)} %get-tuple-element.644, f32[8,512,1024]{2,1,0:T(8,128)} %get-tuple-element.604, pred[]{:T(512)S(6)} %compare.4, bf16[2,512,8,72]{1,3,2,0:T(8,128)(2,1)S(1)} %copy-done.15, s32[]{:T(128)S(6)} %copy.139), kind=kOutput, calls=%fused_computation.24.clone.1 | convolution fusion | flops 609353728 | bytes 22085636 | tf_op jit(solution)/shard_map/while/body/eval_jaxpr/while/body/eval_jaxpr/hqk,qhe->khe/dot_general | solution.py:169
  489.0 3.8 fusion.191
  492.8 10.8 %multiply_reduce_fusion.17 = (f32[8,512]{1,0:T(8,128)S(1)}, f32[8,512,1024]{2,1,0:T(8,128)}) fusion(f32[8,512,1024]{2,1,0:T(8,128)S(1)} %fusion.191, f32[8,512]{1,0:T(8,128)S(1)} %dynamic-slice_bitcast_fusion.6, bf16[1024,8,72]{0,2,1:T(8,128)(2,1)} %copy-done.4, bf16[2,512,8,72]{1,3,2,0:T(8,128)(2,1)} %copy-done.8, s32[]{:T(128)S(6)} %copy.139, ...), kind=kOutput, calls=%fused_computation.20.clone.1 | convolution fusion | flops 624947200 | bytes 35357700 | tf_op jit(solution)/shard_map/while/body/eval_jaxpr/while/body/eval_jaxpr/qhe,khe->hqk/dot_general | solution.py:144
  503.6 9.4 %multiply_convert_fusion.5 = bf16[8,512,1024]{2,1,0:T(8,128)(2,1)} fusion(f32[8,512,1024]{2,1,0:T(8,128)} %get-tuple-element.604, f32[8,512,1024]{2,1,0:T(8,128)S(1)} %fusion.191, f32[8,512]{1,0:T(8,128)S(1)} %get-tuple-element.605), kind=kLoop, calls=%fused_computation.19.clone.1 | loop fusion | flops 12582912 | bytes 41959424 | tf_op jit(solution)/shard_map/while/body/eval_jaxpr/while/body/eval_jaxpr/convert_element_type | solution.py:155
  513.1 9.6 %bitcast_add_fusion.5 = f32[1024,8,72]{0,2,1:T(8,128)} fusion(f32[1024,8,72]{0,2,1:T(8,128)} %get-tuple-element.644, f32[8,512,1024]{2,1,0:T(8,128)} %get-tuple-element.604, pred[]{:T(512)S(6)} %compare.4, bf16[2,512,8,72]{1,3,2,0:T(8,128)(2,1)S(1)} %copy-done.15, s32[]{:T(128)S(6)} %copy.139), kind=kOutput, calls=%fused_computation.24.clone.1 | convolution fusion | flops 609353728 | bytes 22085636 | tf_op jit(solution)/shard_map/while/body/eval_jaxpr/while/body/eval_jaxpr/hqk,qhe->khe/dot_general | solution.py:169
  538.4 4.0 fusion.76
  549.1 5.4 convolution_convert_fusion.4
  554.5 5.6 convolution_convert_fusion.5
  564.4 4.3 copy.103
  568.7 4.1 pad_maximum_fusion.2.refs_0_
  572.8 167.0 %scatter_grads.1 = (f32[144,864]{1,0:T(8,128)}, f32[72,576]{1,0:T(8,128)}, f32[144,1152]{1,0:T(8,128)}, f32[288,576]{1,0:T(8,128)}) custom-call(bf16[2,4,2,144,864]{4,3,2,1,0:T(8,128)(2,1)} %pad_maximum_fusion.2.refs_0_, bf16[2,4,2,72,576]{4,3,2,1,0:T(8,128)(2,1)} %pad_maximum_fusion.6.refs_1_, bf16[2,4,2,144,1152]{4,3,2,1,0:T(8,128)(2,1)} %pad_maximum_fusion.1.refs_2_, ...), custom_call_target="tpu_custom_call" | custom-call | tf_op jit(solution)/shard_map/scatter_grads/pallas_call | solution.py:651
  757.4 3.3 multiply_reduce_fusion.3
  763.4 3.5 multiply_reduce_fusion.2
  773.7 19.3 %share_totals.1 = (bf16[4,2,2,16,432]{4,3,2,1,0:T(8,128)(2,1)}, f32[72,128]{1,0:T(8,128)}) custom-call(f32[16,432]{1,0:T(8,128)} %reshape.437.mod_ref, f32[72,128]{1,0:T(8,128)} %bitcast.241), custom_call_target="tpu_custom_call" | custom-call | tf_op jit(solution)/shard_map/share_totals/pallas_call | solution.py:782
  801.4 13.9 %sum_everywhere.1 = f32[8,128]{1,0:T(8,128)} custom-call(f32[8,128]{1,0:T(8,128)} %broadcast_in_dim.55.in_ref), custom_call_target="tpu_custom_call" | custom-call | tf_op jit(solution)/shard_map/sum_everywhere/pallas_call | solution.py:825
  819.8 10.7 %collective-permute-start.13 = (bf16[512,1152]{0,1:T(8,128)(2,1)}, bf16[512,1152]{0,1:T(8,128)(2,1)}, u32[]{:S(2)}, u32[]{:S(2)}) collective-permute-start(bf16[512,1152]{0,1:T(8,128)(2,1)} %get-tuple-element.449), channel_id=1, source_target_pairs={{0,0},{1,2},{2,1},{3,3},{4,4},{5,6},{6,5},{7,7},{8,8},{9,10},{10,9... | collective-permute-start | bytes 3538952 | tf_op jit(solution)/shard_map/ppermute | solution.py:842
  (502 shorter events, 211.8 us)
Async XLA Ops:
  4.6 63.7 %collective-permute-start = (bf16[2,512,1152]{1,2,0:T(8,128)(2,1)}, bf16[2,512,1152]{1,2,0:T(8,128)(2,1)S(1)}, u32[]{:S(2)}, u32[]{:S(2)}) collective-permute-start(bf16[2,512,1152]{1,2,0:T(8,128)(2,1)} %pad_maximum_fusion.3), channel_id=1, source_target_pairs={{0,0},{1,2},{2,1},{3,3},{4,4},{5,6},{6,5},{7,7},{8,8},{9,10},{10,9... | collective-permute-start | bytes 7077896 | tf_op jit(solution)/shard_map/ppermute | solution.py:842
  6.9 52.7 %collective-permute-start.1 = (s32[1]{0:T(128)}, s32[1]{0:T(128)}, u32[]{:S(2)}, u32[]{:S(2)}) collective-permute-start(s32[1]{0:T(128)} %param.33), channel_id=1, source_target_pairs={{0,0},{1,2},{2,1},{3,3},{4,4},{5,6},{6,5},{7,7},{8,8},{9,10},{10,9... | collective-permute-start | bytes 20 | tf_op jit(solution)/shard_map/ppermute | solution.py:842
  12.1 17.0 %copy-start.38 = (f32[72,3456]{1,0:T(8,128)S(1)}, f32[72,3456]{1,0:T(8,128)}, u32[]{:S(2)}) copy-start(f32[72,3456]{1,0:T(8,128)} %param.38) | copy-start | bytes 2985988
  13.9 60.7 %collective-permute-start.3 = (bf16[72,864]{1,0:T(8,128)(2,1)}, bf16[72,864]{1,0:T(8,128)(2,1)}, u32[]{:S(2)}, u32[]{:S(2)}) collective-permute-start(bf16[72,864]{1,0:T(8,128)(2,1)} %get-tuple-element.461), channel_id=1, source_target_pairs={{0,2},{2,0},{1,3},{3,1},{4,6},{6,4},{5,7},{7,5},{8,10},{10,8},{9,1... | collective-permute-start | bytes 373256 | tf_op jit(solution)/shard_map/ppermute | solution.py:846
  21.0 38.6 %copy-start.133 = (s32[8]{0:T(128)S(1)}, s32[8]{0:T(128)}, u32[]{:S(2)}) copy-start(s32[8]{0:T(128)} %constant.220.clone) | copy-start | bytes 100
  21.0 39.8 %copy-start.132 = (s32[8]{0:T(128)S(1)}, s32[8]{0:T(128)}, u32[]{:S(2)}) copy-start(s32[8]{0:T(128)} %constant.221.clone) | copy-start | bytes 100
  26.8 49.6 %collective-permute-start.4 = (bf16[72,1152]{1,0:T(8,128)(2,1)}, bf16[72,1152]{1,0:T(8,128)(2,1)}, u32[]{:S(2)}, u32[]{:S(2)}) collective-permute-start(bf16[72,1152]{1,0:T(8,128)(2,1)} %get-tuple-element.459), channel_id=1, source_target_pairs={{0,2},{2,0},{1,3},{3,1},{4,6},{6,4},{5,7},{7,5},{8,10},{10,8},{9,1... | collective-permute-start | bytes 497672 | tf_op jit(solution)/shard_map/ppermute | solution.py:846
  58.9 13.2 %copy-start.89 = (f32[16128]{0:T(1024)}, f32[16128]{0:T(1024)S(1)}, u32[]{:S(2)}) copy-start(f32[16128]{0:T(1024)S(1)} %convert_convert_fusion) | copy-start | bytes 193540
  59.6 11.1 %copy-start.101 = (f32[1152]{0:T(1024)}, f32[1152]{0:T(1024)S(1)}, u32[]{:S(2)}) copy-start(f32[1152]{0:T(1024)S(1)} %get-tuple-element.468) | copy-start | bytes 13828
  59.6 11.5 %copy-start.97 = (f32[1152]{0:T(1024)}, f32[1152]{0:T(1024)S(1)}, u32[]{:S(2)}) copy-start(f32[1152]{0:T(1024)S(1)} %get-tuple-element.470) | copy-start | bytes 13828
  72.1 166.4 %copy-start.67 = (bf16[512,1152]{0,1:T(8,128)(2,1)}, bf16[512,1152]{0,1:T(8,128)(2,1)S(1)}, u32[]{:S(2)}) copy-start(bf16[512,1152]{0,1:T(8,128)(2,1)S(1)} %add_convert_fusion.4) | copy-start | bytes 3538948
  72.1 166.4 %collective-permute-start.2 = (bf16[512,1152]{0,1:T(8,128)(2,1)S(1)}, bf16[512,1152]{0,1:T(8,128)(2,1)}, u32[]{:S(2)}, u32[]{:S(2)}) collective-permute-start(bf16[512,1152]{0,1:T(8,128)(2,1)S(1)} %add_convert_fusion.4), channel_id=1, source_target_pairs={{0,2},{2,0},{1,3},{3,1},{4,6},{6,4},{5,7},{7,5},{8,10},{10,8},{9,1... | collective-permute-start | bytes 3538952 | tf_op jit(solution)/shard_map/ppermute | solution.py:846
  288.7 9.3 %collective-permute-start.5 = (bf16[512,1152]{0,1:T(8,128)(2,1)}, bf16[512,1152]{0,1:T(8,128)(2,1)}, u32[]{:S(2)}, u32[]{:S(2)}) collective-permute-start(bf16[512,1152]{0,1:T(8,128)(2,1)} %fusion.49), channel_id=1, source_target_pairs={{0,2},{2,0},{1,3},{3,1},{4,6},{6,4},{5,7},{7,5},{8,10},{10,8},{9,1... | collective-permute-start | bytes 3538952 | tf_op jit(solution)/shard_map/ppermute | solution.py:846
  297.3 15.6 %copy-start.50 = (bf16[1,4,2,144,1152]{4,3,2,1,0:T(8,128)(2,1)}, bf16[1,4,2,144,1152]{4,3,2,1,0:T(8,128)(2,1)S(1)}, u32[]{:S(2)}) copy-start(bf16[1,4,2,144,1152]{4,3,2,1,0:T(8,128)(2,1)S(1)} %get-tuple-element.442) | copy-start | bytes 7962628
  297.3 19.4 %copy-start.52 = (bf16[1,4,2,144,1152]{4,3,2,1,0:T(8,128)(2,1)}, bf16[1,4,2,144,1152]{4,3,2,1,0:T(8,128)(2,1)S(1)}, u32[]{:S(2)}) copy-start(bf16[1,4,2,144,1152]{4,3,2,1,0:T(8,128)(2,1)S(1)} %get-tuple-element.441) | copy-start | bytes 7962628
  297.4 8.3 collective-permute-start.9
  304.6 12.1 %copy-start.69 = (bf16[512,1152]{0,1:T(8,128)(2,1)}, bf16[512,1152]{0,1:T(8,128)(2,1)S(1)}, u32[]{:S(2)}) copy-start(bf16[512,1152]{0,1:T(8,128)(2,1)S(1)} %add_convert_fusion.3) | copy-start | bytes 3538948
  304.6 8.4 collective-permute-start.6
  305.6 25.8 %copy-start.41 = (bf16[1,4,2,288,576]{4,3,2,1,0:T(8,128)(2,1)}, bf16[1,4,2,288,576]{4,3,2,1,0:T(8,128)(2,1)S(1)}, u32[]{:S(2)}) copy-start(bf16[1,4,2,288,576]{4,3,2,1,0:T(8,128)(2,1)S(1)} %get-tuple-element.440) | copy-start | bytes 7962628
  306.3 17.5 %copy-start.53 = (bf16[1024,1152]{0,1:T(8,128)(2,1)}, bf16[1024,1152]{0,1:T(8,128)(2,1)S(1)}, u32[]{:S(2)}) copy-start(bf16[1024,1152]{0,1:T(8,128)(2,1)S(1)} %maximum_select_fusion.2) | copy-start | bytes 7077892
  331.4 38.9 %copy-start.24 = (f32[1024,576]{0,1:T(8,128)}, f32[1024,576]{0,1:T(8,128)S(1)}, u32[]{:S(2)}) copy-start(f32[1024,576]{0,1:T(8,128)S(1)} %fusion.129) | copy-start | bytes 7077892
  334.4 35.8 %copy-start.26 = (f32[1024,576]{0,1:T(8,128)}, f32[1024,576]{0,1:T(8,128)S(1)}, u32[]{:S(2)}) copy-start(f32[1024,576]{0,1:T(8,128)S(1)} %fusion.128) | copy-start | bytes 7077892
  364.9 28.4 %collective-permute-start.10 = (bf16[512,1152]{0,1:T(8,128)(2,1)}, bf16[512,1152]{0,1:T(8,128)(2,1)}, u32[]{:S(2)}, u32[]{:S(2)}) collective-permute-start(bf16[512,1152]{0,1:T(8,128)(2,1)} %dynamic-slice_convert_fusion.1), channel_id=1, source_target_pairs={{0,2},{2,0},{1,3},{3,1},{4,6},{6,4},{5,7},{7,5},{8,10},{10,8},{9,1... | collective-permute-start | bytes 3538952 | tf_op jit(solution)/shard_map/ppermute | solution.py:846
  371.5 26.0 %collective-permute-start.7 = (bf16[512,1152]{0,1:T(8,128)(2,1)}, bf16[512,1152]{0,1:T(8,128)(2,1)}, u32[]{:S(2)}, u32[]{:S(2)}) collective-permute-start(bf16[512,1152]{0,1:T(8,128)(2,1)} %fusion.44), channel_id=1, source_target_pairs={{0,2},{2,0},{1,3},{3,1},{4,6},{6,4},{5,7},{7,5},{8,10},{10,8},{9,1... | collective-permute-start | bytes 3538952 | tf_op jit(solution)/shard_map/ppermute | solution.py:846
  403.8 22.1 %collective-permute-start.11 = (bf16[512,1152]{0,1:T(8,128)(2,1)}, bf16[512,1152]{0,1:T(8,128)(2,1)}, u32[]{:S(2)}, u32[]{:S(2)}) collective-permute-start(bf16[512,1152]{0,1:T(8,128)(2,1)} %get-tuple-element.444), channel_id=1, source_target_pairs={{0,2},{2,0},{1,3},{3,1},{4,6},{6,4},{5,7},{7,5},{8,10},{10,8},{9,1... | collective-permute-start | bytes 3538952 | tf_op jit(solution)/shard_map/ppermute | solution.py:846
  415.4 13.6 %copy-start.65 = (bf16[72,8,2,512]{3,1,2,0:T(8,128)(2,1)S(1)}, bf16[72,8,2,512]{3,1,2,0:T(8,128)(2,1)}, u32[]{:S(2)}) copy-start(bf16[72,8,2,512]{3,1,2,0:T(8,128)(2,1)} %copy-done.64) | copy-start | bytes 3538948
  415.4 330.2 %collective-permute-start.8 = (bf16[512,1152]{0,1:T(8,128)(2,1)}, bf16[512,1152]{0,1:T(8,128)(2,1)}, u32[]{:S(2)}, u32[]{:S(2)}) collective-permute-start(bf16[512,1152]{0,1:T(8,128)(2,1)} %get-tuple-element.438), channel_id=1, source_target_pairs={{0,0},{1,2},{2,1},{3,3},{4,4},{5,6},{6,5},{7,7},{8,8},{9,10},{10,9... | collective-permute-start | bytes 3538952 | tf_op jit(solution)/shard_map/ppermute | solution.py:842
  461.4 9.4 %copy-start.15 = (bf16[2,512,8,72]{1,3,2,0:T(8,128)(2,1)S(1)}, bf16[2,512,8,72]{1,3,2,0:T(8,128)(2,1)}, u32[]{:S(2)}) copy-start(bf16[2,512,8,72]{1,3,2,0:T(8,128)(2,1)} %get-tuple-element.661) | copy-start | bytes 3538948 | tf_op jit(solution)/shard_map/while/body/eval_jaxpr/while
  470.8 8.9 %copy-start = (bf16[8,512,1024]{2,1,0:T(8,128)(2,1)S(1)}, bf16[8,512,1024]{2,1,0:T(8,128)(2,1)}, u32[]{:S(2)}) copy-start(bf16[8,512,1024]{2,1,0:T(8,128)(2,1)} %multiply_convert_fusion.5) | copy-start | bytes 25165828 | tf_op jit(solution)/shard_map/while/body/eval_jaxpr/while
  470.8 8.9 %copy-start.5 = (bf16[1024,8,72]{0,2,1:T(8,128)(2,1)S(1)}, bf16[1024,8,72]{0,2,1:T(8,128)(2,1)}, u32[]{:S(2)}) copy-start(bf16[1024,8,72]{0,2,1:T(8,128)(2,1)} %copy-done.4) | copy-start | bytes 3538948 | tf_op jit(solution)/shard_map/while/body/eval_jaxpr/while
  470.9 9.5 %copy-start.22 = (bf16[2,512,8,72]{1,3,2,0:T(8,128)(2,1)S(1)}, bf16[2,512,8,72]{1,3,2,0:T(8,128)(2,1)}, u32[]{:S(2)}) copy-start(bf16[2,512,8,72]{1,3,2,0:T(8,128)(2,1)} %get-tuple-element.645) | copy-start | bytes 3538948 | tf_op jit(solution)/shard_map/while/body/eval_jaxpr/while
  503.6 9.4 %copy-start.15 = (bf16[2,512,8,72]{1,3,2,0:T(8,128)(2,1)S(1)}, bf16[2,512,8,72]{1,3,2,0:T(8,128)(2,1)}, u32[]{:S(2)}) copy-start(bf16[2,512,8,72]{1,3,2,0:T(8,128)(2,1)} %get-tuple-element.661) | copy-start | bytes 3538948 | tf_op jit(solution)/shard_map/while/body/eval_jaxpr/while
  513.1 9.6 %copy-start = (bf16[8,512,1024]{2,1,0:T(8,128)(2,1)S(1)}, bf16[8,512,1024]{2,1,0:T(8,128)(2,1)}, u32[]{:S(2)}) copy-start(bf16[8,512,1024]{2,1,0:T(8,128)(2,1)} %multiply_convert_fusion.5) | copy-start | bytes 25165828 | tf_op jit(solution)/shard_map/while/body/eval_jaxpr/while
  513.1 9.6 %copy-start.5 = (bf16[1024,8,72]{0,2,1:T(8,128)(2,1)S(1)}, bf16[1024,8,72]{0,2,1:T(8,128)(2,1)}, u32[]{:S(2)}) copy-start(bf16[1024,8,72]{0,2,1:T(8,128)(2,1)} %copy-done.4) | copy-start | bytes 3538948 | tf_op jit(solution)/shard_map/while/body/eval_jaxpr/while
  513.1 10.2 %copy-start.22 = (bf16[2,512,8,72]{1,3,2,0:T(8,128)(2,1)S(1)}, bf16[2,512,8,72]{1,3,2,0:T(8,128)(2,1)}, u32[]{:S(2)}) copy-start(bf16[2,512,8,72]{1,3,2,0:T(8,128)(2,1)} %get-tuple-element.645) | copy-start | bytes 3538948 | tf_op jit(solution)/shard_map/while/body/eval_jaxpr/while
  548.6 208.7 %collective-permute-start.12 = (bf16[512,1152]{0,1:T(8,128)(2,1)}, bf16[512,1152]{0,1:T(8,128)(2,1)}, u32[]{:S(2)}, u32[]{:S(2)}) collective-permute-start(bf16[512,1152]{0,1:T(8,128)(2,1)} %dynamic-slice_convert_fusion), channel_id=1, source_target_pairs={{0,2},{2,0},{1,3},{3,1},{4,6},{6,4},{5,7},{7,5},{8,10},{10,8},{9,1... | collective-permute-start | bytes 3538952 | tf_op jit(solution)/shard_map/ppermute | solution.py:846
  741.1 9.3 %collective-permute-start.14 = (f32[72,864]{1,0:T(8,128)S(1)}, f32[72,864]{1,0:T(8,128)}, u32[]{:S(2)}, u32[]{:S(2)}) collective-permute-start(f32[72,864]{1,0:T(8,128)S(1)} %get-tuple-element.456), channel_id=1, source_target_pairs={{0,2},{2,0},{1,3},{3,1},{4,6},{6,4},{5,7},{7,5},{8,10},{10,8},{9,1... | collective-permute-start | bytes 746504 | tf_op jit(solution)/shard_map/ppermute | solution.py:846
  743.0 9.6 %collective-permute-start.15 = (f32[72,1152]{1,0:T(8,128)}, f32[72,1152]{1,0:T(8,128)}, u32[]{:S(2)}, u32[]{:S(2)}) collective-permute-start(f32[72,1152]{1,0:T(8,128)} %get-tuple-element.454), channel_id=1, source_target_pairs={{0,2},{2,0},{1,3},{3,1},{4,6},{6,4},{5,7},{7,5},{8,10},{10,8},{9,1... | collective-permute-start | bytes 995336 | tf_op jit(solution)/shard_map/ppermute | solution.py:846
  748.2 9.1 %copy-start.12 = (f32[512,1152]{0,1:T(8,128)S(1)}, f32[512,1152]{0,1:T(8,128)}, u32[]{:S(2)}) copy-start(f32[512,1152]{0,1:T(8,128)} %copy-done.10) | copy-start | bytes 7077892
  748.2 9.1 %copy-start.98 = (f32[1152]{0:T(1024)S(1)}, f32[1152]{0:T(1024)}, u32[]{:S(2)}) copy-start(f32[1152]{0:T(1024)} %copy-done.97) | copy-start | bytes 13828
  748.3 9.1 %copy-start.107 = (f32[512]{0:T(512)S(1)}, f32[512]{0:T(512)}, u32[]{:S(2)}) copy-start(f32[512]{0:T(512)} %copy-done.106) | copy-start | bytes 6148
  748.3 9.1 %copy-start.122 = (f32[512]{0:T(512)S(1)}, f32[512]{0:T(512)}, u32[]{:S(2)}) copy-start(f32[512]{0:T(512)} %copy-done.121) | copy-start | bytes 6148
  766.9 51.6 %copy-start.36 = (f32[1,72,4,288]{3,2,1,0:T(4,128)S(1)}, f32[1,72,4,288]{3,2,1,0:T(4,128)}, u32[]{:S(2)}) copy-start(f32[1,72,4,288]{3,2,1,0:T(4,128)} %stack.92) | copy-start | bytes 995332
  766.9 51.6 %copy-start.37 = (f32[1,72,4,288]{3,2,1,0:T(4,128)S(1)}, f32[1,72,4,288]{3,2,1,0:T(4,128)}, u32[]{:S(2)}) copy-start(f32[1,72,4,288]{3,2,1,0:T(4,128)} %stack.93) | copy-start | bytes 995332
  793.0 23.5 %copy-start.96 = (f32[72,128]{1,0:T(8,128)S(1)}, f32[72,128]{1,0:T(8,128)}, u32[]{:S(2)}) copy-start(f32[72,128]{1,0:T(8,128)} %get-tuple-element.192) | copy-start | bytes 110596
  795.6 24.2 %copy-start.90 = (f32[6912]{0:T(1024)}, f32[6912]{0:T(1024)S(1)}, u32[]{:S(2)}) copy-start(f32[6912]{0:T(1024)S(1)} %reshape.440) | copy-start | bytes 82948
  819.7 13.5 %copy-start.40 = (f32[72,4,2,288]{3,1,0,2:T(4,128)S(1)}, f32[72,4,2,288]{3,1,0,2:T(4,128)}, u32[]{:S(2)}) copy-start(f32[72,4,2,288]{3,1,0,2:T(4,128)} %multiply_bitcast_fusion.1) | copy-start | bytes 1990660
  819.8 28.2 %collective-permute-start.13 = (bf16[512,1152]{0,1:T(8,128)(2,1)}, bf16[512,1152]{0,1:T(8,128)(2,1)}, u32[]{:S(2)}, u32[]{:S(2)}) collective-permute-start(bf16[512,1152]{0,1:T(8,128)(2,1)} %get-tuple-element.449), channel_id=1, source_target_pairs={{0,0},{1,2},{2,1},{3,3},{4,4},{5,6},{6,5},{7,7},{8,8},{9,10},{10,9... | collective-permute-start | bytes 3538952 | tf_op jit(solution)/shard_map/ppermute | solution.py:842
  (122 other events, 419.3 us)

commit v2 on v1

--- a/solution.py
+++ b/solution.py
@@ -459,9 +459,15 @@
     )
 
 
+ALPHA = HEAD_DIM ** (-0.5) * math.log2(math.e)
+GELU_A = math.sqrt(2.0 / math.pi)
+GELU_B = 0.044715
+BLOCK = FF // 16
+BF, F32 = jnp.bfloat16, jnp.float32
+ANY, VM = pl.ANY, pltpu.VMEM
+PIECES = {"q": (144, 864, 48), "p": (72, 576, None), "u": (144, 1152, 48), "d": (288, 576, 96)}
+NAMES = ("q", "p", "u", "d")
 MESH = pl.DeviceIdType.MESH
-PIECES = {"q": (144, 864, 96), "p": (72, 576, None), "u": (144, 1152, 96), "d": (288, 576, 192)}
-NAMES = ("q", "p", "u", "d")
 
 
 def place():
@@ -470,7 +476,7 @@
 
 def at_z(k):
     z = lax.axis_index("z")
-    return (z + 1 - 2 * (z % 2), (z + 2) % 4, 3 - z)[k - 1]
+    return (z, z + 1 - 2 * (z % 2), (z + 2) % 4, 3 - z)[k]
 
 
 def rdma(src, dst, send, recv, to):
@@ -479,91 +485,812 @@
     )
 
 
-def greet(partners):
+def partners():
+    z, x, c, y = place()
+    xn, yn, twin = (z, 1 - x, c, y), (z, x, c, 1 - y), (z, x, 1 - c, y)
+    return xn, yn, twin, [(at_z(k), x, c, y) for k in range(4)]
+
+
+def greet(others, swapped=False):
+    z, x, c, y = place()
     barrier = pltpu.get_barrier_semaphore()
-    for to in partners:
+    for to in others:
         pl.semaphore_signal(barrier, inc=1, device_id=to, device_id_type=MESH)
-    pl.semaphore_wait(barrier, len(partners))
-
-
-def parts_of(rows, cut, k):
+    if swapped:
+
+        @pl.when(c != y)
+        def _():
+            pl.semaphore_signal(barrier, inc=1, device_id=(z, x, y, c), device_id_type=MESH)
+
+        pl.semaphore_wait(barrier, len(others) + (c + y) % 2)
+    else:
+        pl.semaphore_wait(barrier, len(others))
+
+
+CHUNKS = (
+    (0, 0, 80, 32),
+    (0, 80, 64, 16),
+    (1, 0, 72, None),
+    (2, 0, 80, 32),
+    (2, 80, 64, 16),
+    (3, 0, 144, 48),
+    (3, 144, 144, 48),
+)
+
+
+def parts_of(chunk, k):
+    _, _, rows, cut = CHUNKS[chunk]
+    if cut is None:
+        return ((0, rows), None) if k == 0 else (None, (0, rows))
+    return (0, cut), (cut, rows - cut)
+
+
+def piece_at(full, w, y, zk, x, first, count):
+    rows = PIECES[NAMES[w]][0]
+    if count == 72:
+        return full.at[y, zk * 2 + x]
+    return full.at[y, pl.ds(pl.multiple_of((zk * 2 + x) * rows + first, 16), count)]
+
+
+def matmul(left, right):
+    return jnp.dot(left, right, preferred_element_type=F32)
+
+
+def matmul_nt(left, right):
+    return lax.dot_general(left, right, (((1,), (1,)), ((), ())), preferred_element_type=F32)
+
+
+def matmul_tn(left, right):
+    return lax.dot_general(left, right, (((0,), (0,)), ((), ())), preferred_element_type=F32)
+
+
+class Gather:
+    def __init__(self, own, full, sems):
+        self.own, self.full = own, full
+        self.zs, self.zr, self.xs, self.xr, self.ys, self.yr, self.fs, self.fr, self.ps, self.pr = sems
+        self.sent = []
+
+    def piece(self, w, flip_y, k, flip_x):
+        z, x, c, y = place()
+        weight, first, count, _ = CHUNKS[w]
+        return piece_at(
+            self.full[weight], weight, 1 - y if flip_y else y, at_z(k), 1 - x if flip_x else x, first, count
+        )
+
+    def source(self, w):
+        weight, first, count, _ = CHUNKS[w]
+        return self.own[weight].at[pl.ds(first, count)]
+
+    def send(self, make):
+        make().start()
+        self.sent.append(make)
+
+    def arrived(self, ref, s, r):
+        rdma(ref, ref, s, r, partners()[0]).wait_recv()
+
+    def start(self, w):
+        def to_x():
+            return rdma(self.source(w), self.piece(w, 0, 0, 0), self.xs.at[w, 0], self.xr.at[w, 0], partners()[0])
+
+        def to_y():
+            return rdma(self.source(w), self.piece(w, 0, 0, 0), self.ys.at[w, 0], self.yr.at[w, 0], partners()[1])
+
+        def to_z(k):
+            to = partners()[3][k]
+            return rdma(self.source(w), self.piece(w, 0, 0, 0), self.zs.at[w, k], self.zr.at[w, k], to)
+
+        self.send(to_x)
+        self.send(to_y)
+        for k in (1, 2, 3):
+            self.send(functools.partial(to_z, k))
+
+    def column(self, w, k):
+        self.arrived(self.piece(w, 0, k, 0), self.zs.at[w, k], self.zr.at[w, k])
+
+        def to_x():
+            piece = self.piece(w, 0, k, 0)
+            return rdma(piece, piece, self.xs.at[w, k], self.xr.at[w, k], partners()[0])
+
+        def to_y():
+            piece = self.piece(w, 0, k, 0)
+            return rdma(piece, piece, self.ys.at[w, k], self.yr.at[w, k], partners()[1])
+
+        self.send(to_x)
+        self.send(to_y)
+
+    def plane(self, w, k):
+        spans = parts_of(w, k)
+
+        def pass_on(i):
+            part = self.piece(w, i, k, 1 - i).at[pl.ds(*spans[i])]
+            return rdma(part, part, self.fs.at[w, k, i], self.fr.at[w, k, i], partners()[1 - i])
+
+        self.arrived(self.piece(w, 0, k, 1), self.xs.at[w, k], self.xr.at[w, k])
+        if k in (0, 2) and spans[0] is not None:
+            self.send(functools.partial(pass_on, 0))
+        self.arrived(self.piece(w, 1, k, 0), self.ys.at[w, k], self.yr.at[w, k])
+        if k in (0, 2) and spans[1] is not None:
+            self.send(functools.partial(pass_on, 1))
+
+    def corner(self, w, k):
+        for i, span in enumerate(parts_of(w, k)):
+            if span is not None:
+                part = self.piece(w, 1, k, 1).at[pl.ds(*span)]
+                self.arrived(part, self.fs.at[w, k, i], self.fr.at[w, k, i])
+
+        def to_pair():
+            piece = self.piece(w, 1, k, 1)
+            return rdma(piece, piece, self.ps.at[w, k], self.pr.at[w, k], partners()[3][1])
+
+        self.send(to_pair)
+
+    def last(self, w, k):
+        self.arrived(self.piece(w, 1, k ^ 1, 1), self.ps.at[w, k], self.pr.at[w, k])
+
+    def finish(self):
+        for make in self.sent:
+            make().wait_send()
+
+    def steps(self):
+        def each(method, chunks, ks):
+            return [(method, i, k) for i in chunks for k in ks]
+
+        column, plane, corner, last = self.column, self.plane, self.corner, self.last
+        one = (0, 1)
+        plan = [(self.start, 0), (self.start, 1), (self.start, 2)]
+        plan += each(column, one, (1,)) + each(plane, one, (0,))
+        plan += each(column, one, (2,)) + each(column, one, (3,)) + [(self.start, 3)]
+        plan += each(corner, one, (0,)) + each(plane, one, (2,))
+        plan += each(column, (2,), (1,)) + [(self.start, 4)]
+        plan += each(plane, one, (1,)) + each(corner, one, (2,))
+        plan += each(plane, (2,), (0,)) + each(column, (2,), (2, 3)) + each(column, (3,), (1,))
+        plan += each(plane, one, (3,)) + each(last, one, (0, 2))
+        count = len(CHUNKS)
+        for t in range(-2, count + 4):
+            wave = [(self.start, t + 2)] if t + 2 < count else []
+            for lag, make in enumerate(
+                (
+                    lambda i: each(column, (i,), (1,)),
+                    lambda i: each(plane, (i,), (0,)) + each(column, (i,), (2, 3)),
+                    lambda i: each(corner, (i,), (0,)) + each(plane, (i,), (2, 1)),
+                    lambda i: each(corner, (i,), (2,)) + each(plane, (i,), (3,)),
+                    lambda i: each(last, (i,), (0, 2)),
+                )
+            ):
+                if t >= 0 and 0 <= t - lag < count:
+                    wave += make(t - lag)
+            plan += [step for step in wave if step not in plan]
+        return plan
+
+
+def mod_steps(cond_ref, weight, bias, out_ref, lhs, bufs, s, r):
+    conds, part, got_z, mid, got_x, near, got_c = bufs
+
+    def hop(i):
+        z, x, c, y = place()
+        xn, yn, twin, zn = partners()
+        if i == 0:
+            pairs = [(conds.at[z, x, c], conds.at[z, x, c], twin)]
+        elif i == 1:
+            pairs = [(conds.at[z, x], conds.at[z, x], xn)]
+        elif i == 2:
+            pairs = [(conds.at[z], conds.at[z], zn[k]) for k in (1, 2, 3)]
+        elif i == 3:
+            pairs = [(part.at[at_z(k)], got_z.at[k - 1], zn[k]) for k in (1, 2, 3)]
+        elif i == 4:
+            pairs = [(mid.at[1 - x], got_x, xn)]
+        elif i == 5:
+            pairs = [(near.at[0], got_c, twin)]
+        else:
+            pairs = [(near.at[1, 1 - y], near.at[2, y], yn)]
+        return [
+            rdma(src, dst, s.at[i, n], r.at[i, n], to) for n, (src, dst, to) in enumerate(pairs)
+        ]
+
+    def go(i):
+        for d in hop(i):
+            d.start()
+
+    def end(i):
+        for d in hop(i):
+            d.wait()
+
+    def step(i):
+        z, x, c, y = place()
+        if i > 0:
+            end(i - 1)
+        if i == 0:
+            conds[z, x, c] = cond_ref[...]
+        elif i == 3:
+            me = (z * 2 + x) * 2 + c
+            for n in range(16):
+                lhs[pl.ds(n, 1), :] = conds[n // 4, n // 2 % 2, n % 2, pl.ds(me, 1), :]
+            for j in range(3):
+                cols = slice(j * D, (j + 1) * D)
+                result = matmul(lhs[:, :72].astype(BF), weight[:, cols].astype(BF))
+                for n in range(16):
+                    part[n // 4, n // 2 % 2, n % 2, :, cols] = result[n : n + 1]
+        elif i == 4:
+            mid[...] = part[z] + got_z[0] + got_z[1] + got_z[2]
+        elif i == 5:
+            near[0] = mid[x] + got_x[...]
+        elif i == 6:
+            near[1] = near[0] + got_c[...]
+            near[2, y] = near[1, y]
+        if i < 7:
+            go(i)
+        else:
+            for n in range(2):
+                out_ref[n] = near[2, n] + bias[:, n * 3456 : (n + 1) * 3456]
+
+    return [functools.partial(step, i) for i in range(8)]
+
+
+def normed_tile(value):
+    average = jnp.mean(value, axis=-1, keepdims=True)
+    centred = value - average
+    spread = jnp.mean(centred * centred, axis=-1, keepdims=True)
+    return centred * lax.rsqrt(spread + 1e-06)
+
+
+def rounded(value):
+    return value.astype(BF).astype(F32)
+
+
+def pick(bucket, entries):
+    return sum(
+        jnp.where(bucket == float(i), float(e * (SIDE // 8)), 0.0) for i, e in enumerate(entries)
+    )
+
+
+def start_rows(tok, table, bucket, first, rows):
+    wide = pick(bucket, col_units)
+    spot = (first + lax.broadcasted_iota(jnp.int32, (rows, 1), 0)).astype(F32)
+    lane = lax.broadcasted_iota(jnp.int32, (1, 64), 1).astype(F32)
+    grid_row = jnp.where((spot >= lane * wide) & (spot < (lane + 1.0) * wide), 1.0, 0.0)
+    left = spot - wide * jnp.sum(grid_row * lane, axis=1, keepdims=True)
+    grid_col = jnp.where(left == lane, 1.0, 0.0)
+    high = table.astype(BF)
+    low = (table - high.astype(F32)).astype(BF)
+    parts = [matmul(hot.astype(BF), high) + matmul(hot.astype(BF), low) for hot in (grid_row, grid_col)]
+    return tok.astype(F32) + jnp.concatenate(parts, axis=1)
+
+
+def forward_kernel(*refs):
+    (tok, cot, bucket_in, table, att_m, proj_m, exp_m, red_m, mod_w, cond_in, bias_in) = refs[:11]
+    gq, gp, gu, gd = full = refs[11:15]
+    (mod_out, lhs, x0_out, dy_out, cl_out, h1_out, q_out, k_out, v_out) = refs[15:24]
+    (attnt_out, lse_out, ba_out, x1_out, h2_out, act_out, der_out, bb_out, y_out, gred_out) = refs[24:34]
+    (oq, op, ou, od, fq, tq, fu, tu) = refs[34:42]
+    mod_bufs = refs[42:49]
+    (xs, x0, dy, bucket, closing, h1, qa, ka, vt, attnt, attn) = refs[49:60]
+    (ps, pr, ds, dr, acc, x1, h2, act, der, ba, bb, yo, gstage) = refs[60:73]
+    (b_all, b_q, b_v, b_u) = refs[73:77]
+    lsem = refs[77]
+    gather_sems = refs[78:88]
+    ms, mr, ws, wr, ts, tr, os, outs_sem, gsem = refs[88:97]
+    z, x, c, y = place()
+    xn, yn, twin, zn = partners()
+    half = x0.shape[0]
+    mine = pl.multiple_of(c * half, half)
+    other = pl.multiple_of((1 - c) * half, half)
+    gather = Gather((oq, op, ou, od), full, gather_sems)
+    mods = mod_steps(cond_in, mod_w, b_all, mod_out, lhs, mod_bufs, ms, mr)
+    greet([xn, yn, twin] + zn[1:], swapped=True)
+    mods[0]()
+
+    def split(master, width, f, t, i):
+        count = master.shape[1] // (2 * width)
+        sides = [
+            jnp.concatenate(
+                [master[:, (2 * j + p) * width : (2 * j + p + 1) * width] for j in range(count)], axis=1
+            )
+            for p in (0, 1)
+        ]
+        t[...] = jnp.where(c == 0, sides[1], sides[0])
+        rdma(t, f.at[c], os.at[0, i], os.at[1, i], twin).start()
+        f[c] = jnp.where(c == 0, sides[0], sides[1])
+
+    def joined(f, t, i, piece):
+        rdma(t, f.at[c], os.at[0, i], os.at[1, i], twin).wait()
+        piece[...] = jnp.concatenate([f[0], f[1]], axis=0).astype(BF)
+
+    split(att_m, HEAD_DIM, fq, tq, 0)
+    mods[1]()
+    split(exp_m, BLOCK, fu, tu, 1)
+    mods[2]()
+    joined(fq, tq, 0, oq)
+    steps = gather.steps()
+    done = [2]
+    gather.start(0)
+    gather.start(1)
+
+    swap_to = (z, x, y, c)
+    PART = 128
+    moves = [(bucket_in, bucket)]
+    for i in range(half // PART):
+        moves.append((xs.at[pl.ds(i * PART, PART)], x0.at[pl.ds(i * PART, PART)]))
+    for i in range(half // PART):
+        moves.append((cot.at[pl.ds(i * PART, PART)], dy.at[pl.ds(i * PART, PART)]))
+
+    def move(i):
+        @pl.when(c != y)
+        def _():
+            rdma(*moves[i], ws.at[i], wr.at[i], swap_to).start()
+
+        @pl.when(c == y)
+        def _():
+            pltpu.make_async_copy(*moves[i], ws.at[i]).start()
+
+    def moved(i):
+        @pl.when(c != y)
+        def _():
+            rdma(*moves[i], ws.at[i], wr.at[i], swap_to).wait()
+
+        @pl.when(c == y)
+        def _():
+            pltpu.make_async_copy(*moves[i], ws.at[i]).wait()
+
+    move(0)
+    for i in range(half // PART):
+        rows = slice(i * PART, (i + 1) * PART)
+        xs[rows, :] = start_rows(
+            tok[rows, :], table[...], bucket_in[0:1, 0:1], y * half + i * PART, PART
+        ).astype(BF)
+        move(1 + i)
+    mods[3]()
+    joined(fu, tu, 1, ou)
+    op[...] = proj_m[...].astype(BF)
+    od[...] = red_m[...].astype(BF)
+    owns = [
+        pltpu.make_async_copy(
+            gather.own[w], piece_at(full[w], w, y, z, x, 0, PIECES[NAMES[w]][0]), lsem.at[w]
+        )
+        for w in range(4)
+    ]
+    for d in owns:
+        d.start()
+    b_all[...] = rounded(bias_in[...])
+
+    def of_core(base, width, count):
+        return jnp.concatenate(
+            [
+                jnp.where(
+                    c == 0,
+                    b_all[:, base + 2 * j * width : base + (2 * j + 1) * width],
+                    b_all[:, base + (2 * j + 1) * width : base + (2 * j + 2) * width],
+                )
+                for j in range(count)
+            ],
+            axis=1,
+        )
+
+    b_q[...] = of_core(6 * D, HEAD_DIM, 8)
+    b_v[...] = of_core(7 * D, HEAD_DIM, 8)
+    b_u[...] = of_core(9 * D, BLOCK, 8)
+    b_p = b_all.at[:, pl.ds(8 * D, D)]
+    b_d = b_all.at[:, pl.ds(9 * D + FF, D)]
+
+    def tick(n):
+        for f, *a in steps[done[0] : done[0] + n]:
+            f(*a)
+        done[0] = min(done[0] + n, len(steps))
+
+    def tick_until(chunk):
+        last = max(i for i, s in enumerate(steps) if s[0] == gather.last and s[1] == chunk)
+        tick(max(0, last + 1 - done[0]))
+
+    tick(3)
+    mods[4]()
+    tick(3)
+    mods[5]()
+    tick(2)
+    mods[6]()
+    tick(2)
+    mods[7]()
+    for i in range(1 + half // PART):
+        moved(i)
+
+    def vec(i):
+        return mod_out[i // 3, :, (i % 3) * D : (i % 3 + 1) * D]
+
+    TILE, WIDE = 128, 256
+    tiles = half // TILE
+
+    def own_tile(ref, t):
+        return ref.at[pl.ds(pl.multiple_of(mine + t * TILE, TILE), TILE)]
+
+    def give(ref, t, i):
+        part = own_tile(ref, t)
+        return rdma(part, part, ts.at[i, t], tr.at[i, t], twin)
+
+    def norm_one(t, _):
+        rows = pl.ds(pl.multiple_of(t * TILE, TILE), TILE)
+        value = normed_tile(x0[rows, :].astype(F32)) * (1.0 + vec(1)) + vec(0)
+        own_tile(h1, t)[...] = value.astype(BF)
+        give(h1, t, 0).start()
+        return 0
+
+    for t in range(tiles):
+        norm_one(t, 0)
+        tick(1)
+    tick_until(1)
+    for i in range(half // PART):
+        move(1 + half // PART + i)
+
+    def both_got(ref, i):
+        for t in range(tiles):
+            give(ref, t, i).wait_send()
+            part = ref.at[pl.ds(pl.multiple_of(other + t * TILE, TILE), TILE)]
+            rdma(part, part, ts.at[i, t], tr.at[i, t], twin).wait_recv()
+
+    out_copies = []
+
+    def put(src, dst):
+        d = pltpu.make_async_copy(src, dst, outs_sem.at[len(out_copies)])
+        d.start()
+        out_copies.append(d)
+
+    def load(src, dst, i):
+        d = pltpu.make_async_copy(src, dst, lsem.at[i])
+        d.start()
+        d.wait()
+
+    owns[0].wait()
+    live = pick(bucket[0:1, 0:1], row_units) * pick(bucket[0:1, 0:1], col_units)
+    lane = lax.broadcasted_iota(jnp.int32, (1, 128), 1)
+
+    def qkv(weight):
+        load(gq, weight, 4)
+
+        def rows_of(i, _):
+            start = pl.multiple_of(i * 256, 256)
+            rows = pl.ds(start, 256)
+            left = h1[rows, :]
+            one = matmul(left, weight[0])
+            two = matmul(left, weight[1])
+            spot = (start + lax.broadcasted_iota(jnp.int32, (256, 1), 0)).astype(F32)
+            mask = jnp.where(lane == HEAD_DIM, jnp.where(spot < live, 0.0, -1e30), 0.0)
+            ones = jnp.where(lane == HEAD_DIM, 1.0, 0.0)
+            for j in range(8):
+                cols = slice(j * HEAD_DIM, (j + 1) * HEAD_DIM)
+                query = one[:, cols] + b_q[:, cols]
+                key = one[:, 576 + j * 72 : 648 + j * 72] if j < 4 else two[:, j * 72 - 288 : j * 72 - 216]
+                value = two[:, 288 + j * 72 : 360 + j * 72] + b_v[:, cols]
+                fill = jnp.zeros((256, 56), F32)
+                qa[j, rows, :] = (jnp.concatenate([query, fill], axis=1) + ones).astype(BF)
+                ka[j, rows, :] = (jnp.concatenate([key, fill], axis=1) + mask).astype(BF)
+                vt[j, :, rows] = value.T.astype(BF)
+            return 0
+
+        rows_of(2 * c, 0)
+        tick(2)
+        rows_of(2 * c + 1, 0)
+        both_got(h1, 0)
+        tick(2)
+        rows_of(2 - 2 * c, 0)
+        tick(2)
+        rows_of(3 - 2 * c, 0)
+
+    pl.run_scoped(qkv, VM((2, D, 864), BF))
+    put(h1, h1_out)
+    tick(1)
+    put(qa, q_out)
+    put(ka, k_out)
+    put(vt, v_out)
+
+    def head(j, _):
+        def queries(i, _):
+            rows = pl.ds(pl.multiple_of(i * 256, 256), 256)
+            scores = matmul_nt(ka[j], qa[j, rows, :]) * ALPHA
+            top = jnp.max(scores, axis=0, keepdims=True)
+            prob = jnp.exp2(scores - top)
+            total = jnp.sum(prob, axis=0, keepdims=True)
+            result = matmul(vt[j], prob.astype(BF)) * (1.0 / total)
+            attnt[j, :, rows] = result
+            lse_out[j, :, rows] = top + jnp.log2(total)
+            return 0
+
+        lax.fori_loop(0, 4, queries, 0)
+        return 0
+
+    for j in range(8):
+        head(j, 0)
+        tick(3)
+
+    for i in range(half // PART):
+        moved(1 + half // PART + i)
+
+    def close(t, _):
+        rows = pl.ds(pl.multiple_of(t * TILE, TILE), TILE)
+        spot = (mine + t * TILE + lax.broadcasted_iota(jnp.int32, (TILE, 1), 0)).astype(F32)
+        outer = jnp.where(spot < live, dy[rows, :].astype(F32), 0.0)
+        dy[rows, :] = outer.astype(BF)
+        own_tile(closing, t)[...] = (outer * vec(5)).astype(BF)
+        give(closing, t, 1).start()
+        return 0
+
+    lax.fori_loop(0, tiles, close, 0)
+    put(attnt, attnt_out)
+    tick_until(2)
+    owns[1].wait()
+
+    def proj(weight, stage, raw):
+        load(gp, raw, 5)
+        for i in (0, 1):
+            for h in range(8):
+                stage[h * 72 : h * 72 + 72, :] = raw[i, h].astype(F32)
+            weight[i] = stage[...].astype(BF)
+
+        def attn_rows(i, _):
+            rows = pl.ds(pl.multiple_of(i * 256, 256), 256)
+            value = jnp.concatenate([attnt[j, :, rows] for j in range(8)], axis=0)
+            attn[rows, :] = value.T.astype(BF)
+            return 0
+
+        lax.fori_loop(0, 4, attn_rows, 0)
+
+        def for_twin(t, _):
+            rows = pl.ds(pl.multiple_of(t * WIDE, WIDE), WIDE)
+            left = attn[pl.ds(pl.multiple_of(other + t * WIDE, WIDE), WIDE), :]
+            for i in (0, 1):
+                ps[rows, i * 576 : (i + 1) * 576] = matmul(left, weight[i]).astype(BF)
+            rdma(ps.at[rows], pr.at[rows], ts.at[2, t], tr.at[2, t], twin).start()
+            return 0
+
+        for t in range(half // WIDE):
+            for_twin(t, 0)
+            tick(1)
+
+        def for_me(t, _):
+            rows = pl.ds(pl.multiple_of(t * WIDE, WIDE), WIDE)
+            left = attn[pl.ds(pl.multiple_of(mine + t * WIDE, WIDE), WIDE), :]
+            for i in (0, 1):
+                acc[rows, i * 576 : (i + 1) * 576] = matmul(left, weight[i])
+            return 0
+
+        for t in range(half // WIDE):
+            for_me(t, 0)
+            tick(1)
+
+    pl.run_scoped(proj, VM((2, 576, 576), BF), VM((576, 576), F32), VM((2, 8, 72, 576), BF))
+
+    def middle(t, _):
+        rows = pl.ds(pl.multiple_of(t * TILE, TILE), TILE)
+        branch = acc[rows, :] + pr[rows, :].astype(F32) + b_p[...]
+        ba[rows, :] = branch.astype(BF)
+        value = x0[rows, :].astype(F32) + vec(2) * branch
+        x1[rows, :] = value
+        own_tile(h2, t)[...] = (normed_tile(value) * (1.0 + vec(4)) + vec(3)).astype(BF)
+        give(h2, t, 3).start()
+        return 0
+
+    def half_got(src, dst, i, t):
+        rows = pl.ds(t * WIDE, WIDE)
+        rdma(src.at[rows], dst.at[rows], ts.at[i, t], tr.at[i, t], twin).wait()
+
+    for t in range(tiles):
+        if t % 2 == 0:
+            half_got(ps, pr, 2, t // 2)
+        middle(t, 0)
+    put(ba, ba_out)
+    put(x1, x1_out)
+    put(x0, x0_out)
+    put(dy, dy_out)
+    tick_until(4)
+    owns[2].wait()
+    both_got(h2, 3)
+    both_got(closing, 1)
+    put(h2, h2_out)
+    put(closing, cl_out)
+
+    def up(weight):
+        load(gu, weight, 6)
+
+        def rows_of(n, _):
+            rows = pl.ds(pl.multiple_of(n * 128, 128), 128)
+            left = h2[rows, :]
+            for i in (0, 1):
+                cols = slice(i * D, (i + 1) * D)
+                u = matmul(left, weight[i]) + b_u[:, cols]
+                square = u * u
+                bent = jnp.tanh(GELU_A * u * (1.0 + GELU_B * square))
+                act[rows, cols] = (0.5 * u * (1.0 + bent)).astype(BF)
+                slope = (0.5 * GELU_A) * u * (1.0 - bent * bent) * (1.0 + 3.0 * GELU_B * square)
+                der[rows, cols] = (0.5 * (1.0 + bent) + slope).astype(BF)
+            return 0
+
+        for n in range(8):
+            rows_of(n, 0)
+            tick(1)
+
+    pl.run_scoped(up, VM((2, D, D), BF))
+    put(act, act_out)
+    put(der, der_out)
+
+    gouts = []
+    for t in range(6):
+        slot = t % 2
+        if t >= 2:
+            gouts[t - 2].wait()
+        left = act[:, t * 384 : (t + 1) * 384]
+        for i in (0, 1):
+            gstage[slot, i] = matmul_tn(left, closing[:, i * 576 : (i + 1) * 576]).astype(BF)
+        d = pltpu.make_async_copy(
+            gstage.at[slot], gred_out.at[:, pl.ds(t * 384, 384)], gsem.at[slot]
+        )
+        d.start()
+        gouts.append(d)
+        tick(2)
+    for d in gouts[-2:]:
+        d.wait()
+    tick(len(steps))
+    owns[3].wait()
+
+    def down(weight):
+        load(gd, weight, 7)
+
+        def for_twin(t, _):
+            rows = pl.ds(pl.multiple_of(t * WIDE, WIDE), WIDE)
+            left = act[pl.ds(pl.multiple_of(other + t * WIDE, WIDE), WIDE), :]
+            for i in (0, 1):
+                ds[rows, i * 576 : (i + 1) * 576] = matmul(left, weight[i]).astype(BF)
+            rdma(ds.at[rows], dr.at[rows], ts.at[4, t], tr.at[4, t], twin).start()
+            return 0
+
+        for t in range(half // WIDE):
+            for_twin(t, 0)
+            tick(1)
+
+        def for_me(t, _):
+            rows = pl.ds(pl.multiple_of(t * WIDE, WIDE), WIDE)
+            left = act[pl.ds(pl.multiple_of(mine + t * WIDE, WIDE), WIDE), :]
+            for i in (0, 1):
+                acc[rows, i * 576 : (i + 1) * 576] = matmul(left, weight[i])
+            return 0
+
+        for t in range(half // WIDE):
+            for_me(t, 0)
+            tick(1)
+
+    pl.run_scoped(down, VM((2, 2304, 576), BF))
+
+    def finish(t, _):
+        rows = pl.ds(pl.multiple_of(t * TILE, TILE), TILE)
+        branch = acc[rows, :] + dr[rows, :].astype(F32) + b_d[...]
+        bb[rows, :] = branch.astype(BF)
+        yo[rows, :] = (x1[rows, :] + vec(5) * branch).astype(BF)
+        return 0
+
+    for t in range(tiles):
+        if t % 2 == 0:
+            half_got(ds, dr, 4, t // 2)
+        finish(t, 0)
+    put(bb, bb_out)
+    put(yo, y_out)
+    for d in out_copies:
+        d.wait()
+    gather.finish()
+
+
+def forward_block(tokens, cotangent, bucket, table, masters, modulate_master, cond, biases):
+    shapes = {
+        "gq": (2, D, 864),
+        "gp": (2, 8, 72, 576),
+        "gu": (2, D, D),
+        "gd": (2, 2304, 576),
+    }
+    half = tokens.shape[0]
+    rows = 2 * half
+    out_shape, out_specs = [], []
+
+    def out(shape, dtype, space=ANY):
+        out_shape.append(jax.ShapeDtypeStruct(shape, dtype))
+        out_specs.append(pl.BlockSpec(memory_space=space))
+
+    for s in shapes.values():
+        out(s, BF)
+    out((2, 1, 3456), F32, VM)
+    out((16, 128), F32, VM)
+    out((half, D), BF)
+    out((half, D), BF)
+    out((rows, D), BF)
+    out((rows, D), BF)
+    out((8, rows, 128), BF)
+    out((8, rows, 128), BF)
+    out((8, 72, rows), BF)
+    out((8, 72, rows), F32)
+    out((8, 1, rows), F32, VM)
+    out((half, D), BF)
+    out((half, D), F32)
+    out((rows, D), BF)
+    out((rows, 2304), BF)
+    out((rows, 2304), BF)
+    out((half, D), BF)
+    out((half, D), BF)
+    out((2, 2304, 576), BF)
+    dma = pltpu.SemaphoreType.DMA
+    scratch = [
+        VM((144, 864), BF),
+        VM((72, 576), BF),
+        VM((144, D), BF),
+        VM((288, 576), BF),
+        VM((2, 72, 864), F32),
+        VM((72, 864), F32),
+        VM((2, 72, D), F32),
+        VM((72, D), F32),
+        VM((4, 2, 2, 16, 128), F32),
+        VM((4, 2, 2, 1, 3456), F32),
+        VM((3, 2, 2, 1, 3456), F32),
+        VM((2, 2, 1, 3456), F32),
+        VM((2, 1, 3456), F32),
+        VM((3, 2, 1, 3456), F32),
+        VM((2, 1, 3456), F32),
+        VM((half, D), BF),
+        VM((half, D), BF),
+        VM((half, D), BF),
+        VM((8, 128), F32),
+        VM((rows, D), BF),
+        VM((rows, D), BF),
+        VM((8, rows, 128), BF),
+        VM((8, rows, 128), BF),
+        VM((8, 72, rows), BF),
+        VM((8, 72, rows), F32),
+        VM((rows, 576), BF),
+        VM((half, D), BF),
+        VM((half, D), BF),
+        VM((half, D), BF),
+        VM((half, D), BF),
+        VM((half, D), F32),
+        VM((half, D), F32),
+        VM((rows, D), BF),
+        VM((rows, 2304), BF),
+        VM((rows, 2304), BF),
+        VM((half, D), BF),
+        VM((half, D), BF),
+        VM((half, D), BF),
+        VM((2, 2, 384, 576), BF),
+        VM((1, 14 * D), F32),
+        VM((1, 576), F32),
+        VM((1, 576), F32),
+        VM((1, 2304), F32),
+        dma((8,)),
+    ]
+    n = len(CHUNKS)
+    scratch += [dma((n, 4))] * 6 + [dma((n, 4, 2))] * 2 + [dma((n, 4))] * 2
+    scratch += [
+        dma((7, 3)),
+        dma((7, 3)),
+        dma((9,)),
+        dma((9,)),
+        dma((5, 4)),
+        dma((5, 4)),
+        dma((2, 2)),
+        dma((20,)),
+        dma((2,)),
+    ]
+    vm = pl.BlockSpec(memory_space=VM)
+    hbm = pl.BlockSpec(memory_space=ANY)
+    return pl.pallas_call(
+        forward_kernel,
+        out_shape=out_shape,
+        in_specs=[vm, hbm] + [vm] * 9,
+        out_specs=out_specs,
+        scratch_shapes=scratch,
+        compiler_params=pltpu.CompilerParams(
+            collective_id=0, has_side_effects=True, vmem_limit_bytes=60 * 2**20
+        ),
+        name="forward_block",
+    )(tokens, cotangent, bucket, table, *masters, modulate_master, cond, biases)
+
+
+OLD_PIECES = {"q": (144, 864, 96), "p": (72, 576, None), "u": (144, 1152, 96), "d": (288, 576, 192)}
+
+
+def old_parts(rows, cut, k):
     if cut is None:
         return ((0, rows), None) if k % 2 == 0 else (None, (0, rows))
     return (0, cut), (cut, rows - cut)
-
-
-def gather_kernel(*refs):
-    own, full = refs[0:4], refs[4:8]
-    lsem, zs, zr, xs, xr, ys, yr, fs, fr = refs[8:]
-    z, x, c, y = place()
-    xn, yn = (z, 1 - x, c, y), (z, x, c, 1 - y)
-    zn = [None] + [(at_z(k), x, c, y) for k in (1, 2, 3)]
-    greet([xn, yn] + zn[1:])
-    pending = []
-    for w in range(4):
-        mine = full[w].at[y, z, x]
-        pltpu.make_async_copy(own[w], mine, lsem.at[w]).start()
-        for k in (1, 2, 3):
-            d = rdma(own[w], mine, zs.at[w, k], zr.at[w, k], zn[k])
-            d.start()
-            pending.append(d)
-        for to, s, r in ((xn, xs, xr), (yn, ys, yr)):
-            d = rdma(own[w], mine, s.at[w, 0], r.at[w, 0], to)
-            d.start()
-            pending.append(d)
-    for w in range(4):
-        rows, _, cut = PIECES[NAMES[w]]
-        for k in (1, 2, 3):
-            piece = full[w].at[y, at_z(k), x]
-            rdma(piece, piece, zs.at[w, k], zr.at[w, k], zn[k]).wait_recv()
-            for to, s, r in ((xn, xs, xr), (yn, ys, yr)):
-                d = rdma(piece, piece, s.at[w, k], r.at[w, k], to)
-                d.start()
-                pending.append(d)
-        for k in range(4):
-            zk = z if k == 0 else at_z(k)
-            by_x, by_y = parts_of(rows, cut, k)
-            piece = full[w].at[y, zk, 1 - x]
-            rdma(piece, piece, xs.at[w, k], xr.at[w, k], xn).wait_recv()
-            if by_x is not None:
-                part = full[w].at[y, zk, 1 - x, pl.ds(*by_x)]
-                d = rdma(part, part, fs.at[w, k, 0], fr.at[w, k, 0], yn)
-                d.start()
-                pending.append(d)
-            piece = full[w].at[1 - y, zk, x]
-            rdma(piece, piece, ys.at[w, k], yr.at[w, k], yn).wait_recv()
-            if by_y is not None:
-                part = full[w].at[1 - y, zk, x, pl.ds(*by_y)]
-                d = rdma(part, part, fs.at[w, k, 1], fr.at[w, k, 1], xn)
-                d.start()
-                pending.append(d)
-    for w in range(4):
-        rows, _, cut = PIECES[NAMES[w]]
-        pltpu.make_async_copy(own[w], full[w].at[y, z, x], lsem.at[w]).wait()
-        for k in range(4):
-            zk = z if k == 0 else at_z(k)
-            for i, span in enumerate(parts_of(rows, cut, k)):
-                if span is not None:
-                    part = full[w].at[1 - y, zk, 1 - x, pl.ds(*span)]
-                    rdma(part, part, fs.at[w, k, i], fr.at[w, k, i], xn).wait_recv()
-    for d in pending:
-        d.wait_send()
-
-
-def gather_weights(own):
-    any_space = pl.BlockSpec(memory_space=pl.ANY)
-    dma = pltpu.SemaphoreType.DMA
-    return pl.pallas_call(
-        gather_kernel,
-        out_shape=[
-            jax.ShapeDtypeStruct((2, 4, 2) + PIECES[n][:2], jnp.bfloat16) for n in NAMES
-        ],
-        in_specs=[any_space] * 4,
-        out_specs=[any_space] * 4,
-        scratch_shapes=[dma((4,))] + [dma((4, 4))] * 6 + [dma((4, 4, 2))] * 2,
-        compiler_params=pltpu.CompilerParams(collective_id=0, has_side_effects=True),
-        name="gather_weights",
-    )(*own)
 
 
 def scatter_kernel(*refs):
@@ -584,10 +1311,10 @@
         return z if k == 0 else at_z(k)
 
     for w in range(4):
-        rows, _, cut = PIECES[NAMES[w]]
+        rows, _, cut = OLD_PIECES[NAMES[w]]
         pltpu.make_async_copy(grads[w], held[w], lsem.at[w]).wait()
         for k in order:
-            spans = parts_of(rows, cut, k)
+            spans = old_parts(rows, cut, k)
             for i, (span, to) in enumerate(zip(spans, (yn, xn))):
                 if span is not None:
                     d = rdma(
@@ -600,9 +1327,9 @@
                     d.start()
                     pending.append(d)
     for w in range(4):
-        rows, _, cut = PIECES[NAMES[w]]
+        rows, _, cut = OLD_PIECES[NAMES[w]]
         for k in order:
-            spans = parts_of(rows, cut, k)
+            spans = old_parts(rows, cut, k)
             for i, span in enumerate(spans):
                 piece = held[w].at[(y, z_of(k), 1 - x) if i == 0 else (1 - y, z_of(k), x)]
                 if span is not None:
@@ -643,7 +1370,7 @@
 
 def scatter_grads(grads):
     dma = pltpu.SemaphoreType.DMA
-    shapes = [PIECES[n][:2] for n in NAMES]
+    shapes = [OLD_PIECES[n][:2] for n in NAMES]
 
     def boxes(*lead):
         return [pltpu.VMEM(lead + s, jnp.bfloat16) for s in shapes]
@@ -666,79 +1393,6 @@
         ),
         name="scatter_grads",
     )(*grads)
-
-
-def mod_kernel(cond_ref, weight_ref, out_ref, lhs, conds, part, got_z, mid, got_x, near, got_c, s, r):
-    z, x, c, y = place()
-    xn, yn, twin = (z, 1 - x, c, y), (z, x, c, 1 - y), (z, x, 1 - c, y)
-    zn = [None] + [(at_z(k), x, c, y) for k in (1, 2, 3)]
-    greet([xn, yn, twin] + zn[1:])
-    conds[z, x, c] = cond_ref[...]
-    d = rdma(conds.at[z, x, c], conds.at[z, x, c], s.at[0], r.at[0], twin)
-    d.start()
-    d.wait()
-    d = rdma(conds.at[z, x], conds.at[z, x], s.at[1], r.at[1], xn)
-    d.start()
-    d.wait()
-    ds = [rdma(conds.at[z], conds.at[z], s.at[1 + k], r.at[1 + k], zn[k]) for k in (1, 2, 3)]
-    for d in ds:
-        d.start()
-    for d in ds:
-        d.wait()
-    me = (z * 2 + x) * 2 + c
-    for i in range(16):
-        lhs[pl.ds(i, 1), :] = conds[i // 4, i // 2 % 2, i % 2, pl.ds(me, 1), :]
-    result = jnp.dot(
-        lhs[:, :72].astype(jnp.bfloat16), weight_ref[...], preferred_element_type=jnp.float32
-    )
-    for i in range(16):
-        part[i // 4, i // 2 % 2, i % 2] = result[i : i + 1]
-    ds = [
-        rdma(part.at[at_z(k)], got_z.at[k - 1], s.at[4 + k], r.at[4 + k], zn[k]) for k in (1, 2, 3)
-    ]
-    for d in ds:
-        d.start()
-    for d in ds:
-        d.wait()
-    mid[...] = part[z] + got_z[0] + got_z[1] + got_z[2]
-    d = rdma(mid.at[1 - x], got_x, s.at[8], r.at[8], xn)
-    d.start()
-    d.wait()
-    near[0] = mid[x] + got_x[...]
-    d = rdma(near.at[0], got_c, s.at[9], r.at[9], twin)
-    d.start()
-    d.wait()
-    near[1] = near[0] + got_c[...]
-    out_ref[y] = near[1, y]
-    d = rdma(near.at[1, 1 - y], out_ref.at[y], s.at[10], r.at[10], yn)
-    d.start()
-    d.wait()
-
-
-def image_modulation(cond, weight):
-    f32, vm = jnp.float32, pltpu.VMEM
-    return pl.pallas_call(
-        mod_kernel,
-        out_shape=[
-            jax.ShapeDtypeStruct((2, 1, 3456), f32),
-            jax.ShapeDtypeStruct((16, 128), f32),
-        ],
-        in_specs=[pl.BlockSpec(memory_space=vm)] * 2,
-        out_specs=[pl.BlockSpec(memory_space=vm)] * 2,
-        scratch_shapes=[
-            vm((4, 2, 2, 16, 128), f32),
-            vm((4, 2, 2, 1, 3456), f32),
-            vm((3, 2, 2, 1, 3456), f32),
-            vm((2, 2, 1, 3456), f32),
-            vm((2, 1, 3456), f32),
-            vm((2, 2, 1, 3456), f32),
-            vm((2, 1, 3456), f32),
-            pltpu.SemaphoreType.DMA((11,)),
-            pltpu.SemaphoreType.DMA((11,)),
-        ],
-        compiler_params=pltpu.CompilerParams(collective_id=2, has_side_effects=True),
-        name="image_modulation",
-    )(cond, weight)
 
 
 def totals_kernel(mod_ref, bias_ref, mods, sums, got_m, got_b, got_z, s, r):
@@ -895,20 +1549,6 @@
     ).reshape(2, 4, 2, rows, cols)
 
 
-def core_columns(shard, width):
-    rows, cols = shard.shape
-    blocks = shard.reshape(rows, cols // (2 * width), 2, width)
-    return blocks.transpose(2, 0, 1, 3).reshape(2, rows, cols // 2)
-
-
-def chip_piece(shard, width):
-    c = lax.axis_index("c")
-    split = core_columns(shard, width)
-    mine = lax.dynamic_index_in_dim(split, c, 0, keepdims=False)
-    other = to_twin(lax.dynamic_index_in_dim(split, 1 - c, 0, keepdims=False))
-    return jnp.where(c == 0, jnp.concatenate([mine, other]), jnp.concatenate([other, mine]))
-
-
 def shard_from_pieces(piece, width):
     c = lax.axis_index("c")
     half = piece.shape[0] // 2
@@ -959,74 +1599,78 @@
     biases_first,
     biases_second,
 ):
+
     z, x, c, y = place()
     bf16, f32 = jnp.bfloat16, jnp.float32
     block = FF // 16
-    own = (
-        chip_piece(attend_master.astype(bf16), HEAD_DIM),
-        project_master.astype(bf16),
-        chip_piece(expand_master.astype(bf16), block),
-        reduce_master.astype(bf16),
-    )
-    weight_q, weight_p, weight_u, weight_d = gather_weights(own)
-    weight_q = weight_q.reshape(2, D, 864)
-    weight_p = weight_p.reshape(2, 576, 576)
-    weight_u = weight_u.reshape(2, D, D)
-    weight_d = weight_d.reshape(2, 2304, 576)
-
     class_row = lax.dynamic_slice_in_dim(class_table, labels[0], 1).astype(f32)
     condition = jax.nn.silu(class_row + time_features(timesteps, D)).astype(bf16).astype(f32)
     cond_tiles = jnp.pad(condition.reshape(16, 72), ((0, 0), (0, 56)))
-    bias_low = biases_master.astype(bf16).astype(f32)
-    modulation, cond_all = image_modulation(cond_tiles, modulate_master.astype(bf16))
-    modulation = modulation.reshape(6 * D) + bias_low[: 6 * D]
+    bucket = jnp.broadcast_to(buckets.astype(f32)[:, None], (8, 128))
+    steps = jnp.arange(64, dtype=f32)[:, None]
+    omegas = jnp.exp(-math.log(10000.0) * jnp.arange(288, dtype=f32) / 288)[None, :]
+    table = jnp.concatenate([jnp.sin(steps * omegas), jnp.cos(steps * omegas)], axis=1)
+    (
+        weight_q,
+        weight_p,
+        weight_u,
+        weight_d,
+        modulation,
+        cond_all,
+        residual_zero,
+        outer_grad,
+        closing_all,
+        hidden_attend,
+        queries,
+        key_rows,
+        value_rows,
+        attn_t,
+        log_sums,
+        branch_attend,
+        residual_one,
+        hidden_expand,
+        activated,
+        slope,
+        branch_expand,
+        output,
+        grad_reduce,
+    ) = forward_block(
+        tokens,
+        cotangent,
+        bucket,
+        table,
+        (attend_master, project_master, expand_master, reduce_master),
+        modulate_master,
+        cond_tiles,
+        biases_master[None, :],
+    )
+
+    modulation = modulation.reshape(6 * D)
     shift_one, scale_one, gating_one, shift_two, scale_two, gating_two = (
         modulation[i * D : (i + 1) * D][None, :] for i in range(6)
     )
-    offset_base = 6 * D
-    bias_query = core_bias(bias_low[offset_base : offset_base + D], HEAD_DIM)
-    bias_value = core_bias(bias_low[offset_base + D : offset_base + 2 * D], HEAD_DIM)
-    bias_proj = bias_low[offset_base + 2 * D : offset_base + 3 * D]
-    bias_hidden = core_bias(bias_low[offset_base + 3 * D : offset_base + 3 * D + FF], block)
-    bias_output = bias_low[offset_base + 3 * D + FF :]
-
-    moved = swap_halves(jnp.stack([tokens, cotangent]))
-    tokens, cotangent = moved[0], moved[1]
-    bucket = swap_halves(buckets)
-    unit_cells = SIDE // 8
-    heights = table_pick(bucket, row_units) * unit_cells
-    widths = table_pick(bucket, col_units) * unit_cells
-    lengths = heights * widths
-    half_rows = tokens.shape[0]
-    position = c * half_rows + jnp.arange(half_rows, dtype=jnp.int32)
-    live_rows = (position < lengths[0]).astype(f32)
-    residual_zero = tokens.astype(f32) + grid_features(position, widths, D)
-
-    hidden_attend = both_halves(modulate(residual_zero, shift_one, scale_one).astype(bf16))
-    packed = wide(hidden_attend, weight_q)
-    queries = (packed[:, :576] + bias_query).astype(bf16)
-    key_rows = packed[:, 576:1152].astype(bf16)
-    value_rows = (packed[:, 1152:] + bias_value).astype(bf16)
-    attention, log_sums = attend(queries, key_rows, value_rows, lengths)
-    branch_attend = sum_halves(wide(attention, weight_p)) + bias_proj
-    residual_one = residual_zero + gating_one * branch_attend
-    hidden_expand = both_halves(modulate(residual_one, shift_two, scale_two).astype(bf16))
-    widened = wide(hidden_expand, weight_u) + bias_hidden
-    activated = jax.nn.gelu(widened, approximate=True).astype(bf16)
-    branch_expand = sum_halves(wide(activated, weight_d)) + bias_output
-    output = swap_halves((residual_one + gating_two * branch_expand).astype(bf16))
-
-    outer_grad = cotangent.astype(f32) * live_rows[:, None]
+    chip_bucket = swap_halves(buckets)
+    unit = SIDE // 8
+    lengths = table_pick(chip_bucket, row_units) * unit * table_pick(chip_bucket, col_units) * unit
+
+    def flat(heads):
+        return heads.transpose(1, 0, 2).reshape(1024, 576)
+
+    queries, key_rows = flat(queries[:, :, :72]), flat(key_rows[:, :, :72])
+    value_rows = value_rows.reshape(576, 1024).T
+    attention = attn_t.reshape(576, 1024).T.astype(bf16)
+    log_sums = log_sums.reshape(8, 2, 512).transpose(1, 0, 2)[None] * math.log(2.0)
+    weight_p = weight_p.reshape(2, 576, 576)
+    output = swap_halves(output)
+    residual_zero = residual_zero.astype(f32)
+    outer_grad = outer_grad.astype(f32)
     gating_later = jnp.sum(outer_grad * branch_expand, axis=0)
     closing_grad = (outer_grad * gating_two).astype(bf16)
-    closing_all = both_halves(closing_grad)
     active_grad = wide_back(closing_all, weight_d)
-    _, gelu_pullback = jax.vjp(lambda inner: jax.nn.gelu(inner, approximate=True), widened)
-    widened_grad = gelu_pullback(active_grad)[0].astype(bf16)
-    grad_reduce = weight_grad(activated, closing_all, "d")
+    widened_grad = (active_grad * slope).astype(bf16)
+    grad_reduce = grad_reduce.reshape(2, 4, 2, 288, 576)
     grad_expand = weight_grad(hidden_expand, widened_grad, "u")
     hidden_grad = sum_halves(wide_back(widened_grad, weight_u))
-
     def norm_back(residual, scaling, gradient):
         average = jnp.mean(residual, axis=-1, keepdims=True)
         centred = residual - average

time: 866 us -> 693 us (0.80)
  the two profiles are of different devices: /device:TPU:0 before, /device:TPU:1 now
where the time goes in v2:
time: 693 us; the launch traced here: 683 us
  Pallas kernels  396 us (57%)
  matrix products  115 us (17%)
  other arithmetic  77.8 us (11%)
  local copies, waits for them, and re-layouts  53.7 us (8%)
  starting transfers between devices  25.6 us (4%)
  between operations  11.7 us (2%)
    pallas_call x1, Pallas kernels, forward_block(): pl.pallas_call(forward_kernel, out_shape=out_shape, in_specs=[vm, hbm] +...  199 us
    pallas_call x1, Pallas kernels, scatter_grads(): pl.pallas_call(scatter_kernel, out_shape=[jax.ShapeDtypeStruct(s, jnp.flo...  166 us
    dot_general x8, matrix products, wide_back(): lax.dot_general(gradient[:, i * half:(i + 1) * half], weight[i], (((1,),...  35.5 us
    dot_general x6, matrix products, weight_grad(): lax.dot_general(left, right[:, i * half:(i + 1) * half], (((0,), (0,)), (...  22 us
    dot_general x2, matrix products, per_block(): jnp.einsum('qhe,khe->hqk', query_block, key_heads, preferred_element_type...  21.5 us
    pallas_call x1, Pallas kernels, share_totals(): pl.pallas_call(totals_kernel, out_shape=[jax.ShapeDtypeStruct((4, 2, 2, 1...  19.1 us
    convert_element_type x2, other arithmetic, per_block(): grad_score = (probability * (grad_prob - inner_sum)).astype(jnp.bfloat16)  18.9 us
    dot_general x2, matrix products, per_block(): jnp.einsum('hqk,qhe->khe', probability.astype(jnp.bfloat16), grad_block,...  18.6 us
  transfers between devices with their start and end apart: 8, of which 1 were waited for; matrix products, arithmetic and copies ran while one was open for 15% of the time, Pallas kernels for 29%

profile of v2, /device:TPU:1, one launch (start us, length us, event | category | flops | bytes accessed | tf_op | source)
XLA Modules:
  0.0 682.6 jit_solution(4664794324466053742)
XLA Ops:
  0.7 4.5 collective-permute-start.2
  12.1 198.7 %forward_block.1 = (bf16[2,1152,864]{2,1,0:T(8,128)(2,1)}, bf16[2,8,72,576]{3,2,1,0:T(8,128)(2,1)}, bf16[2,1152,1152]{2,1,0:T(8,128)(2,1)}, bf16[2,2304,576]{2,1...) custom-call(bf16[512,1152]{1,0:T(8,128)(2,1)} %refs_0_.1, ...), custom_call_target="tpu_custom_call" | custom-call | tf_op jit(solution)/shard_map/forward_block/pallas_call | solution.py:1274
  210.7 6.2 collective-permute-start
  216.9 6.1 fusion.23
  223.0 8.5 %convert_reduce_fusion = (f32[2304]{0:T(1024)}, bf16[1024,2304]{1,0:T(8,128)(2,1)S(1)}) fusion(bf16[1024,2304]{1,0:T(8,128)(2,1)} %get-tuple-element.137, f32[1024,2304]{1,0:T(8,128)S(1)} %fusion.23, bf16[2,2304,576]{2,1,0:T(8,128)(2,1)} %get-tuple-element.136, bf16[1024,1152]{1,0:T(8,128)(2,1)} %get-tuple-element.135), kind=kOutput, calls=%fused_computation.27 | convolution fusion | flops 2732062464 | bytes 23143424 | tf_op jit(solution)/shard_map/dot_general | solution.py:1526
  231.5 7.1 %fusion.33 = f32[1024,1152]{1,0:T(8,128)S(1)} fusion(bf16[2,1152,1152]{2,1,0:T(8,128)(2,1)} %get-tuple-element.138, bf16[1024,2304]{1,0:T(8,128)(2,1)S(1)} %get-tuple-element.307), kind=kOutput, calls=%fused_computation.53 | convolution fusion | flops 2717908992 | bytes 9732096 | tf_op jit(solution)/shard_map/dot_general | solution.py:1526
  238.6 5.6 convolution_add_fusion.1
  244.2 2.9 dynamic-slice_convert_fusion.1
  247.2 7.1 %collective-permute-start.1 = (bf16[512,1152]{1,0:T(8,128)(2,1)}, bf16[512,1152]{1,0:T(8,128)(2,1)}, u32[]{:S(2)}, u32[]{:S(2)}) collective-permute-start(bf16[512,1152]{1,0:T(8,128)(2,1)} %dynamic-slice_convert_fusion.1), channel_id=1, source_target_pairs={{0,2},{2,0},{1,3},{3,1},{4,6},{6,4},{5,7},{7,5},{8,10},{10,8},{9,1... | collective-permute-start | bytes 3538952 | tf_op jit(solution)/shard_map/ppermute | solution.py:1500
  260.9 3.7 copy.66
  264.6 3.0 convert_element_type.177
  269.0 3.7 copy.67
  274.3 2.7 fusion.85
  277.0 5.0 convolution_convert_fusion
  282.1 3.1 multiply_reduce_fusion.1
  285.3 4.1 convert_reduce_fusion.2
  289.4 3.3 convolution_convert_fusion.1
  292.7 2.8 pad_maximum_fusion.refs_2_
  307.8 80.0 %while.26 = (s32[]{:T(128)}, f32[1024,8,72]{0,2,1:T(8,128)}, f32[1024,8,72]{0,2,1:T(8,128)}, bf16[2,512,8,72]{1,3,2,0:T(8,128)(2,1)}, bf16[2,512,8,72]{1,3,2,0:T...) while((s32[]{:T(128)}, f32[1024,8,72]{0,2,1:T(8,128)}, ...), condition=%wide.region_8.9_spmd.clone, body=%wide.region_6.8_spmd.clone.sunk | while | flops 3061183488 | bytes 217860496 | solution.py:186
  308.0 3.8 fusion.120
  311.8 10.7 %multiply_reduce_fusion.15 = (f32[8,512]{1,0:T(8,128)S(1)}, f32[8,512,1024]{2,1,0:T(8,128)}) fusion(f32[8,512,1024]{2,1,0:T(8,128)S(1)} %fusion.120, f32[8,512]{1,0:T(8,128)S(1)} %dynamic-slice_bitcast_fusion.2, bf16[1024,8,72]{0,2,1:T(8,128)(2,1)} %get-tuple-element.408, bf16[2,512,8,72]{1,3,2,0:T(8,128)(2,1)} %get-tuple-element.407, s32[]{:T(128)S(6)} %copy.86, ...), kind=kOutput, calls=%fused_computation.2.clone.1 | convolution fusion | flops 624947200 | bytes 35357700 | tf_op jit(solution)/shard_map/while/body/eval_jaxpr/while/body/eval_jaxpr/qhe,khe->hqk/dot_general | solution.py:144
  322.6 9.4 %multiply_convert_fusion.5 = bf16[8,512,1024]{2,1,0:T(8,128)(2,1)} fusion(f32[8,512,1024]{2,1,0:T(8,128)} %get-tuple-element.377, f32[8,512,1024]{2,1,0:T(8,128)S(1)} %fusion.120, f32[8,512]{1,0:T(8,128)S(1)} %get-tuple-element.378), kind=kLoop, calls=%fused_computation.1.clone.1 | loop fusion | flops 12582912 | bytes 41959424 | tf_op jit(solution)/shard_map/while/body/eval_jaxpr/while/body/eval_jaxpr/convert_element_type | solution.py:155
  332.0 9.0 %bitcast_add_fusion.5 = f32[1024,8,72]{0,2,1:T(8,128)} fusion(f32[1024,8,72]{0,2,1:T(8,128)} %get-tuple-element.393, f32[8,512,1024]{2,1,0:T(8,128)} %get-tuple-element.377, pred[]{:T(512)S(6)} %compare.4, bf16[2,512,8,72]{1,3,2,0:T(8,128)(2,1)S(1)} %copy-done.6, s32[]{:T(128)S(6)} %copy.86), kind=kOutput, calls=%fused_computation.6.clone.1 | convolution fusion | flops 609353728 | bytes 22085636 | tf_op jit(solution)/shard_map/while/body/eval_jaxpr/while/body/eval_jaxpr/hqk,qhe->khe/dot_general | solution.py:169
  341.5 2.7 fusion.121
  347.5 3.8 fusion.120
  351.3 10.7 %multiply_reduce_fusion.15 = (f32[8,512]{1,0:T(8,128)S(1)}, f32[8,512,1024]{2,1,0:T(8,128)}) fusion(f32[8,512,1024]{2,1,0:T(8,128)S(1)} %fusion.120, f32[8,512]{1,0:T(8,128)S(1)} %dynamic-slice_bitcast_fusion.2, bf16[1024,8,72]{0,2,1:T(8,128)(2,1)} %get-tuple-element.408, bf16[2,512,8,72]{1,3,2,0:T(8,128)(2,1)} %get-tuple-element.407, s32[]{:T(128)S(6)} %copy.86, ...), kind=kOutput, calls=%fused_computation.2.clone.1 | convolution fusion | flops 624947200 | bytes 35357700 | tf_op jit(solution)/shard_map/while/body/eval_jaxpr/while/body/eval_jaxpr/qhe,khe->hqk/dot_general | solution.py:144
  362.1 9.4 %multiply_convert_fusion.5 = bf16[8,512,1024]{2,1,0:T(8,128)(2,1)} fusion(f32[8,512,1024]{2,1,0:T(8,128)} %get-tuple-element.377, f32[8,512,1024]{2,1,0:T(8,128)S(1)} %fusion.120, f32[8,512]{1,0:T(8,128)S(1)} %get-tuple-element.378), kind=kLoop, calls=%fused_computation.1.clone.1 | loop fusion | flops 12582912 | bytes 41959424 | tf_op jit(solution)/shard_map/while/body/eval_jaxpr/while/body/eval_jaxpr/convert_element_type | solution.py:155
  371.5 9.6 %bitcast_add_fusion.5 = f32[1024,8,72]{0,2,1:T(8,128)} fusion(f32[1024,8,72]{0,2,1:T(8,128)} %get-tuple-element.393, f32[8,512,1024]{2,1,0:T(8,128)} %get-tuple-element.377, pred[]{:T(512)S(6)} %compare.4, bf16[2,512,8,72]{1,3,2,0:T(8,128)(2,1)S(1)} %copy-done.6, s32[]{:T(128)S(6)} %copy.86), kind=kOutput, calls=%fused_computation.6.clone.1 | convolution fusion | flops 609353728 | bytes 22085636 | tf_op jit(solution)/shard_map/while/body/eval_jaxpr/while/body/eval_jaxpr/hqk,qhe->khe/dot_general | solution.py:169
  381.7 2.7 fusion.121
  389.5 2.5 copy.69
  392.5 3.3 convert_reduce_fusion.4
  396.1 5.9 convolution_convert_fusion.2
  402.0 3.8 convolution_convert_fusion.3
  405.8 2.9 copy.71
  408.6 4.5 copy.72
  413.1 2.9 pad_maximum_fusion.4.refs_1_
  416.0 2.5 pad_maximum_fusion.1.refs_0_
  418.5 165.5 %scatter_grads.1 = (f32[144,864]{1,0:T(8,128)}, f32[72,576]{1,0:T(8,128)}, f32[144,1152]{1,0:T(8,128)}, f32[288,576]{1,0:T(8,128)}) custom-call(bf16[2,4,2,144,864]{4,3,2,1,0:T(8,128)(2,1)} %pad_maximum_fusion.1.refs_0_, bf16[2,4,2,72,576]{4,3,2,1,0:T(8,128)(2,1)} %pad_maximum_fusion.4.refs_1_, bf16[2,4,2,144,1152]{4,3,2,1,0:T(8,128)(2,1)} %pad_maximum_fusion.refs_2_, ...), custom_call_target="tpu_custom_call" | custom-call | tf_op jit(solution)/shard_map/scatter_grads/pallas_call | solution.py:1378
  586.9 2.9 fusion.51
  589.8 3.0 convolution_add_fusion
  602.4 3.4 fusion.42
  606.0 2.2 multiply_reduce_fusion.2
  609.0 19.1 %share_totals.1 = (bf16[4,2,2,16,432]{4,3,2,1,0:T(8,128)(2,1)}, f32[72,128]{1,0:T(8,128)}) custom-call(f32[16,432]{1,0:T(8,128)} %reshape.297.mod_ref, f32[72,128]{1,0:T(8,128)} %bitcast.166), custom_call_target="tpu_custom_call" | custom-call | tf_op jit(solution)/shard_map/share_totals/pallas_call | solution.py:1436
  635.7 12.6 %sum_everywhere.1 = f32[8,128]{1,0:T(8,128)} custom-call(f32[8,128]{1,0:T(8,128)} %broadcast_in_dim.46.in_ref), custom_call_target="tpu_custom_call" | custom-call | tf_op jit(solution)/shard_map/sum_everywhere/pallas_call | solution.py:1479
  657.0 6.5 collective-permute-start.5
  664.2 3.7 multiply_subtract_fusion.1
  673.0 2.2 multiply_subtract_fusion
  678.9 2.4 copy.110
  (289 shorter events, 68.7 us)
Async XLA Ops:
  0.7 294.9 %collective-permute-start.2 = (s32[1]{0:T(128)}, s32[1]{0:T(128)}, u32[]{:S(2)}, u32[]{:S(2)}) collective-permute-start(s32[1]{0:T(128)} %param.31), channel_id=1, source_target_pairs={{0,0},{1,2},{2,1},{3,3},{4,4},{5,6},{6,5},{7,7},{8,8},{9,10},{10,9... | collective-permute-start | bytes 20 | tf_op jit(solution)/shard_map/ppermute | solution.py:1496
  210.7 87.3 %collective-permute-start = (bf16[512,1152]{1,0:T(8,128)(2,1)}, bf16[512,1152]{1,0:T(8,128)(2,1)}, u32[]{:S(2)}, u32[]{:S(2)}) collective-permute-start(bf16[512,1152]{1,0:T(8,128)(2,1)} %get-tuple-element.133), channel_id=1, source_target_pairs={{0,0},{1,2},{2,1},{3,3},{4,4},{5,6},{6,5},{7,7},{8,8},{9,10},{10,9... | collective-permute-start | bytes 3538952 | tf_op jit(solution)/shard_map/ppermute | solution.py:1496
  231.5 7.1 %copy-start.14 = (bf16[1024,2304]{1,0:T(8,128)(2,1)}, bf16[1024,2304]{1,0:T(8,128)(2,1)S(1)}, u32[]{:S(2)}) copy-start(bf16[1024,2304]{1,0:T(8,128)(2,1)S(1)} %get-tuple-element.307) | copy-start | bytes 14155780
  231.5 7.1 %copy-start.73 = (bf16[2,1152,1152]{2,1,0:T(8,128)(2,1)S(1)}, bf16[2,1152,1152]{2,1,0:T(8,128)(2,1)}, u32[]{:S(2)}) copy-start(bf16[2,1152,1152]{2,1,0:T(8,128)(2,1)} %get-tuple-element.138) | copy-start | bytes 15925252
  244.2 11.2 %copy-start.7 = (f32[512,1152]{1,0:T(8,128)S(1)}, f32[512,1152]{1,0:T(8,128)}, u32[]{:S(2)}) copy-start(f32[512,1152]{1,0:T(8,128)} %get-tuple-element.140) | copy-start | bytes 7077892
  247.2 34.9 %collective-permute-start.1 = (bf16[512,1152]{1,0:T(8,128)(2,1)}, bf16[512,1152]{1,0:T(8,128)(2,1)}, u32[]{:S(2)}, u32[]{:S(2)}) collective-permute-start(bf16[512,1152]{1,0:T(8,128)(2,1)} %dynamic-slice_convert_fusion.1), channel_id=1, source_target_pairs={{0,2},{2,0},{1,3},{3,1},{4,6},{6,4},{5,7},{7,5},{8,10},{10,8},{9,1... | collective-permute-start | bytes 3538952 | tf_op jit(solution)/shard_map/ppermute | solution.py:1500
  269.0 3.7 copy-start.51
  269.0 3.8 copy-start.69
  269.0 4.6 copy-start.68
  274.3 7.8 %slice-start.2 = ((s8[4718592]{0:T(1024)(128)(4,1)}), s8[4194304]{0:T(1024)(128)(4,1)S(1)}, s32[]{:S(2)}) async-start(s8[4718592]{0:T(1024)(128)(4,1)} %bitcast.144), calls=%async_computation.2 | async-start | bytes 8388608
  277.0 5.1 slice-start.3
  277.0 5.1 copy-start.63
  277.0 5.1 copy-start.66
  282.1 7.2 %slice-start = ((s8[4718592]{0:T(1024)(128)(4,1)}), s8[4194304]{0:T(1024)(128)(4,1)S(1)}, s32[]{:S(2)}) async-start(s8[4718592]{0:T(1024)(128)(4,1)} %bitcast.142), calls=%async_computation | async-start | bytes 8388608
  285.3 4.1 slice-start.1
  289.4 8.7 %collective-permute-start.3 = (bf16[512,1152]{1,0:T(8,128)(2,1)S(1)}, bf16[512,1152]{1,0:T(8,128)(2,1)S(1)}, u32[]{:S(2)}, u32[]{:S(2)}) collective-permute-start(bf16[512,1152]{1,0:T(8,128)(2,1)S(1)} %get-tuple-element.292), channel_id=1, source_target_pairs={{0,2},{2,0},{1,3},{3,1},{4,6},{6,4},{5,7},{7,5},{8,10},{10,8},{9,1... | collective-permute-start | bytes 3538952 | tf_op jit(solution)/shard_map/ppermute | solution.py:1500
  322.6 9.4 %copy-start.6 = (bf16[2,512,8,72]{1,3,2,0:T(8,128)(2,1)S(1)}, bf16[2,512,8,72]{1,3,2,0:T(8,128)(2,1)}, u32[]{:S(2)}) copy-start(bf16[2,512,8,72]{1,3,2,0:T(8,128)(2,1)} %get-tuple-element.410) | copy-start | bytes 3538948 | tf_op jit(solution)/shard_map/while/body/eval_jaxpr/while
  332.0 9.0 %copy-start = (bf16[8,512,1024]{2,1,0:T(8,128)(2,1)S(1)}, bf16[8,512,1024]{2,1,0:T(8,128)(2,1)}, u32[]{:S(2)}) copy-start(bf16[8,512,1024]{2,1,0:T(8,128)(2,1)} %multiply_convert_fusion.5) | copy-start | bytes 25165828 | tf_op jit(solution)/shard_map/while/body/eval_jaxpr/while
  332.0 9.0 %copy-start.4 = (bf16[1024,8,72]{0,2,1:T(8,128)(2,1)S(1)}, bf16[1024,8,72]{0,2,1:T(8,128)(2,1)}, u32[]{:S(2)}) copy-start(bf16[1024,8,72]{0,2,1:T(8,128)(2,1)} %get-tuple-element.408) | copy-start | bytes 3538948 | tf_op jit(solution)/shard_map/while/body/eval_jaxpr/while
  332.0 9.5 %copy-start.12 = (bf16[2,512,8,72]{1,3,2,0:T(8,128)(2,1)S(1)}, bf16[2,512,8,72]{1,3,2,0:T(8,128)(2,1)}, u32[]{:S(2)}) copy-start(bf16[2,512,8,72]{1,3,2,0:T(8,128)(2,1)} %get-tuple-element.394) | copy-start | bytes 3538948 | tf_op jit(solution)/shard_map/while/body/eval_jaxpr/while
  362.0 9.4 %copy-start.6 = (bf16[2,512,8,72]{1,3,2,0:T(8,128)(2,1)S(1)}, bf16[2,512,8,72]{1,3,2,0:T(8,128)(2,1)}, u32[]{:S(2)}) copy-start(bf16[2,512,8,72]{1,3,2,0:T(8,128)(2,1)} %get-tuple-element.410) | copy-start | bytes 3538948 | tf_op jit(solution)/shard_map/while/body/eval_jaxpr/while
  371.5 9.7 %copy-start = (bf16[8,512,1024]{2,1,0:T(8,128)(2,1)S(1)}, bf16[8,512,1024]{2,1,0:T(8,128)(2,1)}, u32[]{:S(2)}) copy-start(bf16[8,512,1024]{2,1,0:T(8,128)(2,1)} %multiply_convert_fusion.5) | copy-start | bytes 25165828 | tf_op jit(solution)/shard_map/while/body/eval_jaxpr/while
  371.5 9.7 %copy-start.4 = (bf16[1024,8,72]{0,2,1:T(8,128)(2,1)S(1)}, bf16[1024,8,72]{0,2,1:T(8,128)(2,1)}, u32[]{:S(2)}) copy-start(bf16[1024,8,72]{0,2,1:T(8,128)(2,1)} %get-tuple-element.408) | copy-start | bytes 3538948 | tf_op jit(solution)/shard_map/while/body/eval_jaxpr/while
  371.5 10.2 %copy-start.12 = (bf16[2,512,8,72]{1,3,2,0:T(8,128)(2,1)S(1)}, bf16[2,512,8,72]{1,3,2,0:T(8,128)(2,1)}, u32[]{:S(2)}) copy-start(bf16[2,512,8,72]{1,3,2,0:T(8,128)(2,1)} %get-tuple-element.394) | copy-start | bytes 3538948 | tf_op jit(solution)/shard_map/while/body/eval_jaxpr/while
  387.8 4.2 copy-start.3
  392.5 9.5 %copy-start.27 = (bf16[72,8,2,512]{3,1,2,0:T(8,128)(2,1)}, bf16[72,8,2,512]{3,1,2,0:T(8,128)(2,1)S(1)}, u32[]{:S(2)}) copy-start(bf16[72,8,2,512]{3,1,2,0:T(8,128)(2,1)S(1)} %copy.76) | copy-start | bytes 3538948
  396.1 5.9 copy-start.75
  418.5 168.4 %copy-start.28 = (bf16[72,8,2,512]{3,1,2,0:T(8,128)(2,1)S(1)}, bf16[72,8,2,512]{3,1,2,0:T(8,128)(2,1)}, u32[]{:S(2)}) copy-start(bf16[72,8,2,512]{3,1,2,0:T(8,128)(2,1)} %copy-done.27) | copy-start | bytes 3538948
  418.5 168.4 %copy-start.74 = (bf16[2,1152,864]{2,1,0:T(8,128)(2,1)S(1)}, bf16[2,1152,864]{2,1,0:T(8,128)(2,1)}, u32[]{:S(2)}) copy-start(bf16[2,1152,864]{2,1,0:T(8,128)(2,1)} %get-tuple-element.148) | copy-start | bytes 11943940
  585.8 12.0 %collective-permute-start.6 = (f32[72,864]{1,0:T(8,128)}, f32[72,864]{1,0:T(8,128)}, u32[]{:S(2)}, u32[]{:S(2)}) collective-permute-start(f32[72,864]{1,0:T(8,128)} %get-tuple-element.296), channel_id=1, source_target_pairs={{0,2},{2,0},{1,3},{3,1},{4,6},{6,4},{5,7},{7,5},{8,10},{10,8},{9,1... | collective-permute-start | bytes 746504 | tf_op jit(solution)/shard_map/ppermute | solution.py:1500
  592.9 4.1 copy-start.57
  592.9 4.1 copy-start.17
  594.0 8.3 %collective-permute-start.4 = (bf16[512,1152]{1,0:T(8,128)(2,1)}, bf16[512,1152]{1,0:T(8,128)(2,1)}, u32[]{:S(2)}, u32[]{:S(2)}) collective-permute-start(bf16[512,1152]{1,0:T(8,128)(2,1)} %dynamic-slice_convert_fusion), channel_id=1, source_target_pairs={{0,2},{2,0},{1,3},{3,1},{4,6},{6,4},{5,7},{7,5},{8,10},{10,8},{9,1... | collective-permute-start | bytes 3538952 | tf_op jit(solution)/shard_map/ppermute | solution.py:1500
  595.2 4.8 collective-permute-start.7
  596.9 5.5 copy-start.9
  596.9 5.5 copy-start.48
  596.9 5.4 copy-start.55
  596.9 5.4 copy-start.65
  605.9 24.9 %copy-start.67 = (f32[16,128]{1,0:T(8,128)S(1)}, f32[16,128]{1,0:T(8,128)}, u32[]{:S(2)}) copy-start(f32[16,128]{1,0:T(8,128)} %get-tuple-element.151) | copy-start | bytes 24580
  628.0 21.5 %copy-start.46 = (f32[72,128]{1,0:T(8,128)S(1)}, f32[72,128]{1,0:T(8,128)}, u32[]{:S(2)}) copy-start(f32[72,128]{1,0:T(8,128)} %get-tuple-element.163) | copy-start | bytes 110596
  653.5 9.9 %copy-start.43 = (f32[16128]{0:T(1024)S(1)}, f32[16128]{0:T(1024)}, u32[]{:S(2)}) copy-start(f32[16128]{0:T(1024)} %param.51) | copy-start | bytes 193540
  653.5 9.9 %copy-start.49 = (f32[16128]{0:T(1024)S(1)}, f32[16128]{0:T(1024)}, u32[]{:S(2)}) copy-start(f32[16128]{0:T(1024)} %param.53) | copy-start | bytes 193540
  653.5 9.9 %copy-start.50 = (f32[16128]{0:T(1024)S(1)}, f32[16128]{0:T(1024)}, u32[]{:S(2)}) copy-start(f32[16128]{0:T(1024)} %param.52) | copy-start | bytes 193540
  657.0 20.4 %collective-permute-start.5 = (bf16[512,1152]{1,0:T(8,128)(2,1)}, bf16[512,1152]{1,0:T(8,128)(2,1)S(1)}, u32[]{:S(2)}, u32[]{:S(2)}) collective-permute-start(bf16[512,1152]{1,0:T(8,128)(2,1)} %get-tuple-element.288), channel_id=1, source_target_pairs={{0,0},{1,2},{2,1},{3,3},{4,4},{5,6},{6,5},{7,7},{8,8},{9,10},{10,9... | collective-permute-start | bytes 3538952 | tf_op jit(solution)/shard_map/ppermute | solution.py:1496
  664.2 3.7 copy-start.21
  664.2 3.7 copy-start.22
  664.2 3.7 copy-start.40
  664.2 3.7 copy-start.41
  (49 other events, 115.9 us)

commit v3 on v2

--- a/solution.py
+++ b/solution.py
@@ -760,15 +760,15 @@
     (tok, cot, bucket_in, table, att_m, proj_m, exp_m, red_m, mod_w, cond_in, bias_in) = refs[:11]
     gq, gp, gu, gd = full = refs[11:15]
     (mod_out, lhs, x0_out, dy_out, cl_out, h1_out, q_out, k_out, v_out) = refs[15:24]
-    (attnt_out, lse_out, ba_out, x1_out, h2_out, act_out, der_out, bb_out, y_out, gred_out) = refs[24:34]
-    (oq, op, ou, od, fq, tq, fu, tu) = refs[34:42]
-    mod_bufs = refs[42:49]
-    (xs, x0, dy, bucket, closing, h1, qa, ka, vt, attnt, attn) = refs[49:60]
-    (ps, pr, ds, dr, acc, x1, h2, act, der, ba, bb, yo, gstage) = refs[60:73]
-    (b_all, b_q, b_v, b_u) = refs[73:77]
-    lsem = refs[77]
-    gather_sems = refs[78:88]
-    ms, mr, ws, wr, ts, tr, os, outs_sem, gsem = refs[88:97]
+    (attnt_out, lse_out, ba_out, x1_out, h2_out, der_out, bb_out, y_out, gred_out) = refs[24:33]
+    (oq, op, ou, od, fq, tq, fu, tu) = refs[33:41]
+    mod_bufs = refs[41:48]
+    (xs, x0, dy, bucket, closing, h1, qa, ka, vt, attnt, attn) = refs[48:59]
+    (ps, pr, ds, dr, acc, x1, h2, act, der, ba, bb, yo, gstage) = refs[59:72]
+    (b_all, b_q, b_v, b_u) = refs[72:76]
+    lsem = refs[76]
+    gather_sems = refs[77:87]
+    ms, mr, ws, wr, ts, tr, os, outs_sem, gsem = refs[87:96]
     z, x, c, y = place()
     xn, yn, twin, zn = partners()
     half = x0.shape[0]
@@ -1105,7 +1105,6 @@
             tick(1)
 
     pl.run_scoped(up, VM((2, D, D), BF))
-    put(act, act_out)
     put(der, der_out)
 
     gouts = []
@@ -1204,7 +1203,6 @@
     out((half, D), BF)
     out((half, D), F32)
     out((rows, D), BF)
-    out((rows, 2304), BF)
     out((rows, 2304), BF)
     out((half, D), BF)
     out((half, D), BF)
@@ -1284,292 +1282,645 @@
     )(tokens, cotangent, bucket, table, *masters, modulate_master, cond, biases)
 
 
-OLD_PIECES = {"q": (144, 864, 96), "p": (72, 576, None), "u": (144, 1152, 96), "d": (288, 576, 192)}
-
-
-def old_parts(rows, cut, k):
-    if cut is None:
-        return ((0, rows), None) if k % 2 == 0 else (None, (0, rows))
-    return (0, cut), (cut, rows - cut)
-
-
-def scatter_kernel(*refs):
-    grads, outs = refs[0:4], refs[4:8]
-    held, diag, by_x, by_y, by_z = (refs[8 + 4 * i : 12 + 4 * i] for i in range(5))
-    lsem, fs, fr, xs, xr, ys, yr, zs, zr = refs[28:]
+class Scatter:
+    def __init__(self, grads, boxes, outs, sems):
+        self.grads, self.outs = grads, outs
+        self.pair_box, self.diag_box, self.x_box, self.y_box, self.z_box = boxes
+        self.ps, self.pr, self.fs, self.fr, self.xs, self.xr, self.ys, self.yr, self.zs, self.zr = sems
+        self.sent = []
+
+    def piece(self, i, flip_y, k, flip_x):
+        z, x, c, y = place()
+        weight, first, count, _ = CHUNKS[i]
+        return piece_at(
+            self.grads[weight], weight, 1 - y if flip_y else y, at_z(k), 1 - x if flip_x else x, first, count
+        )
+
+    def box(self, boxes, i, n):
+        weight, first, count, _ = CHUNKS[i]
+        return boxes[weight].at[n, pl.ds(first, count)]
+
+    def send(self, make):
+        make().start()
+        self.sent.append(make)
+
+    def arrived(self, ref, s, r):
+        rdma(ref, ref, s, r, partners()[0]).wait_recv()
+
+    def add(self, target, *others):
+        rows = target.shape[0]
+        step = 16 if rows % 16 == 0 else rows
+
+        def some(n, _):
+            at = pl.ds(pl.multiple_of(n * step, step), step) if rows != step else slice(None)
+            total = target[at, :].astype(F32)
+            for o in others:
+                total = total + o[at, :].astype(F32)
+            target[at, :] = total.astype(BF)
+            return 0
+
+        if rows == step:
+            some(0, 0)
+        else:
+            lax.fori_loop(0, rows // step, some, 0)
+
+    def across(self, i, k, by_y):
+        if by_y:
+            return rdma(
+                self.piece(i, 1, k, 0), self.box(self.y_box, i, k), self.ys.at[i, k], self.yr.at[i, k], partners()[1]
+            )
+        return rdma(
+            self.piece(i, 0, k, 1), self.box(self.x_box, i, k), self.xs.at[i, k], self.xr.at[i, k], partners()[0]
+        )
+
+    def start(self, i):
+        def to_pair(k):
+            return rdma(
+                self.piece(i, 1, k ^ 1, 1),
+                self.box(self.pair_box, i, k // 2),
+                self.ps.at[i, k],
+                self.pr.at[i, k],
+                partners()[3][1],
+            )
+
+        for k in (0, 2):
+            self.send(functools.partial(to_pair, k))
+        for k in (1, 3):
+            for by_y in (0, 1):
+                self.send(functools.partial(self.across, i, k, by_y))
+
+    def corner(self, i, k):
+        box = self.box(self.pair_box, i, k // 2)
+        self.arrived(box, self.ps.at[i, k], self.pr.at[i, k])
+        self.add(self.piece(i, 1, k, 1), box)
+        spans = parts_of(i, k)
+
+        def part(n):
+            return rdma(
+                self.piece(i, 1, k, 1).at[pl.ds(*spans[n])],
+                self.box(self.diag_box, i, k // 2).at[pl.ds(*spans[n])],
+                self.fs.at[i, k, n],
+                self.fr.at[i, k, n],
+                partners()[1 - n],
+            )
+
+        for n in (0, 1):
+            if spans[n] is not None:
+                self.send(functools.partial(part, n))
+
+    def plane(self, i, k):
+        spans = parts_of(i, k)
+        for n in (0, 1):
+            if spans[n] is not None:
+                part = self.box(self.diag_box, i, k // 2).at[pl.ds(*spans[n])]
+                self.arrived(part, self.fs.at[i, k, n], self.fr.at[i, k, n])
+                self.add(self.piece(i, n, k, 1 - n).at[pl.ds(*spans[n])], part)
+            self.send(functools.partial(self.across, i, k, n))
+
+    def both(self, i, k):
+        boxes = []
+        for boxes_of, s, r in ((self.x_box, self.xs, self.xr), (self.y_box, self.ys, self.yr)):
+            box = self.box(boxes_of, i, k)
+            self.arrived(box, s.at[i, k], r.at[i, k])
+            boxes.append(box)
+        return boxes
+
+    def column(self, i, k):
+        self.add(self.piece(i, 0, k, 0), *self.both(i, k))
+
+        def along():
+            return rdma(
+                self.piece(i, 0, k, 0),
+                self.box(self.z_box, i, k - 1),
+                self.zs.at[i, k],
+                self.zr.at[i, k],
+                partners()[3][k],
+            )
+
+        self.send(along)
+
+    def last(self, i):
+        weight, first, count, _ = CHUNKS[i]
+        boxes = self.both(i, 0)
+        for k in (1, 2, 3):
+            box = self.box(self.z_box, i, k - 1)
+            self.arrived(box, self.zs.at[i, k], self.zr.at[i, k])
+            boxes.append(box)
+        total = self.piece(i, 0, 0, 0)[...].astype(F32)
+        for box in boxes:
+            total = total + box[...].astype(F32)
+        self.outs[weight][first : first + count, :] = total
+
+    def finish(self):
+        for make in self.sent:
+            make().wait_send()
+
+    def steps(self, i):
+        return (
+            [(self.start, i), (self.corner, i, 0), (self.corner, i, 2)],
+            [(self.plane, i, 0), (self.plane, i, 2), (self.column, i, 1)],
+            [(self.column, i, 3), (self.column, i, 2)],
+            [(self.last, i)],
+        )
+
+
+def total_steps(dm, bs, lhs, mods, bufs, gmod, bias_out, s, r):
+    dmt, got_m, got_b, sb, got_z, near = bufs
+
+    def hop(i):
+        z, x, c, y = place()
+        xn, yn, twin, zn = partners()
+        if i == 0:
+            pairs = [(dm, got_m, twin), (bs, got_b.at[0], twin)]
+        elif i == 1:
+            pairs = [(dmt.at[1 - y], mods.at[z, x, y], yn), (sb.at[0], got_b.at[1], yn)]
+        elif i == 2:
+            pairs = [(mods.at[z, x], mods.at[z, x], xn), (sb.at[1], got_b.at[2], xn)]
+        elif i == 3:
+            pairs = [(mods.at[z], mods.at[z], zn[k]) for k in (1, 2, 3)]
+            pairs += [(sb.at[2], got_z.at[k - 1], zn[k]) for k in (1, 2, 3)]
+        else:
+            pairs = [(near.at[0], near.at[1], yn)]
+        return [
+            rdma(src, dst, s.at[i, n], r.at[i, n], to) for n, (src, dst, to) in enumerate(pairs)
+        ]
+
+    def step(i):
+        z, x, c, y = place()
+        if i > 0:
+            for d in hop(i - 1):
+                d.wait()
+        if i == 1:
+            dmt[...] = rounded(dm[...] + got_m[...])
+            mods[z, x, y] = dmt[y]
+            sb[0] = bs[...] + got_b[0]
+        elif i == 2:
+            sb[1] = sb[0] + got_b[1]
+        elif i == 3:
+            sb[2] = sb[1] + got_b[2]
+        elif i == 4:
+            rows = [mods[n // 4, n // 2 % 2, n % 2] for n in range(16)]
+            total = rows[0]
+            for row in rows[1:]:
+                total = total + row
+            near[0] = total
+            bias_out[:, 6 * D :] = (sb[2] + got_z[0]) + (got_z[1] + got_z[2])
+            left = lhs[:, :72].astype(BF)
+            right = jnp.concatenate(rows, axis=0).astype(BF)
+            for j in range(3):
+                cols = slice(j * D, (j + 1) * D)
+                gmod[:, cols] = matmul_tn(left, right[:, cols])
+        elif i == 5:
+            for n in (0, 1):
+                bias_out[:, n * 3456 : (n + 1) * 3456] = jnp.where(y == n, near[0], near[1])
+        if i < 5:
+            for d in hop(i):
+                d.start()
+
+    return [functools.partial(step, i) for i in range(6)]
+
+
+def backward_kernel(*refs):
+    gq, gp, gu, gd, mod, lhs = refs[:6]
+    (x0_in, dy_in, cl_in, h1_in, q_in, k_in, v_in, at_in, lse) = refs[6:15]
+    (ba_in, x1_in, h2_in, der_in, bb_in, y_in, gred) = refs[15:22]
+    (out, ig_out, s_att, s_proj, s_exp, s_red, gmod, bias_out, norm_out) = refs[22:31]
+    grads = refs[31:35]
+    boxes = [refs[35 + 4 * i : 39 + 4 * i] for i in range(5)]
+    fq, fu, gotq, gotu = refs[55:59]
+    dba, dx1, ps, pr, dm, bs, mods = refs[59:66]
+    total_bufs = refs[66:72]
+    sq = refs[72]
+    lsem = refs[73]
+    scatter_sems = refs[74:84]
+    ts, tr, ws, wr, hs, hr, ns, nr = refs[84:92]
     z, x, c, y = place()
-    xn, yn = (z, 1 - x, c, y), (z, x, c, 1 - y)
-    zn = [None] + [(at_z(k), x, c, y) for k in (1, 2, 3)]
-    f32 = jnp.float32
-    for w in range(4):
-        pltpu.make_async_copy(grads[w], held[w], lsem.at[w]).start()
-    greet([xn, yn] + zn[1:])
-    pending = []
-    order = (3, 2, 1, 0)
-
-    def z_of(k):
-        return z if k == 0 else at_z(k)
-
-    for w in range(4):
-        rows, _, cut = OLD_PIECES[NAMES[w]]
-        pltpu.make_async_copy(grads[w], held[w], lsem.at[w]).wait()
-        for k in order:
-            spans = old_parts(rows, cut, k)
-            for i, (span, to) in enumerate(zip(spans, (yn, xn))):
-                if span is not None:
-                    d = rdma(
-                        held[w].at[1 - y, z_of(k), 1 - x, pl.ds(*span)],
-                        diag[w].at[k, pl.ds(*span)],
-                        fs.at[w, k, i],
-                        fr.at[w, k, i],
-                        to,
-                    )
-                    d.start()
-                    pending.append(d)
-    for w in range(4):
-        rows, _, cut = OLD_PIECES[NAMES[w]]
-        for k in order:
-            spans = old_parts(rows, cut, k)
-            for i, span in enumerate(spans):
-                piece = held[w].at[(y, z_of(k), 1 - x) if i == 0 else (1 - y, z_of(k), x)]
-                if span is not None:
-                    part = diag[w].at[k, pl.ds(*span)]
-                    rdma(part, part, fs.at[w, k, i], fr.at[w, k, i], xn).wait_recv()
-                    target = piece.at[pl.ds(*span)]
-                    target[...] = (target[...].astype(f32) + part[...].astype(f32)).astype(
-                        jnp.bfloat16
-                    )
-                box, to, s, r = ((by_x, xn, xs, xr), (by_y, yn, ys, yr))[i]
-                d = rdma(piece, box[w].at[k], s.at[w, k], r.at[w, k], to)
-                d.start()
-                pending.append(d)
-    for w in range(4):
-        for k in order:
-            for box, s, r in ((by_x, xs, xr), (by_y, ys, yr)):
-                part = box[w].at[k]
-                rdma(part, part, s.at[w, k], r.at[w, k], xn).wait_recv()
-            piece = held[w].at[y, z_of(k), x]
-            total = piece[...].astype(f32) + by_x[w][k].astype(f32) + by_y[w][k].astype(f32)
-            if k == 0:
-                outs[w][...] = total
-            else:
-                piece[...] = total.astype(jnp.bfloat16)
-                d = rdma(piece, by_z[w].at[k - 1], zs.at[w, k - 1], zr.at[w, k - 1], zn[k])
-                d.start()
-                pending.append(d)
-    for w in range(4):
-        total = outs[w][...]
-        for k in (1, 2, 3):
-            part = by_z[w].at[k - 1]
-            rdma(part, part, zs.at[w, k - 1], zr.at[w, k - 1], zn[k]).wait_recv()
-            total = total + part[...].astype(f32)
-        outs[w][...] = total
-    for d in pending:
-        d.wait_send()
-
-
-def scatter_grads(grads):
-    dma = pltpu.SemaphoreType.DMA
-    shapes = [OLD_PIECES[n][:2] for n in NAMES]
-
-    def boxes(*lead):
-        return [pltpu.VMEM(lead + s, jnp.bfloat16) for s in shapes]
-
-    return pl.pallas_call(
-        scatter_kernel,
-        out_shape=[jax.ShapeDtypeStruct(s, jnp.float32) for s in shapes],
-        in_specs=[pl.BlockSpec(memory_space=pl.ANY)] * 4,
-        out_specs=[pl.BlockSpec(memory_space=pltpu.VMEM)] * 4,
-        scratch_shapes=boxes(2, 4, 2)
-        + boxes(4)
-        + boxes(4)
-        + boxes(4)
-        + boxes(3)
-        + [dma((4,))]
-        + [dma((4, 4, 2))] * 2
-        + [dma((4, 4))] * 6,
-        compiler_params=pltpu.CompilerParams(
-            collective_id=1, has_side_effects=True, vmem_limit_bytes=56 * 2**20
-        ),
-        name="scatter_grads",
-    )(*grads)
-
-
-def totals_kernel(mod_ref, bias_ref, mods, sums, got_m, got_b, got_z, s, r):
-    z, x, c, y = place()
-    xn, yn, twin = (z, 1 - x, c, y), (z, x, c, 1 - y), (z, x, 1 - c, y)
-    zn = [None] + [(at_z(k), x, c, y) for k in (1, 2, 3)]
-    greet([xn, yn, twin] + zn[1:])
-    d = rdma(mod_ref, got_m, s.at[0], r.at[0], twin)
-    e = rdma(bias_ref, got_b.at[0], s.at[1], r.at[1], twin)
-    d.start()
-    e.start()
-    d.wait()
-    e.wait()
-    mods[z, x, y] = (mod_ref[...] + got_m[...]).astype(jnp.bfloat16)
-    sums[...] = bias_ref[...] + got_b[0]
-    d = rdma(mods.at[z, x, y], mods.at[z, x, y], s.at[2], r.at[2], yn)
-    e = rdma(sums, got_b.at[1], s.at[3], r.at[3], yn)
-    d.start()
-    e.start()
-    d.wait()
-    e.wait()
-    sums[...] = sums[...] + got_b[1]
-    d = rdma(mods.at[z, x], mods.at[z, x], s.at[4], r.at[4], xn)
-    e = rdma(sums, got_b.at[2], s.at[5], r.at[5], xn)
-    d.start()
-    e.start()
-    d.wait()
-    e.wait()
-    got_z[0] = sums[...] + got_b[2]
-    ds = [rdma(mods.at[z], mods.at[z], s.at[5 + k], r.at[5 + k], zn[k]) for k in (1, 2, 3)]
-    ds += [rdma(got_z.at[0], got_z.at[k], s.at[8 + k], r.at[8 + k], zn[k]) for k in (1, 2, 3)]
-    for d in ds:
+    xn, yn, twin, zn = partners()
+    half = dx1.shape[0]
+    mine = pl.multiple_of(c * half, half)
+    other = pl.multiple_of((1 - c) * half, half)
+    scatter = Scatter(grads, boxes, (fq, s_proj, fu, s_red), scatter_sems)
+    hops = total_steps(dm, bs, lhs, mods, total_bufs, gmod, bias_out, hs, hr)
+    pltpu.make_async_copy(gred, grads[3], lsem.at[0]).start()
+    greet([xn, yn, twin] + zn[1:], swapped=True)
+    dm[...] = jnp.zeros_like(dm)
+    bs[...] = jnp.zeros_like(bs)
+    TILE, WIDE = 128, 256
+    swap_to = (z, x, y, c)
+
+    def vec(i):
+        return mod[i // 3, :, (i % 3) * D : (i % 3 + 1) * D]
+
+    def add_mod(i, value):
+        cols = slice((i % 3) * D, (i % 3 + 1) * D)
+        dm[i // 3, :, cols] = dm[i // 3, :, cols] + jnp.sum(value, axis=0, keepdims=True)
+
+    def add_bias(at, value):
+        cols = slice(at, at + value.shape[1])
+        bs[:, cols] = bs[:, cols] + value
+
+    def load(src, dst, i):
+        d = pltpu.make_async_copy(src, dst, lsem.at[i])
         d.start()
-    for d in ds:
-        d.wait()
-    sums[...] = (got_z[0] + got_z[1]) + (got_z[2] + got_z[3])
-
-
-def share_totals(mod_grad, bias_grad):
-    f32, vm = jnp.float32, pltpu.VMEM
-    return pl.pallas_call(
-        totals_kernel,
-        out_shape=[
-            jax.ShapeDtypeStruct((4, 2, 2, 16, 432), jnp.bfloat16),
-            jax.ShapeDtypeStruct((72, 128), f32),
-        ],
-        in_specs=[pl.BlockSpec(memory_space=vm)] * 2,
-        out_specs=[pl.BlockSpec(memory_space=vm)] * 2,
-        scratch_shapes=[
-            vm((16, 432), f32),
-            vm((3, 72, 128), f32),
-            vm((4, 72, 128), f32),
-            pltpu.SemaphoreType.DMA((12,)),
-            pltpu.SemaphoreType.DMA((12,)),
-        ],
-        compiler_params=pltpu.CompilerParams(collective_id=3, has_side_effects=True),
-        name="share_totals",
-    )(mod_grad, bias_grad)
-
-
-def norm_kernel(in_ref, out_ref, box, got_z, s, r):
-    z, x, c, y = place()
-    xn, yn, twin = (z, 1 - x, c, y), (z, x, c, 1 - y), (z, x, 1 - c, y)
-    zn = [None] + [(at_z(k), x, c, y) for k in (1, 2, 3)]
-    greet([xn, yn, twin] + zn[1:])
-    total = in_ref[...]
+        return d
+
+    queue = []
+
+    def tick(n):
+        for _ in range(min(n, len(queue))):
+            f, *a = queue.pop(0)
+            f(*a)
+
+    def moves(i):
+        if i == 0:
+            return y_in, out
+        rows = pl.ds((i - 1) * TILE, TILE)
+        return dba.at[rows], ig_out.at[rows]
+
+    def move(i):
+        @pl.when(c != y)
+        def _():
+            rdma(*moves(i), ws.at[i], wr.at[i], swap_to).start()
+
+        @pl.when(c == y)
+        def _():
+            pltpu.make_async_copy(*moves(i), ws.at[i]).start()
+
+    def moved(i):
+        @pl.when(c != y)
+        def _():
+            rdma(*moves(i), ws.at[i], wr.at[i], swap_to).wait()
+
+        @pl.when(c == y)
+        def _():
+            pltpu.make_async_copy(*moves(i), ws.at[i]).wait()
+
+    load_d = pltpu.make_async_copy(gred, grads[3], lsem.at[0])
+    load_d.wait()
+    scatter.start(5)
+    scatter.start(6)
+    five, six = scatter.steps(5), scatter.steps(6)
+    queue += five[0][1:] + six[0][1:] + five[1] + six[1] + five[2] + six[2] + five[3] + six[3]
+
+    def own_tile(ref, t):
+        return ref.at[pl.ds(pl.multiple_of(mine + t * TILE, TILE), TILE)]
+
+    def widen(du):
+        def through(weight, closing, der):
+            loads = [load(gd, weight, 1), load(cl_in, closing, 2)]
+            ders = [load(der_in.at[pl.ds(0, TILE)], der.at[0], 3)]
+            for d in loads:
+                d.wait()
+            sums = jnp.zeros((1, 2304), F32)
+            for n in range(8):
+                rows = slice(n * TILE, (n + 1) * TILE)
+                if n < 7:
+                    ders.append(load(der_in.at[pl.ds((n + 1) * TILE, TILE)], der.at[(n + 1) % 2], 3 + (n + 1) % 2))
+                left = closing[rows, :]
+                value = matmul_nt(left[:, :576], weight[0]) + matmul_nt(left[:, 576:], weight[1])
+                ders[n].wait()
+                value = (value * der[n % 2].astype(F32)).astype(BF)
+                du[rows, :] = value
+                sums = sums + jnp.sum(value.astype(F32), axis=0, keepdims=True)
+                tick(1)
+            for j in range(8):
+                block = sums[:, j * BLOCK : (j + 1) * BLOCK]
+                for p in (0, 1):
+                    add_bias(3 * D + (2 * j + p) * BLOCK, jnp.where(c == p, block, 0.0))
+
+        pl.run_scoped(through, VM((2, 2304, 576), BF), VM((2 * half, D), BF), VM((2, TILE, 2304), BF))
+
+        def expand_grad(h2):
+            load(h2_in, h2, 2).wait()
+            for t in range(3):
+                left = h2[:, t * 384 : (t + 1) * 384]
+                for i in (0, 1):
+                    grads[2][i, t * 384 : (t + 1) * 384, :] = matmul_tn(
+                        left, du[:, i * D : (i + 1) * D]
+                    ).astype(BF)
+                    tick(1)
+
+        pl.run_scoped(expand_grad, VM((2 * half, D), BF))
+        scatter.start(3)
+        scatter.start(4)
+        three, four = scatter.steps(3), scatter.steps(4)
+        queue.extend(three[0][1:] + four[0][1:] + three[1] + four[1] + three[2] + four[2] + three[3] + four[3])
+        move(0)
+
+        def back(weight):
+            load(gu, weight, 1).wait()
+
+            def product(start):
+                left = du[pl.ds(start, WIDE), :]
+                return matmul_nt(left[:, :D], weight[0]) + matmul_nt(left[:, D:], weight[1])
+
+            for t in range(half // WIDE):
+                rows = pl.ds(t * WIDE, WIDE)
+                ps[rows, :] = product(pl.multiple_of(other + t * WIDE, WIDE)).astype(BF)
+                rdma(ps.at[rows], pr.at[rows], ts.at[0, t], tr.at[0, t], twin).start()
+                tick(1)
+            for t in range(half // WIDE):
+                dx1[pl.ds(t * WIDE, WIDE), :] = product(pl.multiple_of(mine + t * WIDE, WIDE))
+                tick(1)
+
+        pl.run_scoped(back, VM((2, D, D), BF))
+
+    pl.run_scoped(widen, VM((2 * half, 2304), BF))
+
+    def half_got(i, t):
+        rows = pl.ds(t * WIDE, WIDE)
+        rdma(ps.at[rows], pr.at[rows], ts.at[i, t], tr.at[i, t], twin).wait()
+
+    def norm_back(value, scaling, gradient):
+        average = jnp.mean(value, axis=-1, keepdims=True)
+        centred = value - average
+        inverse = lax.rsqrt(jnp.mean(centred * centred, axis=-1, keepdims=True) + 1e-06)
+        normed = centred * inverse
+        inner = gradient * (1.0 + scaling)
+        part = inner - jnp.mean(inner, axis=-1, keepdims=True)
+        part = part - normed * jnp.mean(inner * normed, axis=-1, keepdims=True)
+        return part * inverse, normed
+
+    def middle(x1, dy, ba, bb):
+        loads = [load(x1_in, x1, 1), load(dy_in, dy, 2), load(ba_in, ba, 3), load(bb_in, bb, 4)]
+        for d in loads:
+            d.wait()
+        for t in range(half // TILE):
+            if t % 2 == 0:
+                half_got(0, t // 2)
+            rows = slice(t * TILE, (t + 1) * TILE)
+            gradient = dx1[rows, :] + pr[rows, :].astype(F32)
+            part, normed = norm_back(x1[rows, :], vec(4), gradient)
+            add_mod(3, gradient)
+            add_mod(4, gradient * normed)
+            outer = dy[rows, :].astype(F32)
+            add_mod(5, outer * bb[rows, :].astype(F32))
+            add_bias(9216 - D, jnp.sum(rounded(outer * vec(5)), axis=0, keepdims=True))
+            total = outer + part
+            dx1[rows, :] = total
+            add_mod(2, total * ba[rows, :].astype(F32))
+            branch = (total * vec(2)).astype(BF)
+            own_tile(dba, t)[...] = branch
+            tile = own_tile(dba, t)
+            rdma(tile, tile, ts.at[1, t], tr.at[1, t], twin).start()
+            add_bias(2 * D, jnp.sum(branch.astype(F32), axis=0, keepdims=True))
+            tick(1)
+
+    pl.run_scoped(middle, VM((half, D), F32), VM((half, D), BF), VM((half, D), BF), VM((half, D), BF))
+
+    def attention(dot, dqkv):
+        def project(weight, stage, raw, attnt, attn):
+            loads = [load(gp, raw, 1), load(at_in, attnt, 2)]
+            for d in loads:
+                d.wait()
+            for i in (0, 1):
+                for h in range(8):
+                    stage[h * 72 : h * 72 + 72, :] = raw[i, h].astype(F32)
+                weight[i] = stage[...].astype(BF)
+            attn[...] = jnp.concatenate([attnt[h] for h in range(8)], axis=0).astype(BF)
+            for t in range(half // TILE):
+                tile = own_tile(dba, t)
+                rdma(tile, tile, ts.at[1, t], tr.at[1, t], twin).wait_send()
+                part = dba.at[pl.ds(pl.multiple_of(other + t * TILE, TILE), TILE)]
+                rdma(part, part, ts.at[1, t], tr.at[1, t], twin).wait_recv()
+            for n in range(4):
+                rows = slice(n * WIDE, (n + 1) * WIDE)
+                right = dba[rows, :]
+                value = matmul_nt(weight[0], right[:, :576]) + matmul_nt(weight[1], right[:, 576:])
+                for h in range(8):
+                    dot[h, :, rows] = value[h * 72 : h * 72 + 72, :].astype(BF)
+                tick(1)
+            for i in (0, 1):
+                stage[...] = matmul(attn[...], dba[:, i * 576 : (i + 1) * 576])
+                for h in range(8):
+                    grads[1][i, h] = stage[h * 72 : h * 72 + 72, :].astype(BF)
+
+        pl.run_scoped(
+            project,
+            VM((2, 576, 576), BF),
+            VM((576, 576), F32),
+            VM((2, 8, 72, 576), BF),
+            VM((8, 72, 2 * half), F32),
+            VM((576, 2 * half), BF),
+        )
+        scatter.start(2)
+        two = scatter.steps(2)
+        queue.extend(two[0][1:] + two[1] + two[2] + two[3])
+
+        def heads(qa, ka, vt, at, dk, dv, dq):
+            def fetch(h):
+                n = h % 2
+                return [
+                    load(src.at[h], dst.at[n], 1 + 4 * n + m)
+                    for m, (src, dst) in enumerate(((q_in, qa), (k_in, ka), (v_in, vt), (at_in, at)))
+                ]
+
+            coming = fetch(0)
+            for h in range(8):
+                n = h % 2
+                for d in coming:
+                    d.wait()
+                if h < 7:
+                    coming = fetch(h + 1)
+                value = vt[n].T
+                key_t = ka[n, :, :72].T
+                inner = jnp.sum(at[n] * dot[h].astype(F32), axis=0, keepdims=True)
+                dk[...] = jnp.zeros_like(dk)
+                dv[...] = jnp.zeros_like(dv)
+                for i in range(4):
+                    rows = slice(i * 256, (i + 1) * 256)
+                    query = qa[n, rows, :]
+                    grad = dot[h, :, rows]
+                    scores = matmul_nt(ka[n], query)
+                    prob = jnp.exp2(scores * ALPHA - lse[h, :, rows])
+                    change = matmul(value, grad) - inner[:, rows]
+                    dscore = (prob * change).astype(BF)
+                    dv[...] += matmul_nt(grad, prob.astype(BF))
+                    dk[...] += matmul_nt(query[:, :72].T, dscore)
+                    dq[:, rows] = matmul(key_t, dscore)
+                    if i % 2 == 1:
+                        tick(1)
+                scale = HEAD_DIM ** (-0.5)
+                dqkv[0, :, h * 72 : h * 72 + 72] = (dq[...] * scale).T.astype(BF)
+                key_grad = (dk[...] * scale).T.astype(BF)
+                if h < 4:
+                    dqkv[0, :, 576 + h * 72 : 648 + h * 72] = key_grad
+                else:
+                    dqkv[1, :, h * 72 - 288 : h * 72 - 216] = key_grad
+                dqkv[1, :, 288 + h * 72 : 360 + h * 72] = dv[...].T.astype(BF)
+
+        pl.run_scoped(
+            heads,
+            VM((2, 2 * half, 128), BF),
+            VM((2, 2 * half, 128), BF),
+            VM((2, 72, 2 * half), BF),
+            VM((2, 72, 2 * half), F32),
+            VM((72, 2 * half), F32),
+            VM((72, 2 * half), F32),
+            VM((72, 2 * half), F32),
+        )
+
+        def attend_grad(h1):
+            load(h1_in, h1, 1).wait()
+            for t in range(3):
+                left = h1[:, t * 384 : (t + 1) * 384]
+                for i in (0, 1):
+                    grads[0][i, t * 384 : (t + 1) * 384, :] = matmul_tn(left, dqkv[i]).astype(BF)
+                    tick(1)
+
+        pl.run_scoped(attend_grad, VM((2 * half, D), BF))
+        scatter.start(0)
+        scatter.start(1)
+        zero, one = scatter.steps(0), scatter.steps(1)
+        queue.extend(zero[0][1:] + one[0][1:] + zero[1] + one[1] + zero[2] + one[2] + zero[3] + one[3])
+
+        def back(weight, x0):
+            loads = [load(gq, weight, 1), load(x0_in, x0, 2)]
+            for d in loads:
+                d.wait()
+
+            def product(start):
+                rows = pl.ds(start, WIDE)
+                return matmul_nt(dqkv[0, rows, :], weight[0]) + matmul_nt(dqkv[1, rows, :], weight[1])
+
+            for t in range(half // WIDE):
+                rows = pl.ds(t * WIDE, WIDE)
+                ps[rows, :] = product(pl.multiple_of(other + t * WIDE, WIDE)).astype(BF)
+                rdma(ps.at[rows], pr.at[rows], ts.at[2, t], tr.at[2, t], twin).start()
+                tick(1)
+            for t in range(half // WIDE):
+                value = product(pl.multiple_of(mine + t * WIDE, WIDE))
+                half_got(2, t)
+                tick(1)
+                for n in range(WIDE // TILE):
+                    rows = slice(t * WIDE + n * TILE, t * WIDE + (n + 1) * TILE)
+                    gradient = value[n * TILE : (n + 1) * TILE, :] + pr[rows, :].astype(F32)
+                    part, normed = norm_back(x0[rows, :].astype(F32), vec(1), gradient)
+                    add_mod(0, gradient)
+                    add_mod(1, gradient * normed)
+                    dba[rows, :] = (dx1[rows, :] + part).astype(BF)
+                    move(1 + t * (WIDE // TILE) + n)
+
+        pl.run_scoped(back, VM((2, D, 864), BF), VM((half, D), BF))
+        for i in (0, 1):
+            sums = jnp.sum(dqkv[i].astype(F32), axis=0, keepdims=True)
+            for j in range(8):
+                block = sums[:, i * 288 + j * 72 : i * 288 + j * 72 + 72]
+                for p in (0, 1):
+                    add_bias(i * D + (2 * j + p) * 72, jnp.where(c == p, block, 0.0))
+
+    pl.run_scoped(attention, VM((8, 72, 2 * half), BF), VM((2, 2 * half, 864), BF))
+    for hop in hops:
+        hop()
+        tick(3)
+    tick(len(queue))
+
+    last_half = 72
+    def give(f, got, i):
+        return rdma(f.at[pl.ds(pl.multiple_of((1 - c) * 72, 8), 72)], got, ts.at[3, i], tr.at[3, i], twin)
+
+    give(fq, gotq, 0).start()
+    give(fu, gotu, 1).start()
+
+    def squares(value):
+        return jnp.sum(jnp.sum(value * value, axis=0, keepdims=True), axis=1, keepdims=True)
+
+    bias_squares = squares(bias_out[...])
+    total = squares(fq[...]) + squares(fu[...]) + squares(s_proj[...]) + squares(s_red[...]) + squares(gmod[...])
+    total = jnp.broadcast_to(total, (8, 128))
     for i, to in enumerate((twin, yn, xn)):
-        box[2 * i] = total
-        d = rdma(box.at[2 * i], box.at[2 * i + 1], s.at[i], r.at[i], to)
+        sq[2 * i] = total
+        d = rdma(sq.at[2 * i], sq.at[2 * i + 1], ns.at[i], nr.at[i], to)
         d.start()
         d.wait()
-        total = total + box[2 * i + 1]
-    got_z[0] = total
-    ds = [rdma(got_z.at[0], got_z.at[k], s.at[2 + k], r.at[2 + k], zn[k]) for k in (1, 2, 3)]
-    for d in ds:
+        total = total + sq[2 * i + 1]
+    sq[6] = total
+    last = [rdma(sq.at[6], sq.at[6 + k], ns.at[2 + k], nr.at[2 + k], zn[k]) for k in (1, 2, 3)]
+    for d in last:
         d.start()
-    for d in ds:
+
+    def interleave(f, got, shard, width, i):
+        give(f, got, i).wait()
+        own = jnp.where(c == 0, f[:72, :], f[72:, :])
+        sides = (jnp.where(c == 0, own, got[...]), jnp.where(c == 0, got[...], own))
+        count = own.shape[1] // width
+        shard[...] = jnp.concatenate(
+            [sides[p][:, j * width : (j + 1) * width] for j in range(count) for p in (0, 1)], axis=1
+        )
+
+    interleave(fq, gotq, s_att, HEAD_DIM, 0)
+    interleave(fu, gotu, s_exp, BLOCK, 1)
+    for d in last:
         d.wait()
-    out_ref[...] = (got_z[0] + got_z[1]) + (got_z[2] + got_z[3])
-
-
-def sum_everywhere(value):
-    f32, vm = jnp.float32, pltpu.VMEM
+    norm_out[...] = (sq[6] + sq[7]) + (sq[8] + sq[9]) + bias_squares
+    for i in range(1 + half // TILE):
+        moved(i)
+    scatter.finish()
+
+
+def backward_block(kept):
+    half = kept[6].shape[0]
+    rows = 2 * half
+    sd = jax.ShapeDtypeStruct
+    vm = pl.BlockSpec(memory_space=VM)
+    hbm = pl.BlockSpec(memory_space=ANY)
+    sizes = ((D, 864), (72, 576), (D, D), (2304, 576))
+    pieces = [PIECES[n][:2] for n in NAMES]
+    dma = pltpu.SemaphoreType.DMA
+    n = len(CHUNKS)
+    scratch = [
+        VM((2, D, 864), BF),
+        VM((2, 8, 72, 576), BF),
+        VM((2, D, D), BF),
+        VM((2, 2304, 576), BF),
+    ]
+    for count in (2, 2, 4, 4, 3):
+        scratch += [VM((count,) + p, BF) for p in pieces]
+    scratch += [
+        VM((144, 864), F32),
+        VM((144, D), F32),
+        VM((72, 864), F32),
+        VM((72, D), F32),
+        VM((rows, D), BF),
+        VM((half, D), F32),
+        VM((half, D), BF),
+        VM((half, D), BF),
+        VM((2, 1, 3456), F32),
+        VM((1, 9216), F32),
+        VM((4, 2, 2, 1, 3456), F32),
+        VM((2, 1, 3456), F32),
+        VM((2, 1, 3456), F32),
+        VM((3, 1, 9216), F32),
+        VM((3, 1, 9216), F32),
+        VM((3, 1, 9216), F32),
+        VM((2, 1, 3456), F32),
+        VM((10, 8, 128), F32),
+        dma((9,)),
+    ]
+    scratch += [dma((n, 4))] * 2 + [dma((n, 4, 2))] * 2 + [dma((n, 4))] * 6
+    scratch += [dma((4, 4))] * 2 + [dma((5,))] * 2 + [dma((5, 6))] * 2 + [dma((6,))] * 2
+    places = [hbm] * 4 + [vm, vm] + [hbm] * 8 + [vm] + [hbm] * 7
     return pl.pallas_call(
-        norm_kernel,
-        out_shape=jax.ShapeDtypeStruct((8, 128), f32),
-        in_specs=[pl.BlockSpec(memory_space=vm)],
-        out_specs=pl.BlockSpec(memory_space=vm),
-        scratch_shapes=[
-            vm((6, 8, 128), f32),
-            vm((4, 8, 128), f32),
-            pltpu.SemaphoreType.DMA((6,)),
-            pltpu.SemaphoreType.DMA((6,)),
+        backward_kernel,
+        out_shape=[
+            sd((half, D), BF),
+            sd((half, D), BF),
+            sd((72, 1728), F32),
+            sd((72, 576), F32),
+            sd((72, 2304), F32),
+            sd((288, 576), F32),
+            sd((72, 3456), F32),
+            sd((1, 14 * D), F32),
+            sd((8, 128), F32),
         ],
-        compiler_params=pltpu.CompilerParams(collective_id=4, has_side_effects=True),
-        name="sum_everywhere",
-    )(value)
-
-
-def swap_halves(value):
-    return lax.ppermute(value, ("c", "y"), [(0, 0), (1, 2), (2, 1), (3, 3)])
-
-
-def to_twin(value):
-    return lax.ppermute(value, "c", [(0, 1), (1, 0)])
-
-
-def both_halves(value):
-    c = lax.axis_index("c")
-    other = to_twin(value)
-    return jnp.where(c == 0, jnp.concatenate([value, other]), jnp.concatenate([other, value]))
-
-
-def sum_halves(value):
-    c = lax.axis_index("c")
-    half = value.shape[0] // 2
-    mine = lax.dynamic_slice_in_dim(value, c * half, half)
-    other = to_twin(lax.dynamic_slice_in_dim(value, (1 - c) * half, half).astype(jnp.bfloat16))
-    return mine + other.astype(jnp.float32)
-
-
-def wide(left, weight):
-    return jnp.concatenate(
-        [jnp.dot(left, weight[i], preferred_element_type=jnp.float32) for i in (0, 1)], axis=1
-    )
-
-
-def wide_back(gradient, weight):
-    half = weight.shape[2]
-    return sum(
-        lax.dot_general(
-            gradient[:, i * half : (i + 1) * half],
-            weight[i],
-            (((1,), (1,)), ((), ())),
-            preferred_element_type=jnp.float32,
-        )
-        for i in (0, 1)
-    )
-
-
-def weight_grad(left, right, name):
-    rows, cols, _ = PIECES[name]
-    half = right.shape[1] // 2
-    return jnp.stack(
-        [
-            lax.dot_general(
-                left,
-                right[:, i * half : (i + 1) * half],
-                (((0,), (0,)), ((), ())),
-                preferred_element_type=jnp.float32,
-            ).astype(jnp.bfloat16)
-            for i in (0, 1)
-        ]
-    ).reshape(2, 4, 2, rows, cols)
-
-
-def shard_from_pieces(piece, width):
-    c = lax.axis_index("c")
-    half = piece.shape[0] // 2
-    mine = lax.dynamic_slice_in_dim(piece, c * half, half)
-    other = to_twin(lax.dynamic_slice_in_dim(piece, (1 - c) * half, half))
-    split = jnp.where(c == 0, jnp.stack([mine, other]), jnp.stack([other, mine]))
-    cols = piece.shape[1]
-    return split.reshape(2, half, cols // width, width).transpose(1, 2, 0, 3).reshape(half, 2 * cols)
-
-
-def core_bias(piece, width):
-    c = lax.axis_index("c")
-    blocks = piece.reshape(-1, 2, width)
-    return lax.dynamic_index_in_dim(blocks, c, 1, keepdims=False).reshape(-1)
-
-
-def bias_slot(piece, width):
-    c = lax.axis_index("c")
-    blocks = piece.reshape(-1, 1, width)
-    pick = (jnp.arange(2) == c).astype(jnp.float32)[None, :, None]
-    return (blocks * pick).reshape(-1)
+        in_specs=places,
+        out_specs=[hbm, hbm] + [vm] * 7,
+        scratch_shapes=scratch,
+        compiler_params=pltpu.CompilerParams(
+            collective_id=1, has_side_effects=True, vmem_limit_bytes=62 * 2**20
+        ),
+        name="backward_block",
+    )(*kept)
 
 
 def on_device_fast(
@@ -1610,31 +1961,7 @@
     steps = jnp.arange(64, dtype=f32)[:, None]
     omegas = jnp.exp(-math.log(10000.0) * jnp.arange(288, dtype=f32) / 288)[None, :]
     table = jnp.concatenate([jnp.sin(steps * omegas), jnp.cos(steps * omegas)], axis=1)
-    (
-        weight_q,
-        weight_p,
-        weight_u,
-        weight_d,
-        modulation,
-        cond_all,
-        residual_zero,
-        outer_grad,
-        closing_all,
-        hidden_attend,
-        queries,
-        key_rows,
-        value_rows,
-        attn_t,
-        log_sums,
-        branch_attend,
-        residual_one,
-        hidden_expand,
-        activated,
-        slope,
-        branch_expand,
-        output,
-        grad_reduce,
-    ) = forward_block(
+    kept = forward_block(
         tokens,
         cotangent,
         bucket,
@@ -1644,101 +1971,20 @@
         cond_tiles,
         biases_master[None, :],
     )
-
-    modulation = modulation.reshape(6 * D)
-    shift_one, scale_one, gating_one, shift_two, scale_two, gating_two = (
-        modulation[i * D : (i + 1) * D][None, :] for i in range(6)
-    )
-    chip_bucket = swap_halves(buckets)
-    unit = SIDE // 8
-    lengths = table_pick(chip_bucket, row_units) * unit * table_pick(chip_bucket, col_units) * unit
-
-    def flat(heads):
-        return heads.transpose(1, 0, 2).reshape(1024, 576)
-
-    queries, key_rows = flat(queries[:, :, :72]), flat(key_rows[:, :, :72])
-    value_rows = value_rows.reshape(576, 1024).T
-    attention = attn_t.reshape(576, 1024).T.astype(bf16)
-    log_sums = log_sums.reshape(8, 2, 512).transpose(1, 0, 2)[None] * math.log(2.0)
-    weight_p = weight_p.reshape(2, 576, 576)
-    output = swap_halves(output)
-    residual_zero = residual_zero.astype(f32)
-    outer_grad = outer_grad.astype(f32)
-    gating_later = jnp.sum(outer_grad * branch_expand, axis=0)
-    closing_grad = (outer_grad * gating_two).astype(bf16)
-    active_grad = wide_back(closing_all, weight_d)
-    widened_grad = (active_grad * slope).astype(bf16)
-    grad_reduce = grad_reduce.reshape(2, 4, 2, 288, 576)
-    grad_expand = weight_grad(hidden_expand, widened_grad, "u")
-    hidden_grad = sum_halves(wide_back(widened_grad, weight_u))
-    def norm_back(residual, scaling, gradient):
-        average = jnp.mean(residual, axis=-1, keepdims=True)
-        centred = residual - average
-        inverse = lax.rsqrt(jnp.mean(centred * centred, axis=-1, keepdims=True) + 1e-06)
-        normed = centred * inverse
-        inner = gradient * (1.0 + scaling)
-        part = (
-            inner
-            - jnp.mean(inner, axis=-1, keepdims=True)
-            - normed * jnp.mean(inner * normed, axis=-1, keepdims=True)
-        ) * inverse
-        return part, jnp.sum(gradient, axis=0), jnp.sum(gradient * normed, axis=0)
-
-    residual_part, shift_later, scale_later = norm_back(residual_one, scale_two, hidden_grad)
-    middle_grad = outer_grad + residual_part
-    gating_early = jnp.sum(middle_grad * branch_attend, axis=0)
-    branch_grad = (middle_grad * gating_one).astype(bf16)
-    branch_all = both_halves(branch_grad)
-    heads_grad = wide_back(branch_all, weight_p).astype(bf16)
-    grad_project = weight_grad(attention, branch_all, "p")
-    query_grad, keyrow_grad, value_grad = attend_back(
-        queries, key_rows, value_rows, heads_grad, log_sums, lengths
-    )
-    packed_grad = jnp.concatenate([query_grad, keyrow_grad, value_grad], axis=1)
-    grad_attend = weight_grad(hidden_attend, packed_grad, "q")
-    normed_grad = sum_halves(wide_back(packed_grad, weight_q))
-    input_part, shift_early, scale_early = norm_back(residual_zero, scale_one, normed_grad)
-    input_grad = swap_halves((middle_grad + input_part).astype(bf16)).astype(f32)
-
-    mod_grad = jnp.concatenate(
-        [shift_early, scale_early, gating_early, shift_later, scale_later, gating_later]
-    )
-    bias_share = jnp.concatenate(
-        [
-            bias_slot(jnp.sum(query_grad.astype(f32), axis=0), HEAD_DIM),
-            bias_slot(jnp.sum(value_grad.astype(f32), axis=0), HEAD_DIM),
-            jnp.sum(branch_grad.astype(f32), axis=0),
-            bias_slot(jnp.sum(widened_grad.astype(f32), axis=0), block),
-            jnp.sum(closing_grad.astype(f32), axis=0),
-        ]
-    )
-    sums_q, sums_p, sums_u, sums_d = scatter_grads(
-        (grad_attend, grad_project, grad_expand, grad_reduce)
-    )
-    mods, bias_sums = share_totals(mod_grad.reshape(16, 432), bias_share.reshape(72, 128))
-    mods = mods.reshape(16, 2, 3456)
-    grad_mod = lax.dot_general(
-        cond_all[:, :72].astype(bf16),
-        lax.dynamic_index_in_dim(mods, y, 1, keepdims=False),
-        (((0,), (0,)), ((), ())),
-        preferred_element_type=f32,
-    )
-    bias_total = jnp.concatenate([jnp.sum(mods.astype(f32), axis=0).reshape(-1), bias_sums.reshape(-1)])
-    grad_attend = shard_from_pieces(sums_q, HEAD_DIM)
-    grad_expand = shard_from_pieces(sums_u, block)
-    reduced = (grad_mod, grad_attend, sums_p, grad_expand, sums_d)
-    local_squares = sum(jnp.sum(gradient * gradient) for gradient in reduced)
-    square_total = sum_everywhere(jnp.full((8, 128), local_squares))[0, 0]
-    grad_norm = jnp.sqrt(square_total + jnp.sum(bias_total * bias_total))
+    (output, input_grad, grad_attend, grad_project, grad_expand, grad_reduce, grad_mod, bias_total, squares) = (
+        backward_block(kept)
+    )
+    grad_norm = jnp.sqrt(squares[0, 0])
+    bias_total = bias_total[0]
     clip_factor = jnp.minimum(1.0, 1.0 / (grad_norm + 1e-06))
     correction = 1.0 - jnp.power(0.5, step_count.astype(f32))
     rate = 0.5 * D ** (-0.5)
     states = (
         (modulate_master, modulate_first, modulate_second, grad_mod, rate),
         (attend_master, attend_first, attend_second, grad_attend, rate),
-        (project_master, project_first, project_second, sums_p, rate),
+        (project_master, project_first, project_second, grad_project, rate),
         (expand_master, expand_first, expand_second, grad_expand, rate),
-        (reduce_master, reduce_first, reduce_second, sums_d, 0.5 * FF ** (-0.5)),
+        (reduce_master, reduce_first, reduce_second, grad_reduce, 0.5 * FF ** (-0.5)),
         (biases_master, biases_first, biases_second, bias_total, 0.1),
     )
     updates = []
@@ -1746,7 +1992,7 @@
         updates += adam_update(
             master, first, second, gradient, learn_rate, clip_factor, correction
         )
-    return (output, input_grad, grad_norm, *updates)
+    return (output, input_grad.astype(f32), grad_norm, *updates)
 
 
 def fast_solution(mesh):

time: 693 us -> 473 us (0.68)
  the two profiles are of different devices: /device:TPU:1 before, /device:TPU:0 now
where the time goes in v3:
time: 473 us; the launch traced here: 465 us
  Pallas kernels  438 us (93%)
  other arithmetic  15.3 us (3%)
  local copies, waits for them, and re-layouts  5.61 us (1%)
  between operations  5.6 us (1%)
    pallas_call x1, Pallas kernels, backward_block(): pl.pallas_call(backward_kernel, out_shape=[sd((half, D), BF), sd((half, D...  235 us
    pallas_call x1, Pallas kernels, forward_block(): pl.pallas_call(forward_kernel, out_shape=out_shape, in_specs=[vm, hbm] +...  203 us
    sub x6, other arithmetic, adam_update(): master - learn_rate * (direction + 0.1 * master)  10.1 us

profile of v3, /device:TPU:0, one launch (start us, length us, event | category | flops | bytes accessed | tf_op | source)
XLA Modules:
  0.0 464.7 jit_solution(16686264037147801573)
XLA Ops:
  2.0 0.1 fusion.8
  2.1 0.8 convert_reduce_fusion
  2.9 0.1 reshape.81
  3.0 0.6 pad_convert_fusion.refs_9_
  3.6 0.4 fusion.6
  4.0 0.8 pad_maximum_fusion.refs_3_
  4.7 1.5 broadcast_in_dim.8.refs_10_
  6.9 0.6 broadcast_in_dim.7.refs_2_
  7.5 203.2 %forward_block.1 = (bf16[2,1152,864]{2,1,0:T(8,128)(2,1)}, bf16[2,8,72,576]{3,2,1,0:T(8,128)(2,1)}, bf16[2,1152,1152]{2,1,0:T(8,128)(2,1)}, bf16[2,2304,576]{2,1...) custom-call(bf16[512,1152]{1,0:T(8,128)(2,1)} %refs_0_.1, ...), custom_call_target="tpu_custom_call" | custom-call | tf_op jit(solution)/shard_map/forward_block/pallas_call | solution.py:1272
  210.7 0.0 copy-start.17
  210.7 0.0 copy-start.21
  210.7 0.0 copy-start.22
  210.7 0.0 copy-start.1
  210.7 0.0 copy-start.9
  210.8 235.0 %backward_block.1 = (bf16[512,1152]{1,0:T(8,128)(2,1)}, bf16[512,1152]{1,0:T(8,128)(2,1)}, f32[72,1728]{1,0:T(8,128)}, f32[72,576]{1,0:T(8,128)}, f32[72,2304]{1...) custom-call(bf16[2,1152,864]{2,1,0:T(8,128)(2,1)} %get-tuple-element.52.refs_0_, ...), custom_call_target="tpu_custom_call" | custom-call | tf_op jit(solution)/shard_map/backward_block/pallas_call | solution.py:1903
  445.7 1.2 slice.3
  447.7 1.0 multiply_reduce_fusion
  449.4 0.0 copy-done.17
  449.4 0.0 copy-done.21
  449.4 0.0 copy-done.22
  449.4 0.7 multiply_subtract_fusion.5
  450.1 0.0 copy-done.1
  450.1 0.0 copy-done.9
  450.1 0.0 copy-start.12
  450.1 0.0 copy-start.13
  450.1 3.2 multiply_subtract_fusion.1
  453.4 0.0 copy-done.2
  453.4 0.0 copy-done.11
  453.4 0.0 copy-done.12
  453.4 0.0 copy-done.13
  453.4 0.0 copy-start.10
  453.4 0.0 copy-start.18
  453.4 0.0 copy-start.19
  453.4 0.0 copy-start.20
  453.4 0.0 copy-start.3
  453.4 0.0 copy-start.14
  453.5 0.0 copy-start.15
  453.5 1.7 multiply_subtract_fusion.2
  455.1 0.0 copy-done.10
  455.2 0.9 multiply_subtract_fusion.4
  456.1 1.4 multiply_subtract_fusion.3
  457.5 0.0 copy-done
  457.5 0.7 copy-done.6
  458.2 0.3 copy-done.7
  458.5 2.2 multiply_subtract_fusion
  460.7 1.6 convert_element_type.25
  462.3 0.1 copy-done.5
  462.4 1.0 copy.51
  (19 shorter events, 0.0 us)
Async XLA Ops:
  210.7 238.7 %copy-start.17 = (f32[16128]{0:T(1024)S(1)}, f32[16128]{0:T(1024)}, u32[]{:S(2)}) copy-start(f32[16128]{0:T(1024)} %param.47) | copy-start | bytes 193540
  210.7 238.7 %copy-start.21 = (f32[16128]{0:T(1024)S(1)}, f32[16128]{0:T(1024)}, u32[]{:S(2)}) copy-start(f32[16128]{0:T(1024)} %param.49) | copy-start | bytes 193540
  210.7 238.7 %copy-start.22 = (f32[16128]{0:T(1024)S(1)}, f32[16128]{0:T(1024)}, u32[]{:S(2)}) copy-start(f32[16128]{0:T(1024)} %param.48) | copy-start | bytes 193540
  210.7 239.4 %copy-start.1 = (f32[288,576]{1,0:T(8,128)S(1)}, f32[288,576]{1,0:T(8,128)}, u32[]{:S(2)}) copy-start(f32[288,576]{1,0:T(8,128)} %refs_7_.1) | copy-start | bytes 1990660
  210.7 239.4 %copy-start.9 = (f32[288,576]{1,0:T(8,128)S(1)}, f32[288,576]{1,0:T(8,128)}, u32[]{:S(2)}) copy-start(f32[288,576]{1,0:T(8,128)} %param.46) | copy-start | bytes 1990660
  450.1 3.3 copy-start.2
  450.1 3.3 copy-start.11
  450.1 3.3 copy-start.12
  450.1 3.3 copy-start.13
  453.4 1.8 copy-start.10
  453.4 1.7 copy-start.18
  453.4 1.7 copy-start.19
  453.4 1.7 copy-start.20
  453.4 2.6 copy-start.3
  453.4 2.6 copy-start.14
  453.5 2.6 copy-start.15
  453.5 2.6 copy-start.16
  455.2 2.4 copy-start.8
  456.0 1.5 copy-start
  456.0 2.1 copy-start.6
  456.0 2.4 copy-start.7
  458.5 2.2 copy-start.4
  460.7 1.7 copy-start.5
